TPU v7x, 256 devices: a whole 4x4x8 slice. The times are simulated.
256 devices in a mesh: seq: 32 (over z, x_lo, core), fsdp: 8 (over y, x_hi).
Axes of the slice: x: 4 (x_hi: 2, x_lo: 2; x = x_hi * 2 + x_lo), y: 4, z: 8, core: 2. Of those that a mesh axis runs over, the one named last changes fastest.
Arguments:
- query_rows: bfloat16 [4096, 3072], P('seq', 'fsdp'), may hold values from -7 to 7
- key_rows: bfloat16 [4096, 3072], P('seq', 'fsdp'), may hold values from -7 to 7
- value_rows: bfloat16 [4096, 3072], P('seq', 'fsdp'), may hold values from -6 to 6
- tile_mask: int32 [32, 32], replicated, may hold values from 0 to 1, as said below
- up_weight: bfloat16 [3072, 10240], P('seq', 'fsdp'), may hold values from -0.109375 to 0.109375
- cotangent: bfloat16 [4096, 10240], P('seq', 'fsdp'), may hold values from -48 to 48
Outputs:
- scaled_act: bfloat16 [4096, 10240], P('seq', 'fsdp')
- grad_query: float32 [4096, 3072], P('seq', 'fsdp')
- grad_key: float32 [4096, 3072], P('seq', 'fsdp')
- grad_value: float32 [4096, 3072], P('seq', 'fsdp')
Inputs may be any that keep to these rules, and one draw needn't show every extreme that they name: Tiles are numbered slab by slab and within a slab row by row over 2 x 2 tiles. tile_mask[i, j] is 1 exactly where tile j's slab is at most one away from tile i's, its row at most a distance of 0 or 1 (drawn for each tile i) from tile i's row, and its column at most a distance of 0 or 1 (drawn for each tile i) from tile i's column; 0 elsewhere.
All inputs are finite; a program needn't handle non-finite values.
Results may differ from a plain program's by a relative error of at most 0.022.
Values may be sent and summed in bfloat16 or wider, within the bound.
No kernel may reach another device: no remote copies, remote signals or barrier semaphores. Data moves between devices by JAX's collectives and lax.ppermute only.
A program may use at most 64 MiB of HBM per device.

v0:
```python
import jax
import jax.numpy as jnp
from jax import lax
from jax.sharding import PartitionSpec as P

HD = 128
TILE = 128
GH = 2
GW = 2


MASKED = -1e30
EPSILON = 1e-05


def shifted(value, axis, steps):
    count = lax.axis_size(axis)
    pairs = [(source, (source + steps) % count) for source in range(count)]
    return lax.ppermute(value, axis, pairs)


def passed_along(value, axis, steps):
    count = lax.axis_size(axis)
    first, last = (max(0, -steps), min(count, count - steps))
    return lax.ppermute(value, axis, [(source, source + steps) for source in range(first, last)])


def gelu_tanh(values):
    return jax.nn.gelu(values, approximate=True)


def widen_mask(mask_block, tile_len):
    query_tiles, key_tiles = mask_block.shape
    grown_mask = jnp.broadcast_to(
        mask_block[:, None, :, None], (query_tiles, tile_len, key_tiles, tile_len)
    )
    return grown_mask.reshape(query_tiles * tile_len, key_tiles * tile_len)


def split_heads(flat_rows):
    return flat_rows.reshape(flat_rows.shape[0], flat_rows.shape[1] // HD, HD)


def attend_all(query_heads, pair_rows, allowed, score_scale):
    half_width = pair_rows.shape[1] // 2
    key_heads = split_heads(pair_rows[:, :half_width])
    value_heads = split_heads(pair_rows[:, half_width:])
    scores = (
        jnp.einsum("qhd,khd->hqk", query_heads, key_heads, preferred_element_type=jnp.float32)
        * score_scale
    )
    scores = jnp.where(allowed[None], scores, MASKED)
    top_score = jnp.max(scores, axis=-1, keepdims=True)
    row_total = jnp.sum(
        jnp.where(allowed[None], jnp.exp(scores - top_score), 0.0), axis=-1, keepdims=True
    )
    log_total = top_score + jnp.log(row_total)
    weights = jnp.where(allowed[None], jnp.exp(scores - log_total), 0.0).astype(jnp.bfloat16)
    mixed_rows = jnp.einsum(
        "hqk,khd->qhd", weights, value_heads, preferred_element_type=jnp.float32
    )
    attn_out = mixed_rows.reshape(mixed_rows.shape[0], -1).astype(jnp.bfloat16)
    return (attn_out, log_total[:, :, 0])


def score_grads(query_heads, grad_heads, log_total, row_delta, pair_rows, allowed, score_scale):
    half_width = pair_rows.shape[1] // 2
    key_heads = split_heads(pair_rows[:, :half_width])
    value_heads = split_heads(pair_rows[:, half_width:])
    scores = (
        jnp.einsum("qhd,khd->hqk", query_heads, key_heads, preferred_element_type=jnp.float32)
        * score_scale
    )
    weights = jnp.where(allowed[None], jnp.exp(scores - log_total[:, :, None]), 0.0)
    grad_prob = jnp.einsum(
        "qhd,khd->hqk", grad_heads, value_heads, preferred_element_type=jnp.float32
    )
    dscores = (weights * (grad_prob - row_delta[:, :, None])).astype(jnp.bfloat16)
    return (dscores, weights.astype(jnp.bfloat16), key_heads)


def query_terms(dscores, key_heads, score_scale):
    query_grads = (
        jnp.einsum("hqk,khd->qhd", dscores, key_heads, preferred_element_type=jnp.float32)
        * score_scale
    )
    return query_grads.reshape(query_grads.shape[0], -1)


def key_terms(dscores, prob_bf, query_heads, grad_heads, score_scale):
    grad_keys = (
        jnp.einsum("hqk,qhd->khd", dscores, query_heads, preferred_element_type=jnp.float32)
        * score_scale
    )
    grad_values = jnp.einsum(
        "hqk,qhd->khd", prob_bf, grad_heads, preferred_element_type=jnp.float32
    )
    key_count = grad_keys.shape[0]
    joined = jnp.concatenate(
        [grad_keys.reshape(key_count, -1), grad_values.reshape(key_count, -1)], axis=1
    )
    return lax.optimization_barrier(joined.astype(jnp.bfloat16))


def body(query_rows, key_rows, value_rows, tile_mask, up_weight, cotangent):
    row_count, feat_width = query_rows.shape
    tiles_here = row_count // TILE
    seq_count = lax.axis_size("seq")
    seq_place = lax.axis_index("seq")
    total_rows = row_count * seq_count
    reach_devs = min(-(-(2 * GH * GW - 1) // tiles_here), seq_count - 1)
    score_scale = HD ** (-0.5)

    def tile_block(row_anchor, col_anchor):
        inside = (
            (row_anchor >= 0)
            & (row_anchor < seq_count)
            & (col_anchor >= 0)
            & (col_anchor < seq_count)
        )
        row_start = jnp.clip(row_anchor, 0, seq_count - 1) * tiles_here
        col_start = jnp.clip(col_anchor, 0, seq_count - 1) * tiles_here
        mask_block = lax.dynamic_slice(tile_mask, (row_start, col_start), (tiles_here, tiles_here))
        return widen_mask((mask_block > 0) & inside, TILE)

    def pair_mask(distance):
        return jnp.concatenate(
            [
                tile_block(seq_place, seq_place - distance),
                tile_block(seq_place, seq_place + distance),
            ],
            axis=1,
        )

    query_heads = split_heads(query_rows)
    own_pair = jnp.concatenate([key_rows, value_rows], axis=1)
    lower_store = jnp.zeros((reach_devs, row_count, 2 * feat_width), jnp.bfloat16)
    upper_store = jnp.zeros((reach_devs, row_count, 2 * feat_width), jnp.bfloat16)

    def cycle_step(distance, loop_carry):
        passing, lower_store, upper_store = loop_carry
        passing = shifted(passing, "seq", 1)
        lower_store = lax.cond(
            distance <= reach_devs,
            lambda stored: lax.dynamic_update_slice(stored, passing[None], (distance - 1, 0, 0)),
            lambda stored: stored,
            lower_store,
        )
        upper_store = lax.cond(
            distance >= seq_count - reach_devs,
            lambda stored: lax.dynamic_update_slice(
                stored, passing[None], (seq_count - distance - 1, 0, 0)
            ),
            lambda stored: stored,
            upper_store,
        )
        return (passing, lower_store, upper_store)

    _, lower_store, upper_store = lax.fori_loop(
        1, seq_count, cycle_step, (own_pair, lower_store, upper_store)
    )
    near_rows = jnp.concatenate(
        [
            own_pair,
            lower_store.reshape(-1, 2 * feat_width),
            upper_store.reshape(-1, 2 * feat_width),
        ],
        axis=0,
    )
    near_masks = [tile_block(seq_place, seq_place)]
    near_masks = near_masks + [
        tile_block(seq_place, seq_place - distance) for distance in range(1, reach_devs + 1)
    ]
    near_masks = near_masks + [
        tile_block(seq_place, seq_place + distance) for distance in range(1, reach_devs + 1)
    ]
    attn_out, log_total = attend_all(
        query_heads, near_rows, jnp.concatenate(near_masks, axis=1), score_scale
    )
    full_rows = lax.all_gather(attn_out, "fsdp", axis=1, tiled=True)
    hidden = jnp.dot(
        full_rows,
        lax.all_gather(up_weight, "seq", axis=0, tiled=True),
        preferred_element_type=jnp.float32,
    )
    activated, gelu_pull = jax.vjp(gelu_tanh, hidden)
    mean_power = lax.psum(jnp.sum(activated * activated, axis=0), "seq") / total_rows
    inv_scale = lax.rsqrt(mean_power + EPSILON)
    scaled_act = (activated * inv_scale).astype(jnp.bfloat16)
    grad_scaled = cotangent.astype(jnp.float32)
    grad_inv = lax.psum(jnp.sum(grad_scaled * activated, axis=0), "seq")
    grad_power = grad_inv * -0.5 * inv_scale * inv_scale * inv_scale
    grad_act = grad_scaled * inv_scale + grad_power * (2.0 / total_rows) * activated
    grad_hidden = gelu_pull(grad_act)[0].astype(jnp.bfloat16)
    back_part = lax.dot_general(
        grad_hidden,
        lax.all_gather(up_weight, "seq", axis=0, tiled=True),
        (((1,), (1,)), ((), ())),
        preferred_element_type=jnp.float32,
    )
    attn_grad = lax.psum_scatter(
        back_part.astype(jnp.bfloat16), "fsdp", scatter_dimension=1, tiled=True
    )
    grad_heads = split_heads(attn_grad)
    out_heads = split_heads(attn_out)
    row_delta = jnp.einsum("qhd,qhd->hq", grad_heads, out_heads, preferred_element_type=jnp.float32)
    dscores, prob_bf, key_heads = score_grads(
        query_heads,
        grad_heads,
        log_total,
        row_delta,
        own_pair,
        tile_block(seq_place, seq_place),
        score_scale,
    )
    query_grads = query_terms(dscores, key_heads, score_scale)
    key_grads = key_terms(dscores, prob_bf, query_heads, grad_heads, score_scale).astype(
        jnp.float32
    )

    def step_terms(distance, query_grads):
        from_lower = lax.dynamic_index_in_dim(lower_store, distance - 1, 0, keepdims=False)
        from_upper = lax.dynamic_index_in_dim(upper_store, distance - 1, 0, keepdims=False)
        pair_rows = jnp.concatenate([from_lower, from_upper], axis=0)
        dscores, prob_bf, key_heads = score_grads(
            query_heads,
            grad_heads,
            log_total,
            row_delta,
            pair_rows,
            pair_mask(distance),
            score_scale,
        )
        query_grads = query_grads + query_terms(dscores, key_heads, score_scale)
        key_parts = key_terms(dscores, prob_bf, query_heads, grad_heads, score_scale)
        return (query_grads, key_parts[:row_count], key_parts[row_count:])

    def relay_step(turn_index, loop_carry):
        query_grads, to_lower, to_upper = loop_carry
        query_grads, lower_parts, upper_parts = step_terms(reach_devs - turn_index, query_grads)
        to_lower = passed_along(
            (to_lower + lower_parts.astype(jnp.float32)).astype(jnp.bfloat16), "seq", -1
        ).astype(jnp.float32)
        to_upper = passed_along(
            (to_upper + upper_parts.astype(jnp.float32)).astype(jnp.bfloat16), "seq", 1
        ).astype(jnp.float32)
        return (query_grads, to_lower, to_upper)

    zero_grads = jnp.zeros((row_count, 2 * feat_width), jnp.float32)
    query_grads, to_lower, to_upper = lax.fori_loop(
        0, reach_devs, relay_step, (query_grads, zero_grads, zero_grads)
    )
    key_grads = key_grads + to_lower + to_upper
    return (scaled_act, query_grads, key_grads[:, :feat_width], key_grads[:, feat_width:])


def solution(mesh):
    placed = (
        P("seq", "fsdp"),
        P("seq", "fsdp"),
        P("seq", "fsdp"),
        P(),
        P("seq", "fsdp"),
        P("seq", "fsdp"),
    )
    return jax.shard_map(
        body,
        mesh=mesh,
        in_specs=placed,
        out_specs=(P("seq", "fsdp"), P("seq", "fsdp"), P("seq", "fsdp"), P("seq", "fsdp")),
        check_vma=False,
    )
```

profile of v0, /device:TPU:2, one launch (start us, length us, event | category | flops | bytes accessed | tf_op | source)
XLA Modules:
  0.0 630.1 jit_solution(8651254405504068203)
XLA Ops:
  8.0 2.0 fusion.57
  21.3 225.1 %while.45 = (s32[]{:T(128)}, bf16[128,768]{1,0:T(8,128)(2,1)S(1)}, bf16[7,128,768]{2,1,0:T(8,128)(2,1)S(1)}, bf16[7,128,768]{2,1,0:T(8,128)(2,1)S(1)}, s32[]{:T(128)}, /*index=5*/s32[]{:T(128)}, s32[]{:T(128)}) while((s32[]{:T(128)}, bf16[128,768]{1,0:T(8,128)(2,1)S(1)}, bf16[7,128,768]{2,1,0:T(8,128)(2,1)S(1)}, ...), condition=%wide.region_5.0_spmd, body=%wide.region_0.0_spmd.sunk | while | flops 14 | bytes 1966389 | solution.py:159
  21.5 7.3 %collective-permute-done = bf16[128,768]{1,0:T(8,128)(2,1)S(1)} collective-permute-done((bf16[128,768]{1,0:T(8,128)(2,1)S(1)}, bf16[128,768]{1,0:T(8,128)(2,1)S(1)}, u32[]{:S(2)}, u32[]{:S(2)}) %collective-permute-start) | collective-permute-done | bytes 196640 | tf_op jit(solution)/shard_map/while/body/eval_jaxpr/ppermute | solution.py:19
  29.1 6.4 %collective-permute-done = bf16[128,768]{1,0:T(8,128)(2,1)S(1)} collective-permute-done((bf16[128,768]{1,0:T(8,128)(2,1)S(1)}, bf16[128,768]{1,0:T(8,128)(2,1)S(1)}, u32[]{:S(2)}, u32[]{:S(2)}) %collective-permute-start) | collective-permute-done | bytes 196640 | tf_op jit(solution)/shard_map/while/body/eval_jaxpr/ppermute | solution.py:19
  35.7 2.3 collective-permute-start
  38.0 4.3 collective-permute-done
  42.4 5.2 collective-permute-start
  48.7 9.0 %collective-permute-start = (bf16[128,768]{1,0:T(8,128)(2,1)S(1)}, bf16[128,768]{1,0:T(8,128)(2,1)S(1)}, u32[]{:S(2)}, u32[]{:S(2)}) collective-permute-start(bf16[128,768]{1,0:T(8,128)(2,1)S(1)} %get-tuple-element.853), channel_id=1, source_target_pairs={{0,8},{8,16},{16,24},{24,32},{32,40},{40,48},{48,56},{56,64},{64,7... | collective-permute-start | bytes 589832 | tf_op jit(solution)/shard_map/while/body/eval_jaxpr/ppermute | solution.py:19
  58.9 7.1 %collective-permute-start = (bf16[128,768]{1,0:T(8,128)(2,1)S(1)}, bf16[128,768]{1,0:T(8,128)(2,1)S(1)}, u32[]{:S(2)}, u32[]{:S(2)}) collective-permute-start(bf16[128,768]{1,0:T(8,128)(2,1)S(1)} %get-tuple-element.853), channel_id=1, source_target_pairs={{0,8},{8,16},{16,24},{24,32},{32,40},{40,48},{48,56},{56,64},{64,7... | collective-permute-start | bytes 589832 | tf_op jit(solution)/shard_map/while/body/eval_jaxpr/ppermute | solution.py:19
  67.2 7.3 %collective-permute-start = (bf16[128,768]{1,0:T(8,128)(2,1)S(1)}, bf16[128,768]{1,0:T(8,128)(2,1)S(1)}, u32[]{:S(2)}, u32[]{:S(2)}) collective-permute-start(bf16[128,768]{1,0:T(8,128)(2,1)S(1)} %get-tuple-element.853), channel_id=1, source_target_pairs={{0,8},{8,16},{16,24},{24,32},{32,40},{40,48},{48,56},{56,64},{64,7... | collective-permute-start | bytes 589832 | tf_op jit(solution)/shard_map/while/body/eval_jaxpr/ppermute | solution.py:19
  75.7 5.8 collective-permute-start
  82.6 5.0 collective-permute-start
  88.7 5.0 collective-permute-start
  94.8 5.0 collective-permute-start
  100.9 5.0 collective-permute-start
  107.2 4.8 collective-permute-start
  112.0 2.5 collective-permute-done
  114.5 3.6 collective-permute-start
  118.1 3.7 collective-permute-done
  121.8 2.4 collective-permute-start
  124.2 4.9 collective-permute-done
  130.3 6.1 collective-permute-done
  136.5 7.2 %collective-permute-done = bf16[128,768]{1,0:T(8,128)(2,1)S(1)} collective-permute-done((bf16[128,768]{1,0:T(8,128)(2,1)S(1)}, bf16[128,768]{1,0:T(8,128)(2,1)S(1)}, u32[]{:S(2)}, u32[]{:S(2)}) %collective-permute-start) | collective-permute-done | bytes 196640 | tf_op jit(solution)/shard_map/while/body/eval_jaxpr/ppermute | solution.py:19
  143.9 7.2 %collective-permute-done = bf16[128,768]{1,0:T(8,128)(2,1)S(1)} collective-permute-done((bf16[128,768]{1,0:T(8,128)(2,1)S(1)}, bf16[128,768]{1,0:T(8,128)(2,1)S(1)}, u32[]{:S(2)}, u32[]{:S(2)}) %collective-permute-start) | collective-permute-done | bytes 196640 | tf_op jit(solution)/shard_map/while/body/eval_jaxpr/ppermute | solution.py:19
  151.2 7.2 %collective-permute-done = bf16[128,768]{1,0:T(8,128)(2,1)S(1)} collective-permute-done((bf16[128,768]{1,0:T(8,128)(2,1)S(1)}, bf16[128,768]{1,0:T(8,128)(2,1)S(1)}, u32[]{:S(2)}, u32[]{:S(2)}) %collective-permute-start) | collective-permute-done | bytes 196640 | tf_op jit(solution)/shard_map/while/body/eval_jaxpr/ppermute | solution.py:19
  158.5 7.2 %collective-permute-done = bf16[128,768]{1,0:T(8,128)(2,1)S(1)} collective-permute-done((bf16[128,768]{1,0:T(8,128)(2,1)S(1)}, bf16[128,768]{1,0:T(8,128)(2,1)S(1)}, u32[]{:S(2)}, u32[]{:S(2)}) %collective-permute-start) | collective-permute-done | bytes 196640 | tf_op jit(solution)/shard_map/while/body/eval_jaxpr/ppermute | solution.py:19
  165.8 7.2 %collective-permute-done = bf16[128,768]{1,0:T(8,128)(2,1)S(1)} collective-permute-done((bf16[128,768]{1,0:T(8,128)(2,1)S(1)}, bf16[128,768]{1,0:T(8,128)(2,1)S(1)}, u32[]{:S(2)}, u32[]{:S(2)}) %collective-permute-start) | collective-permute-done | bytes 196640 | tf_op jit(solution)/shard_map/while/body/eval_jaxpr/ppermute | solution.py:19
  173.1 7.2 %collective-permute-done = bf16[128,768]{1,0:T(8,128)(2,1)S(1)} collective-permute-done((bf16[128,768]{1,0:T(8,128)(2,1)S(1)}, bf16[128,768]{1,0:T(8,128)(2,1)S(1)}, u32[]{:S(2)}, u32[]{:S(2)}) %collective-permute-start) | collective-permute-done | bytes 196640 | tf_op jit(solution)/shard_map/while/body/eval_jaxpr/ppermute | solution.py:19
  180.4 7.2 %collective-permute-done = bf16[128,768]{1,0:T(8,128)(2,1)S(1)} collective-permute-done((bf16[128,768]{1,0:T(8,128)(2,1)S(1)}, bf16[128,768]{1,0:T(8,128)(2,1)S(1)}, u32[]{:S(2)}, u32[]{:S(2)}) %collective-permute-start) | collective-permute-done | bytes 196640 | tf_op jit(solution)/shard_map/while/body/eval_jaxpr/ppermute | solution.py:19
  187.8 7.2 %collective-permute-done = bf16[128,768]{1,0:T(8,128)(2,1)S(1)} collective-permute-done((bf16[128,768]{1,0:T(8,128)(2,1)S(1)}, bf16[128,768]{1,0:T(8,128)(2,1)S(1)}, u32[]{:S(2)}, u32[]{:S(2)}) %collective-permute-start) | collective-permute-done | bytes 196640 | tf_op jit(solution)/shard_map/while/body/eval_jaxpr/ppermute | solution.py:19
  195.1 7.2 %collective-permute-done = bf16[128,768]{1,0:T(8,128)(2,1)S(1)} collective-permute-done((bf16[128,768]{1,0:T(8,128)(2,1)S(1)}, bf16[128,768]{1,0:T(8,128)(2,1)S(1)}, u32[]{:S(2)}, u32[]{:S(2)}) %collective-permute-start) | collective-permute-done | bytes 196640 | tf_op jit(solution)/shard_map/while/body/eval_jaxpr/ppermute | solution.py:19
  202.4 7.2 %collective-permute-done = bf16[128,768]{1,0:T(8,128)(2,1)S(1)} collective-permute-done((bf16[128,768]{1,0:T(8,128)(2,1)S(1)}, bf16[128,768]{1,0:T(8,128)(2,1)S(1)}, u32[]{:S(2)}, u32[]{:S(2)}) %collective-permute-start) | collective-permute-done | bytes 196640 | tf_op jit(solution)/shard_map/while/body/eval_jaxpr/ppermute | solution.py:19
  209.8 7.2 %collective-permute-done = bf16[128,768]{1,0:T(8,128)(2,1)S(1)} collective-permute-done((bf16[128,768]{1,0:T(8,128)(2,1)S(1)}, bf16[128,768]{1,0:T(8,128)(2,1)S(1)}, u32[]{:S(2)}, u32[]{:S(2)}) %collective-permute-start) | collective-permute-done | bytes 196640 | tf_op jit(solution)/shard_map/while/body/eval_jaxpr/ppermute | solution.py:19
  217.1 7.2 %collective-permute-done = bf16[128,768]{1,0:T(8,128)(2,1)S(1)} collective-permute-done((bf16[128,768]{1,0:T(8,128)(2,1)S(1)}, bf16[128,768]{1,0:T(8,128)(2,1)S(1)}, u32[]{:S(2)}, u32[]{:S(2)}) %collective-permute-start) | collective-permute-done | bytes 196640 | tf_op jit(solution)/shard_map/while/body/eval_jaxpr/ppermute | solution.py:19
  224.5 7.2 %collective-permute-done = bf16[128,768]{1,0:T(8,128)(2,1)S(1)} collective-permute-done((bf16[128,768]{1,0:T(8,128)(2,1)S(1)}, bf16[128,768]{1,0:T(8,128)(2,1)S(1)}, u32[]{:S(2)}, u32[]{:S(2)}) %collective-permute-start) | collective-permute-done | bytes 196640 | tf_op jit(solution)/shard_map/while/body/eval_jaxpr/ppermute | solution.py:19
  231.8 7.2 %collective-permute-done = bf16[128,768]{1,0:T(8,128)(2,1)S(1)} collective-permute-done((bf16[128,768]{1,0:T(8,128)(2,1)S(1)}, bf16[128,768]{1,0:T(8,128)(2,1)S(1)}, u32[]{:S(2)}, u32[]{:S(2)}) %collective-permute-start) | collective-permute-done | bytes 196640 | tf_op jit(solution)/shard_map/while/body/eval_jaxpr/ppermute | solution.py:19
  239.2 7.2 %collective-permute-done = bf16[128,768]{1,0:T(8,128)(2,1)S(1)} collective-permute-done((bf16[128,768]{1,0:T(8,128)(2,1)S(1)}, bf16[128,768]{1,0:T(8,128)(2,1)S(1)}, u32[]{:S(2)}, u32[]{:S(2)}) %collective-permute-start) | collective-permute-done | bytes 196640 | tf_op jit(solution)/shard_map/while/body/eval_jaxpr/ppermute | solution.py:19
  247.5 2.0 fusion.55
  251.5 2.6 copy.98
  256.8 37.0 %all_gather.7 = bf16[128,3072]{0,1:T(8,128)(2,1)S(1)} all-gather(bf16[128,384]{0,1:T(8,128)(2,1)S(1)} %bitcast.179), channel_id=1, replica_groups=mesh['seq'=32,'fsdp'=8] {'fsdp'}, dimensions={1}, use_global_device_ids=true | all-gather | bytes 884736 | tf_op jit(solution)/shard_map/all_gather | solution.py:180
  293.8 4.7 fusion.27
  298.5 110.5 %all-reduce.1 = (f32[1280]{0:T(1024)S(1)}, f32[1280]{0:T(1024)S(1)}) all-reduce(f32[1280]{0:T(1024)S(1)} %get-tuple-element.648, f32[1280]{0:T(1024)S(1)} %get-tuple-element.647), channel_id=1, replica_groups=mesh['seq'=32,'fsdp'=8] {'seq'}, use_global_device_ids=true, to_apply=%region_9.10 | all-reduce | flops 2560 | bytes 20480 | tf_op jit(solution)/shard_map/psum | solution.py:187
  409.0 6.1 convolution_convert_fusion.1
  417.8 90.2 %reduce-scatter.4.cloned.1.call-done = bf16[384,128]{1,0:T(8,128)(2,1)} async-done(((bf16[3072,128]{1,0:T(8,128)(2,1)}), bf16[384,128]{1,0:T(8,128)(2,1)}) %reduce-scatter.4.cloned.1.call-update) | async-done | bytes 98320
  512.5 107.3 %while.46 = (s32[]{:T(128)}, f32[128,384]{0,1:T(8,128)S(1)}, f32[128,768]{0,1:T(8,128)S(1)}, f32[128,768]{0,1:T(8,128)S(1)}, bf16[7,128,768]{2,1,0:T(8,128)(2,1)...) while((s32[]{:T(128)}, f32[128,384]{0,1:T(8,128)S(1)}, ...), condition=%wide.region_14.15_spmd.clone, body=%wide.region_13.14_spmd.clone.sunk | while | flops 129466392 | bytes 12194087 | solution.py:250
  518.0 1.9 collective-permute-start.1
  519.9 2.4 collective-permute-start.2
  523.1 4.8 collective-permute-done.2
  533.4 1.9 collective-permute-start.1
  535.4 2.4 collective-permute-start.2
  538.5 4.7 collective-permute-done.2
  548.7 1.9 collective-permute-start.1
  550.7 2.4 collective-permute-start.2
  553.9 4.7 collective-permute-done.2
  564.0 1.9 collective-permute-start.1
  566.0 2.4 collective-permute-start.2
  569.2 4.7 collective-permute-done.2
  581.3 2.4 collective-permute-start.2
  584.5 4.7 collective-permute-done.2
  594.6 1.9 collective-permute-start.1
  596.6 2.4 collective-permute-start.2
  599.8 4.7 collective-permute-done.2
  611.9 2.4 collective-permute-start.2
  615.1 4.7 collective-permute-done.2
  (346 shorter events, 70.3 us)
Async XLA Ops:
  7.2 286.6 %all-gather.2.cloned.1.call-start = ((), (), s32[]{:S(2)}) async-start(), calls=%async_computation.1 | async-start | bytes 8110080 | tf_op jit(solution)/shard_map/all_gather | solution.py:183
  7.9 500.1 %reduce-scatter.4.cloned.1.call-start = ((), (), s32[]{:S(2)}) async-start(), calls=%async_computation.2 | async-start | bytes 884736
  21.4 7.4 %collective-permute-start = (bf16[128,768]{1,0:T(8,128)(2,1)S(1)}, bf16[128,768]{1,0:T(8,128)(2,1)S(1)}, u32[]{:S(2)}, u32[]{:S(2)}) collective-permute-start(bf16[128,768]{1,0:T(8,128)(2,1)S(1)} %get-tuple-element.853), channel_id=1, source_target_pairs={{0,8},{8,16},{16,24},{24,32},{32,40},{40,48},{48,56},{56,64},{64,7... | collective-permute-start | bytes 589832 | tf_op jit(solution)/shard_map/while/body/eval_jaxpr/ppermute | solution.py:19
  28.8 6.8 %collective-permute-start = (bf16[128,768]{1,0:T(8,128)(2,1)S(1)}, bf16[128,768]{1,0:T(8,128)(2,1)S(1)}, u32[]{:S(2)}, u32[]{:S(2)}) collective-permute-start(bf16[128,768]{1,0:T(8,128)(2,1)S(1)} %get-tuple-element.853), channel_id=1, source_target_pairs={{0,8},{8,16},{16,24},{24,32},{32,40},{40,48},{48,56},{56,64},{64,7... | collective-permute-start | bytes 589832 | tf_op jit(solution)/shard_map/while/body/eval_jaxpr/ppermute | solution.py:19
  35.7 6.6 %collective-permute-start = (bf16[128,768]{1,0:T(8,128)(2,1)S(1)}, bf16[128,768]{1,0:T(8,128)(2,1)S(1)}, u32[]{:S(2)}, u32[]{:S(2)}) collective-permute-start(bf16[128,768]{1,0:T(8,128)(2,1)S(1)} %get-tuple-element.853), channel_id=1, source_target_pairs={{0,8},{8,16},{16,24},{24,32},{32,40},{40,48},{48,56},{56,64},{64,7... | collective-permute-start | bytes 589832 | tf_op jit(solution)/shard_map/while/body/eval_jaxpr/ppermute | solution.py:19
  42.4 6.3 collective-permute-start
  48.7 10.1 %collective-permute-start = (bf16[128,768]{1,0:T(8,128)(2,1)S(1)}, bf16[128,768]{1,0:T(8,128)(2,1)S(1)}, u32[]{:S(2)}, u32[]{:S(2)}) collective-permute-start(bf16[128,768]{1,0:T(8,128)(2,1)S(1)} %get-tuple-element.853), channel_id=1, source_target_pairs={{0,8},{8,16},{16,24},{24,32},{32,40},{40,48},{48,56},{56,64},{64,7... | collective-permute-start | bytes 589832 | tf_op jit(solution)/shard_map/while/body/eval_jaxpr/ppermute | solution.py:19
  58.9 8.1 %collective-permute-start = (bf16[128,768]{1,0:T(8,128)(2,1)S(1)}, bf16[128,768]{1,0:T(8,128)(2,1)S(1)}, u32[]{:S(2)}, u32[]{:S(2)}) collective-permute-start(bf16[128,768]{1,0:T(8,128)(2,1)S(1)} %get-tuple-element.853), channel_id=1, source_target_pairs={{0,8},{8,16},{16,24},{24,32},{32,40},{40,48},{48,56},{56,64},{64,7... | collective-permute-start | bytes 589832 | tf_op jit(solution)/shard_map/while/body/eval_jaxpr/ppermute | solution.py:19
  67.2 8.4 %collective-permute-start = (bf16[128,768]{1,0:T(8,128)(2,1)S(1)}, bf16[128,768]{1,0:T(8,128)(2,1)S(1)}, u32[]{:S(2)}, u32[]{:S(2)}) collective-permute-start(bf16[128,768]{1,0:T(8,128)(2,1)S(1)} %get-tuple-element.853), channel_id=1, source_target_pairs={{0,8},{8,16},{16,24},{24,32},{32,40},{40,48},{48,56},{56,64},{64,7... | collective-permute-start | bytes 589832 | tf_op jit(solution)/shard_map/while/body/eval_jaxpr/ppermute | solution.py:19
  75.7 6.9 %collective-permute-start = (bf16[128,768]{1,0:T(8,128)(2,1)S(1)}, bf16[128,768]{1,0:T(8,128)(2,1)S(1)}, u32[]{:S(2)}, u32[]{:S(2)}) collective-permute-start(bf16[128,768]{1,0:T(8,128)(2,1)S(1)} %get-tuple-element.853), channel_id=1, source_target_pairs={{0,8},{8,16},{16,24},{24,32},{32,40},{40,48},{48,56},{56,64},{64,7... | collective-permute-start | bytes 589832 | tf_op jit(solution)/shard_map/while/body/eval_jaxpr/ppermute | solution.py:19
  82.6 6.1 collective-permute-start
  88.7 6.1 collective-permute-start
  94.8 6.1 collective-permute-start
  100.9 6.3 collective-permute-start
  107.2 7.3 %collective-permute-start = (bf16[128,768]{1,0:T(8,128)(2,1)S(1)}, bf16[128,768]{1,0:T(8,128)(2,1)S(1)}, u32[]{:S(2)}, u32[]{:S(2)}) collective-permute-start(bf16[128,768]{1,0:T(8,128)(2,1)S(1)} %get-tuple-element.853), channel_id=1, source_target_pairs={{0,8},{8,16},{16,24},{24,32},{32,40},{40,48},{48,56},{56,64},{64,7... | collective-permute-start | bytes 589832 | tf_op jit(solution)/shard_map/while/body/eval_jaxpr/ppermute | solution.py:19
  114.5 7.3 %collective-permute-start = (bf16[128,768]{1,0:T(8,128)(2,1)S(1)}, bf16[128,768]{1,0:T(8,128)(2,1)S(1)}, u32[]{:S(2)}, u32[]{:S(2)}) collective-permute-start(bf16[128,768]{1,0:T(8,128)(2,1)S(1)} %get-tuple-element.853), channel_id=1, source_target_pairs={{0,8},{8,16},{16,24},{24,32},{32,40},{40,48},{48,56},{56,64},{64,7... | collective-permute-start | bytes 589832 | tf_op jit(solution)/shard_map/while/body/eval_jaxpr/ppermute | solution.py:19
  121.8 7.3 %collective-permute-start = (bf16[128,768]{1,0:T(8,128)(2,1)S(1)}, bf16[128,768]{1,0:T(8,128)(2,1)S(1)}, u32[]{:S(2)}, u32[]{:S(2)}) collective-permute-start(bf16[128,768]{1,0:T(8,128)(2,1)S(1)} %get-tuple-element.853), channel_id=1, source_target_pairs={{0,8},{8,16},{16,24},{24,32},{32,40},{40,48},{48,56},{56,64},{64,7... | collective-permute-start | bytes 589832 | tf_op jit(solution)/shard_map/while/body/eval_jaxpr/ppermute | solution.py:19
  129.1 7.3 %collective-permute-start = (bf16[128,768]{1,0:T(8,128)(2,1)S(1)}, bf16[128,768]{1,0:T(8,128)(2,1)S(1)}, u32[]{:S(2)}, u32[]{:S(2)}) collective-permute-start(bf16[128,768]{1,0:T(8,128)(2,1)S(1)} %get-tuple-element.853), channel_id=1, source_target_pairs={{0,8},{8,16},{16,24},{24,32},{32,40},{40,48},{48,56},{56,64},{64,7... | collective-permute-start | bytes 589832 | tf_op jit(solution)/shard_map/while/body/eval_jaxpr/ppermute | solution.py:19
  136.5 7.3 %collective-permute-start = (bf16[128,768]{1,0:T(8,128)(2,1)S(1)}, bf16[128,768]{1,0:T(8,128)(2,1)S(1)}, u32[]{:S(2)}, u32[]{:S(2)}) collective-permute-start(bf16[128,768]{1,0:T(8,128)(2,1)S(1)} %get-tuple-element.853), channel_id=1, source_target_pairs={{0,8},{8,16},{16,24},{24,32},{32,40},{40,48},{48,56},{56,64},{64,7... | collective-permute-start | bytes 589832 | tf_op jit(solution)/shard_map/while/body/eval_jaxpr/ppermute | solution.py:19
  143.8 7.3 %collective-permute-start = (bf16[128,768]{1,0:T(8,128)(2,1)S(1)}, bf16[128,768]{1,0:T(8,128)(2,1)S(1)}, u32[]{:S(2)}, u32[]{:S(2)}) collective-permute-start(bf16[128,768]{1,0:T(8,128)(2,1)S(1)} %get-tuple-element.853), channel_id=1, source_target_pairs={{0,8},{8,16},{16,24},{24,32},{32,40},{40,48},{48,56},{56,64},{64,7... | collective-permute-start | bytes 589832 | tf_op jit(solution)/shard_map/while/body/eval_jaxpr/ppermute | solution.py:19
  151.1 7.3 %collective-permute-start = (bf16[128,768]{1,0:T(8,128)(2,1)S(1)}, bf16[128,768]{1,0:T(8,128)(2,1)S(1)}, u32[]{:S(2)}, u32[]{:S(2)}) collective-permute-start(bf16[128,768]{1,0:T(8,128)(2,1)S(1)} %get-tuple-element.853), channel_id=1, source_target_pairs={{0,8},{8,16},{16,24},{24,32},{32,40},{40,48},{48,56},{56,64},{64,7... | collective-permute-start | bytes 589832 | tf_op jit(solution)/shard_map/while/body/eval_jaxpr/ppermute | solution.py:19
  158.4 7.3 %collective-permute-start = (bf16[128,768]{1,0:T(8,128)(2,1)S(1)}, bf16[128,768]{1,0:T(8,128)(2,1)S(1)}, u32[]{:S(2)}, u32[]{:S(2)}) collective-permute-start(bf16[128,768]{1,0:T(8,128)(2,1)S(1)} %get-tuple-element.853), channel_id=1, source_target_pairs={{0,8},{8,16},{16,24},{24,32},{32,40},{40,48},{48,56},{56,64},{64,7... | collective-permute-start | bytes 589832 | tf_op jit(solution)/shard_map/while/body/eval_jaxpr/ppermute | solution.py:19
  165.7 7.3 %collective-permute-start = (bf16[128,768]{1,0:T(8,128)(2,1)S(1)}, bf16[128,768]{1,0:T(8,128)(2,1)S(1)}, u32[]{:S(2)}, u32[]{:S(2)}) collective-permute-start(bf16[128,768]{1,0:T(8,128)(2,1)S(1)} %get-tuple-element.853), channel_id=1, source_target_pairs={{0,8},{8,16},{16,24},{24,32},{32,40},{40,48},{48,56},{56,64},{64,7... | collective-permute-start | bytes 589832 | tf_op jit(solution)/shard_map/while/body/eval_jaxpr/ppermute | solution.py:19
  173.0 7.3 %collective-permute-start = (bf16[128,768]{1,0:T(8,128)(2,1)S(1)}, bf16[128,768]{1,0:T(8,128)(2,1)S(1)}, u32[]{:S(2)}, u32[]{:S(2)}) collective-permute-start(bf16[128,768]{1,0:T(8,128)(2,1)S(1)} %get-tuple-element.853), channel_id=1, source_target_pairs={{0,8},{8,16},{16,24},{24,32},{32,40},{40,48},{48,56},{56,64},{64,7... | collective-permute-start | bytes 589832 | tf_op jit(solution)/shard_map/while/body/eval_jaxpr/ppermute | solution.py:19
  180.4 7.3 %collective-permute-start = (bf16[128,768]{1,0:T(8,128)(2,1)S(1)}, bf16[128,768]{1,0:T(8,128)(2,1)S(1)}, u32[]{:S(2)}, u32[]{:S(2)}) collective-permute-start(bf16[128,768]{1,0:T(8,128)(2,1)S(1)} %get-tuple-element.853), channel_id=1, source_target_pairs={{0,8},{8,16},{16,24},{24,32},{32,40},{40,48},{48,56},{56,64},{64,7... | collective-permute-start | bytes 589832 | tf_op jit(solution)/shard_map/while/body/eval_jaxpr/ppermute | solution.py:19
  187.7 7.3 %collective-permute-start = (bf16[128,768]{1,0:T(8,128)(2,1)S(1)}, bf16[128,768]{1,0:T(8,128)(2,1)S(1)}, u32[]{:S(2)}, u32[]{:S(2)}) collective-permute-start(bf16[128,768]{1,0:T(8,128)(2,1)S(1)} %get-tuple-element.853), channel_id=1, source_target_pairs={{0,8},{8,16},{16,24},{24,32},{32,40},{40,48},{48,56},{56,64},{64,7... | collective-permute-start | bytes 589832 | tf_op jit(solution)/shard_map/while/body/eval_jaxpr/ppermute | solution.py:19
  195.0 7.3 %collective-permute-start = (bf16[128,768]{1,0:T(8,128)(2,1)S(1)}, bf16[128,768]{1,0:T(8,128)(2,1)S(1)}, u32[]{:S(2)}, u32[]{:S(2)}) collective-permute-start(bf16[128,768]{1,0:T(8,128)(2,1)S(1)} %get-tuple-element.853), channel_id=1, source_target_pairs={{0,8},{8,16},{16,24},{24,32},{32,40},{40,48},{48,56},{56,64},{64,7... | collective-permute-start | bytes 589832 | tf_op jit(solution)/shard_map/while/body/eval_jaxpr/ppermute | solution.py:19
  202.3 7.3 %collective-permute-start = (bf16[128,768]{1,0:T(8,128)(2,1)S(1)}, bf16[128,768]{1,0:T(8,128)(2,1)S(1)}, u32[]{:S(2)}, u32[]{:S(2)}) collective-permute-start(bf16[128,768]{1,0:T(8,128)(2,1)S(1)} %get-tuple-element.853), channel_id=1, source_target_pairs={{0,8},{8,16},{16,24},{24,32},{32,40},{40,48},{48,56},{56,64},{64,7... | collective-permute-start | bytes 589832 | tf_op jit(solution)/shard_map/while/body/eval_jaxpr/ppermute | solution.py:19
  209.7 7.3 %collective-permute-start = (bf16[128,768]{1,0:T(8,128)(2,1)S(1)}, bf16[128,768]{1,0:T(8,128)(2,1)S(1)}, u32[]{:S(2)}, u32[]{:S(2)}) collective-permute-start(bf16[128,768]{1,0:T(8,128)(2,1)S(1)} %get-tuple-element.853), channel_id=1, source_target_pairs={{0,8},{8,16},{16,24},{24,32},{32,40},{40,48},{48,56},{56,64},{64,7... | collective-permute-start | bytes 589832 | tf_op jit(solution)/shard_map/while/body/eval_jaxpr/ppermute | solution.py:19
  217.0 7.3 %collective-permute-start = (bf16[128,768]{1,0:T(8,128)(2,1)S(1)}, bf16[128,768]{1,0:T(8,128)(2,1)S(1)}, u32[]{:S(2)}, u32[]{:S(2)}) collective-permute-start(bf16[128,768]{1,0:T(8,128)(2,1)S(1)} %get-tuple-element.853), channel_id=1, source_target_pairs={{0,8},{8,16},{16,24},{24,32},{32,40},{40,48},{48,56},{56,64},{64,7... | collective-permute-start | bytes 589832 | tf_op jit(solution)/shard_map/while/body/eval_jaxpr/ppermute | solution.py:19
  224.4 7.3 %collective-permute-start = (bf16[128,768]{1,0:T(8,128)(2,1)S(1)}, bf16[128,768]{1,0:T(8,128)(2,1)S(1)}, u32[]{:S(2)}, u32[]{:S(2)}) collective-permute-start(bf16[128,768]{1,0:T(8,128)(2,1)S(1)} %get-tuple-element.853), channel_id=1, source_target_pairs={{0,8},{8,16},{16,24},{24,32},{32,40},{40,48},{48,56},{56,64},{64,7... | collective-permute-start | bytes 589832 | tf_op jit(solution)/shard_map/while/body/eval_jaxpr/ppermute | solution.py:19
  231.7 7.3 %collective-permute-start = (bf16[128,768]{1,0:T(8,128)(2,1)S(1)}, bf16[128,768]{1,0:T(8,128)(2,1)S(1)}, u32[]{:S(2)}, u32[]{:S(2)}) collective-permute-start(bf16[128,768]{1,0:T(8,128)(2,1)S(1)} %get-tuple-element.853), channel_id=1, source_target_pairs={{0,8},{8,16},{16,24},{24,32},{32,40},{40,48},{48,56},{56,64},{64,7... | collective-permute-start | bytes 589832 | tf_op jit(solution)/shard_map/while/body/eval_jaxpr/ppermute | solution.py:19
  239.1 7.3 %collective-permute-start = (bf16[128,768]{1,0:T(8,128)(2,1)S(1)}, bf16[128,768]{1,0:T(8,128)(2,1)S(1)}, u32[]{:S(2)}, u32[]{:S(2)}) collective-permute-start(bf16[128,768]{1,0:T(8,128)(2,1)S(1)} %get-tuple-element.853), channel_id=1, source_target_pairs={{0,8},{8,16},{16,24},{24,32},{32,40},{40,48},{48,56},{56,64},{64,7... | collective-permute-start | bytes 589832 | tf_op jit(solution)/shard_map/while/body/eval_jaxpr/ppermute | solution.py:19
  246.4 1.1 copy-start.1
  249.5 1.9 copy-start.5
  254.5 1.5 copy-start.2
  409.0 7.4 %copy-start.3 = (bf16[128,384]{1,0:T(8,128)(2,1)S(1)}, bf16[128,384]{1,0:T(8,128)(2,1)}, u32[]{:S(2)}) copy-start(bf16[128,384]{1,0:T(8,128)(2,1)} %param.15) | copy-start | bytes 294916
  409.0 7.5 %copy-start.4 = (bf16[128,384]{1,0:T(8,128)(2,1)S(1)}, bf16[128,384]{1,0:T(8,128)(2,1)}, u32[]{:S(2)}) copy-start(bf16[128,384]{1,0:T(8,128)(2,1)} %param.16) | copy-start | bytes 294916
  512.5 4.4 copy-start
  518.0 5.1 collective-permute-start.1
  519.9 8.0 %collective-permute-start.2 = (bf16[128,768]{0,1:T(8,128)(2,1)S(1)}, bf16[128,768]{0,1:T(8,128)(2,1)S(1)}, u32[]{:S(2)}, u32[]{:S(2)}) collective-permute-start(bf16[128,768]{0,1:T(8,128)(2,1)S(1)} %get-tuple-element.844), channel_id=1, source_target_pairs={{0,8},{8,16},{16,24},{24,32},{32,40},{40,48},{48,56},{56,64},{64,7... | collective-permute-start | bytes 589832 | tf_op jit(solution)/shard_map/while/body/eval_jaxpr/ppermute | solution.py:25
  528.0 4.4 copy-start
  533.4 5.1 collective-permute-start.1
  535.4 7.9 %collective-permute-start.2 = (bf16[128,768]{0,1:T(8,128)(2,1)S(1)}, bf16[128,768]{0,1:T(8,128)(2,1)S(1)}, u32[]{:S(2)}, u32[]{:S(2)}) collective-permute-start(bf16[128,768]{0,1:T(8,128)(2,1)S(1)} %get-tuple-element.844), channel_id=1, source_target_pairs={{0,8},{8,16},{16,24},{24,32},{32,40},{40,48},{48,56},{56,64},{64,7... | collective-permute-start | bytes 589832 | tf_op jit(solution)/shard_map/while/body/eval_jaxpr/ppermute | solution.py:25
  543.3 4.4 copy-start
  548.7 5.1 collective-permute-start.1
  550.7 7.9 %collective-permute-start.2 = (bf16[128,768]{0,1:T(8,128)(2,1)S(1)}, bf16[128,768]{0,1:T(8,128)(2,1)S(1)}, u32[]{:S(2)}, u32[]{:S(2)}) collective-permute-start(bf16[128,768]{0,1:T(8,128)(2,1)S(1)} %get-tuple-element.844), channel_id=1, source_target_pairs={{0,8},{8,16},{16,24},{24,32},{32,40},{40,48},{48,56},{56,64},{64,7... | collective-permute-start | bytes 589832 | tf_op jit(solution)/shard_map/while/body/eval_jaxpr/ppermute | solution.py:25
  558.6 4.4 copy-start
  564.0 5.1 collective-permute-start.1
  566.0 7.9 %collective-permute-start.2 = (bf16[128,768]{0,1:T(8,128)(2,1)S(1)}, bf16[128,768]{0,1:T(8,128)(2,1)S(1)}, u32[]{:S(2)}, u32[]{:S(2)}) collective-permute-start(bf16[128,768]{0,1:T(8,128)(2,1)S(1)} %get-tuple-element.844), channel_id=1, source_target_pairs={{0,8},{8,16},{16,24},{24,32},{32,40},{40,48},{48,56},{56,64},{64,7... | collective-permute-start | bytes 589832 | tf_op jit(solution)/shard_map/while/body/eval_jaxpr/ppermute | solution.py:25
  573.9 4.4 copy-start
  579.3 5.1 collective-permute-start.1
  581.3 7.9 %collective-permute-start.2 = (bf16[128,768]{0,1:T(8,128)(2,1)S(1)}, bf16[128,768]{0,1:T(8,128)(2,1)S(1)}, u32[]{:S(2)}, u32[]{:S(2)}) collective-permute-start(bf16[128,768]{0,1:T(8,128)(2,1)S(1)} %get-tuple-element.844), channel_id=1, source_target_pairs={{0,8},{8,16},{16,24},{24,32},{32,40},{40,48},{48,56},{56,64},{64,7... | collective-permute-start | bytes 589832 | tf_op jit(solution)/shard_map/while/body/eval_jaxpr/ppermute | solution.py:25
  589.2 4.4 copy-start
  594.6 5.1 collective-permute-start.1
  596.6 7.9 %collective-permute-start.2 = (bf16[128,768]{0,1:T(8,128)(2,1)S(1)}, bf16[128,768]{0,1:T(8,128)(2,1)S(1)}, u32[]{:S(2)}, u32[]{:S(2)}) collective-permute-start(bf16[128,768]{0,1:T(8,128)(2,1)S(1)} %get-tuple-element.844), channel_id=1, source_target_pairs={{0,8},{8,16},{16,24},{24,32},{32,40},{40,48},{48,56},{56,64},{64,7... | collective-permute-start | bytes 589832 | tf_op jit(solution)/shard_map/while/body/eval_jaxpr/ppermute | solution.py:25
  604.5 4.4 copy-start
  610.0 5.1 collective-permute-start.1
  611.9 7.9 %collective-permute-start.2 = (bf16[128,768]{0,1:T(8,128)(2,1)S(1)}, bf16[128,768]{0,1:T(8,128)(2,1)S(1)}, u32[]{:S(2)}, u32[]{:S(2)}) collective-permute-start(bf16[128,768]{0,1:T(8,128)(2,1)S(1)} %get-tuple-element.844), channel_id=1, source_target_pairs={{0,8},{8,16},{16,24},{24,32},{32,40},{40,48},{48,56},{56,64},{64,7... | collective-permute-start | bytes 589832 | tf_op jit(solution)/shard_map/while/body/eval_jaxpr/ppermute | solution.py:25
Sparse Core Ops, SparseCore 0:
  9.9 76.3 all-gather.1
  416.5 91.5 reduce-scatter.3
where the time goes:
time: 639 us; the launch traced here: 630 us
  waiting for transfers between devices  280 us (44%)
  blocking collectives  147 us (23%)
  starting transfers between devices  101 us (16%)
  local copies, waits for them, and re-layouts  36.7 us (6%)
  between operations  23.7 us (4%)
  matrix products  23.5 us (4%)
  loops' own time  11.6 us (2%)
    ppermute x31, waiting for transfers between devices, shifted(): return lax.ppermute(value, axis, pairs)  153 us
    psum x1, blocking collectives, body(): lax.psum(jnp.sum(activated * activated, axis=0), 'seq') / total_rows  110 us
    unnamed x3, waiting for transfers between devices  90.9 us
    ppermute x31, starting transfers between devices, shifted(): return lax.ppermute(value, axis, pairs)  70.3 us
    all_gather x1, blocking collectives, body(): full_rows = lax.all_gather(attn_out, 'fsdp', axis=1, tiled=True)  37 us
    ppermute x14, waiting for transfers between devices, passed_along(): lax.ppermute(value, axis, [(source, source + steps) for source in range(f...  36.6 us
    ppermute x14, starting transfers between devices, passed_along(): lax.ppermute(value, axis, [(source, source + steps) for source in range(f...  30.3 us
  transfers between devices with their start and end apart: 47, of which 46 were waited for; matrix products, arithmetic and copies ran while one was open for 3% of the time, Pallas kernels for 0%

commit v1 on v0

v1 whole, which is shorter than its diff:
```python
import functools

import jax
import jax.numpy as jnp
from jax import lax
from jax.experimental import pallas as pl
from jax.experimental.pallas import tpu as pltpu
from jax.sharding import Mesh, PartitionSpec as P

HD = 128
TILE = 128
TOKENS = 4096
EPSILON = 1e-05
MASKED = -1e30
ROOT = 0.7978845608028654
CUBIC = 0.044715
PLANES = 8
NEAR = ((0, 0), (0, -1), (0, 1), (1, 0), (1, -1), (1, 1))
SEQ = ("z", "xl", "core")
FSDP = ("y", "xh")
NT = (((1,), (1,)), ((), ()))
TN = (((0,), (0,)), ((), ()))
VMEM = pltpu.VMEM
SMEM = pltpu.SMEM


def dot(a, b, dims=(((1,), (0,)), ((), ()))):
    return lax.dot_general(a, b, dims, preferred_element_type=jnp.float32)


def attend_kernel(place, mask, query, near_a, near_b, out, probs):
    z, xl, core = place[0], place[1], place[2]
    me = 4 * z + 2 * xl + core

    def bias_row(other_core):
        parts = []
        for dx, dz in NEAR:
            plane = z + dz
            inside = (plane >= 0) & (plane < PLANES)
            tile = 4 * jnp.clip(plane, 0, PLANES - 1) + 2 * (xl if dx == 0 else 1 - xl) + (1 - core if other_core else core)
            value = jnp.where(inside & (mask[me, tile] > 0), 0.0, MASKED).astype(jnp.float32)
            parts.append(jnp.full((1, TILE), value, jnp.float32))
        return jnp.concatenate(parts, axis=1)

    bias_a, bias_b = bias_row(False), bias_row(True)
    width = near_a.shape[1] // 2
    half = near_a.shape[0]
    scale = HD ** (-0.5)
    for head in range(width // HD):
        cols = slice(head * HD, (head + 1) * HD)
        vcols = slice(width + head * HD, width + (head + 1) * HD)
        q = query[:, cols]
        s_a = dot(q, near_a[:, cols], NT) * scale + bias_a
        s_b = dot(q, near_b[:, cols], NT) * scale + bias_b
        top = jnp.maximum(jnp.max(s_a, axis=1, keepdims=True), jnp.max(s_b, axis=1, keepdims=True))
        e_a = jnp.exp(s_a - top)
        e_b = jnp.exp(s_b - top)
        inv = 1.0 / (jnp.sum(e_a, axis=1, keepdims=True) + jnp.sum(e_b, axis=1, keepdims=True))
        p_a = e_a * inv
        p_b = e_b * inv
        probs[head, :, :half] = p_a
        probs[head, :, half:] = p_b
        mixed = dot(p_a.astype(jnp.bfloat16), near_a[:, vcols]) + dot(p_b.astype(jnp.bfloat16), near_b[:, vcols])
        out[:, :, cols] = jnp.broadcast_to(mixed.astype(jnp.bfloat16)[None], (out.shape[0],) + mixed.shape)


def attend(place, mask, query, near_a, near_b, copies):
    rows, width = query.shape
    heads = width // HD
    keys = 2 * near_a.shape[0]
    return pl.pallas_call(
        attend_kernel,
        out_shape=(
            jax.ShapeDtypeStruct((copies, rows, width), jnp.bfloat16),
            jax.ShapeDtypeStruct((heads, rows, keys), jnp.float32),
        ),
        in_specs=[pl.BlockSpec(memory_space=SMEM)] * 2 + [pl.BlockSpec(memory_space=VMEM)] * 3,
        out_specs=(pl.BlockSpec(memory_space=VMEM),) * 2,
        compiler_params=pltpu.CompilerParams(vmem_limit_bytes=24 << 20),
        cost_estimate=pl.CostEstimate(flops=4 * rows * keys * width, bytes_accessed=8 << 20, transcendentals=heads * rows * keys),
    )(place, mask, query, near_a, near_b)


def up_kernel(rows_in, weight, cot, act_out, slope_out, sums, total):
    step = pl.program_id(0)
    part = dot(rows_in[0], weight[...])

    @pl.when(step == 0)
    def _():
        total[...] = part

    @pl.when(step > 0)
    def _():
        total[...] += part

    @pl.when(step == pl.num_programs(0) - 1)
    def _():
        width = total.shape[1]
        chunks = width // 128
        for r in range(chunks):
            cols = slice(r * 128, (r + 1) * 128)
            v = total[:, cols]
            t = jnp.tanh(ROOT * (v + CUBIC * (v * v * v)))
            act = 0.5 * v * (1.0 + t)
            act_out[:, cols] = act
            slope_out[:, cols] = 0.5 * (1.0 + t) + 0.5 * v * (1.0 - t * t) * (ROOT * (1.0 + 3.0 * CUBIC * (v * v)))
            power = jnp.sum(act * act, axis=0, keepdims=True)
            pull = jnp.sum(act * cot[:, cols].astype(jnp.float32), axis=0, keepdims=True)
            sums[:, r : r + 1, :] = jnp.broadcast_to(power[None], (sums.shape[0], 1, 128))
            sums[:, chunks + r : chunks + r + 1, :] = jnp.broadcast_to(pull[None], (sums.shape[0], 1, 128))
        rest = sums.shape[1] - 2 * chunks
        sums[:, 2 * chunks :, :] = jnp.zeros((sums.shape[0], rest, 128), jnp.float32)


def up(rows_in, weight, cot, copies):
    parts, rows, depth = rows_in.shape
    width = weight.shape[1]
    lines = -(-2 * (width // 128) // 8) * 8
    return pl.pallas_call(
        up_kernel,
        grid=(parts,),
        out_shape=(
            jax.ShapeDtypeStruct((rows, width), jnp.float32),
            jax.ShapeDtypeStruct((rows, width), jnp.float32),
            jax.ShapeDtypeStruct((copies, lines, 128), jnp.float32),
        ),
        in_specs=[
            pl.BlockSpec((1, rows, depth), lambda i: (i, 0, 0)),
            pl.BlockSpec((depth, width), lambda i: (i, 0)),
            pl.BlockSpec((rows, width), lambda i: (0, 0)),
        ],
        out_specs=(
            pl.BlockSpec((rows, width), lambda i: (0, 0)),
            pl.BlockSpec((rows, width), lambda i: (0, 0)),
            pl.BlockSpec((copies, lines, 128), lambda i: (0, 0, 0)),
        ),
        scratch_shapes=[pltpu.VMEM((rows, width), jnp.float32)],
        compiler_params=pltpu.CompilerParams(vmem_limit_bytes=24 << 20),
        cost_estimate=pl.CostEstimate(
            flops=2 * rows * width * parts * depth, bytes_accessed=weight.size * 2, transcendentals=rows * width
        ),
    )(rows_in, weight, cot)


def down_kernel(act, slope, cot, sums, weight, out, scaled, grad):
    @pl.when(pl.program_id(0) == 0)
    def _():
        chunks = act.shape[1] // 128
        total = jnp.sum(sums[...], axis=0)
        for r in range(chunks):
            cols = slice(r * 128, (r + 1) * 128)
            a = act[:, cols]
            c = cot[:, cols].astype(jnp.float32)
            inv = lax.rsqrt(total[r : r + 1, :] * (1.0 / TOKENS) + EPSILON)
            pull = total[chunks + r : chunks + r + 1, :]
            scaled[:, cols] = (a * inv).astype(jnp.bfloat16)
            back = pull * -0.5 * inv * inv * inv * (2.0 / TOKENS)
            grad[:, cols] = ((c * inv + back * a) * slope[:, cols]).astype(jnp.bfloat16)

    out[0] = dot(grad[...], weight[...], NT).astype(jnp.bfloat16)


def down(act, slope, cot, sums, weight, parts):
    rows, width = act.shape
    depth = weight.shape[0] // parts
    whole = lambda i: (0, 0)
    return pl.pallas_call(
        down_kernel,
        grid=(parts,),
        out_shape=(
            jax.ShapeDtypeStruct((parts, rows, depth), jnp.bfloat16),
            jax.ShapeDtypeStruct((rows, width), jnp.bfloat16),
        ),
        in_specs=[
            pl.BlockSpec((rows, width), whole),
            pl.BlockSpec((rows, width), whole),
            pl.BlockSpec((rows, width), whole),
            pl.BlockSpec(sums.shape, lambda i: (0, 0, 0)),
            pl.BlockSpec((depth, width), lambda i: (i, 0)),
        ],
        out_specs=(
            pl.BlockSpec((1, rows, depth), lambda i: (i, 0, 0)),
            pl.BlockSpec((rows, width), whole),
        ),
        scratch_shapes=[pltpu.VMEM((rows, width), jnp.bfloat16)],
        compiler_params=pltpu.CompilerParams(vmem_limit_bytes=24 << 20),
        cost_estimate=pl.CostEstimate(
            flops=2 * rows * width * parts * depth, bytes_accessed=weight.size * 2, transcendentals=0
        ),
    )(act, slope, cot, sums, weight)


def backward_kernel(query, near_a, near_b, attn, probs, partial, grad_query, grad_a, grad_b):
    width = query.shape[1]
    half = near_a.shape[0]
    scale = HD ** (-0.5)
    for head in range(width // HD):
        cols = slice(head * HD, (head + 1) * HD)
        vcols = slice(width + head * HD, width + (head + 1) * HD)
        grad = partial[0, :, cols].astype(jnp.float32)
        for i in range(1, partial.shape[0]):
            grad = grad + partial[i, :, cols].astype(jnp.float32)
        g = grad.astype(jnp.bfloat16)
        delta = jnp.sum(g.astype(jnp.float32) * attn[0, :, cols].astype(jnp.float32), axis=1, keepdims=True)
        q = query[:, cols]
        out = None
        for side, (near, result) in enumerate(((near_a, grad_a), (near_b, grad_b))):
            p = probs[head, :, side * half : (side + 1) * half]
            d = (p * (dot(g, near[:, vcols], NT) - delta)).astype(jnp.bfloat16)
            term = dot(d, near[:, cols])
            out = term if out is None else out + term
            result[:, cols] = (dot(d, q, TN) * scale).astype(jnp.bfloat16)
            result[:, vcols] = dot(p.astype(jnp.bfloat16), g, TN).astype(jnp.bfloat16)
        grad_query[:, cols] = out * scale


def backward(query, near_a, near_b, attn, probs, partial):
    rows, width = query.shape
    copies = attn.shape[0]
    return pl.pallas_call(
        backward_kernel,
        grid=(1,),
        out_shape=(
            jax.ShapeDtypeStruct((rows, width), jnp.float32),
            jax.ShapeDtypeStruct(near_a.shape, jnp.bfloat16),
            jax.ShapeDtypeStruct(near_b.shape, jnp.bfloat16),
        ),
        in_specs=[
            pl.BlockSpec(query.shape, lambda i: (0, 0)),
            pl.BlockSpec(near_a.shape, lambda i: (0, 0)),
            pl.BlockSpec(near_b.shape, lambda i: (0, 0)),
            pl.BlockSpec((1,) + attn.shape[1:], lambda i: (0, 0, 0)),
            pl.BlockSpec(probs.shape, lambda i: (0, 0, 0)),
            pl.BlockSpec(partial.shape, lambda i: (0, 0, 0)),
        ],
        out_specs=(
            pl.BlockSpec((rows, width), lambda i: (0, 0)),
            pl.BlockSpec(near_a.shape, lambda i: (0, 0)),
            pl.BlockSpec(near_b.shape, lambda i: (0, 0)),
        ),
        compiler_params=pltpu.CompilerParams(vmem_limit_bytes=32 << 20),
        cost_estimate=pl.CostEstimate(
            flops=8 * rows * 2 * near_a.shape[0] * width, bytes_accessed=8 << 20, transcendentals=0
        ),
    )(query, near_a, near_b, attn, probs, partial)


def swap(value, axis):
    return lax.ppermute(value, axis, [(0, 1), (1, 0)])


def up_plane(value):
    return lax.ppermute(value, "z", [(i, (i + 1) % PLANES) for i in range(PLANES)])


def down_plane(value):
    return lax.ppermute(value, "z", [(i, (i - 1) % PLANES) for i in range(PLANES)])


def body(query, key, value, tile_mask, weight, cot):
    rows, width = query.shape
    place = jnp.stack([lax.axis_index("z"), lax.axis_index("xl"), lax.axis_index("core")]).astype(jnp.int32)
    full_weight = lax.all_gather(weight, SEQ, axis=0, tiled=True)
    own = jnp.concatenate([key, value], axis=1)
    from_low = up_plane(own)
    from_high = down_plane(own)
    own_x = swap(own, "xl")
    far_x = swap(jnp.concatenate([from_low, from_high], axis=0), "xl")
    near_a = jnp.concatenate([own, from_low, from_high, own_x, far_x], axis=0)
    near_b = swap(near_a, "core")
    copies = lax.axis_size(FSDP)
    attn, probs = attend(place, tile_mask, query, near_a, near_b, copies)
    full_rows = lax.all_to_all(attn, FSDP, 0, 0)
    act, slope, sums = up(full_rows, full_weight, cot, lax.axis_size(SEQ))
    sums = lax.all_to_all(sums, SEQ, 0, 0)
    back, scaled = down(act, slope, cot, sums, full_weight, copies)
    partial = lax.all_to_all(back, FSDP, 0, 0)
    grad_query, grad_a, grad_b = backward(query, near_a, near_b, attn, probs, partial)
    f32 = jnp.float32
    grad_a = grad_a.astype(f32) + swap(grad_b, "core").astype(f32)
    side = grad_a[3 * rows :].astype(jnp.bfloat16)
    mine = grad_a[: 3 * rows] + swap(side, "xl").astype(f32)
    far = mine[rows:].astype(jnp.bfloat16)
    grad_own = mine[:rows] + down_plane(far[:rows]).astype(f32) + up_plane(far[rows:]).astype(f32)
    return scaled, grad_query, grad_own[:, :width], grad_own[:, width:]


def solution(mesh):
    fine = Mesh(mesh.devices.reshape(PLANES, 2, 2, 4, 2), SEQ + FSDP)
    both = P(SEQ, FSDP)
    return jax.shard_map(
        body,
        mesh=fine,
        in_specs=(both, both, both, P(), both, both),
        out_specs=(both,) * 4,
        check_vma=False,
    )
```

time: 639 us -> 181 us (0.28); the launches traced: 630 us -> 181 us
  waiting for transfers between devices: 280 us -> 63.5 us
  starting transfers between devices: 101 us -> 11.1 us
  blocking collectives: 147 us -> 69.6 us
  local copies, waits for them, and re-layouts: 36.7 us -> 8.62 us
  matrix products: 23.5 us -> 0 us
  Pallas kernels: 0 us -> 13.5 us
  loops' own time: 11.6 us -> 0 us
  between operations: 23.7 us -> 14.2 us
    ppermute x45 -> x9, waiting for transfers between devices: 189 us -> 58.4 us  [the longest x5 45.4 us: swap(): return lax.ppermute(value, axis, [(0, 1), (1, 0)])]
    psum x1 -> x0, blocking collectives: 110 us -> none  [body(): lax.psum(jnp.sum(activated * activated, axis=0), 'seq') / total_rows]
    unnamed x3 -> x1, waiting for transfers between devices: 90.9 us -> 0.68 us
    ppermute x45 -> x9, starting transfers between devices: 101 us -> 11.1 us  [the longest x2 6.02 us: down_plane(): lax.ppermute(value, 'z', [(i, (i - 1) % PLANES) for i in range(PLANES)])]
    all_to_all x0 -> x3, blocking collectives: none -> 69.6 us  [the longest x1 29.4 us: body(): full_rows = lax.all_to_all(attn, FSDP, 0, 0)]
    all_gather x1 -> x0, blocking collectives: 37 us -> none  [body(): full_rows = lax.all_gather(attn_out, 'fsdp', axis=1, tiled=True)]
    dot_general x44 -> x0, matrix products: 23.5 us -> none  [the longest x1 6.14 us: body(): lax.dot_general(grad_hidden, lax.all_gather(up_weight, 'seq', axis=0, til...]
    dynamic_slice x29 -> x0, local copies, waits for them, and re-layouts: 20.9 us -> none  [the longest x8 11.9 us: tile_block(): lax.dynamic_slice(tile_mask, (row_start, col_start), (tiles_here, tiles_h...]
  transfers between devices with their start and end apart: 47 -> 10, of which waited for: 46 -> 9; matrix products, arithmetic and copies ran while one was open for 3% -> 1% of each run, Pallas kernels for 0% -> 1%
where the time goes in v1:
time: 181 us
  blocking collectives  69.6 us (38%)
  waiting for transfers between devices  63.5 us (35%)
  between operations  14.2 us (8%)
  Pallas kernels  13.5 us (7%)
  starting transfers between devices  11.1 us (6%)
  local copies, waits for them, and re-layouts  8.62 us (5%)
    ppermute x5, waiting for transfers between devices, swap(): return lax.ppermute(value, axis, [(0, 1), (1, 0)])  45.4 us
    all_to_all x1, blocking collectives, body(): full_rows = lax.all_to_all(attn, FSDP, 0, 0)  29.4 us
    all_to_all x1, blocking collectives, body(): sums = lax.all_to_all(sums, SEQ, 0, 0)  20.5 us
    all_to_all x1, blocking collectives, body(): partial = lax.all_to_all(back, FSDP, 0, 0)  19.7 us
    ppermute x2, waiting for transfers between devices, down_plane(): lax.ppermute(value, 'z', [(i, (i - 1) % PLANES) for i in range(PLANES)])  8.25 us
    unnamed x22, local copies, waits for them, and re-layouts  6.81 us
    ppermute x2, starting transfers between devices, down_plane(): lax.ppermute(value, 'z', [(i, (i - 1) % PLANES) for i in range(PLANES)])  6.02 us
    ppermute x2, waiting for transfers between devices, up_plane(): lax.ppermute(value, 'z', [(i, (i + 1) % PLANES) for i in range(PLANES)])  4.71 us
  transfers between devices with their start and end apart: 10, of which 9 were waited for; matrix products, arithmetic and copies ran while one was open for 1% of the time, Pallas kernels for 1%

profile of v1, /device:TPU:2, one launch (start us, length us, event | category | flops | bytes accessed | tf_op | source)
XLA Modules:
  0.0 181.1 jit_solution(16644718004502222696)
XLA Ops:
  7.2 0.0 all-gather.2.cloned.1.call-start
  7.2 0.7 all-gather.2.cloned.1.call-update
  7.9 0.9 constant_dynamic-update-slice_fusion.1
  8.8 0.9 constant_dynamic-update-slice_fusion
  9.7 5.9 %collective-permute-start.1 = (bf16[128,768]{1,0:T(8,128)(2,1)S(1)}, bf16[128,768]{1,0:T(8,128)(2,1)S(1)}, u32[]{:S(2)}, u32[]{:S(2)}) collective-permute-start(bf16[128,768]{1,0:T(8,128)(2,1)S(1)} %get-tuple-element.30), channel_id=1, source_target_pairs={{0,224},{32,0},{64,32},{96,64},{128,96},{160,128},{192,160},{224,1... | collective-permute-start | bytes 589832 | tf_op jit(solution)/shard_map/ppermute | solution.py:257
  15.7 0.0 collective-permute-start
  15.7 4.2 %collective-permute-done.1 = bf16[128,768]{1,0:T(8,128)(2,1)S(1)} collective-permute-done((bf16[128,768]{1,0:T(8,128)(2,1)S(1)}, bf16[128,768]{1,0:T(8,128)(2,1)S(1)}, u32[]{:S(2)}, u32[]{:S(2)}) %collective-permute-start.1) | collective-permute-done | bytes 196640 | tf_op jit(solution)/shard_map/ppermute | solution.py:257
  19.8 3.4 %collective-permute-done = bf16[128,768]{1,0:T(8,128)(2,1)S(1)} collective-permute-done((bf16[128,768]{1,0:T(8,128)(2,1)S(1)}, bf16[128,768]{1,0:T(8,128)(2,1)S(1)}, u32[]{:S(2)}, u32[]{:S(2)}) %collective-permute-start) | collective-permute-done | bytes 196640 | tf_op jit(solution)/shard_map/ppermute | solution.py:253
  23.3 0.0 copy-start.6
  23.3 0.0 copy-start.8
  23.3 0.6 collective-permute-start.3
  23.9 1.5 collective-permute-start.2
  25.5 25.2 %collective-permute-done.2 = bf16[128,768]{1,0:T(8,128)(2,1)S(1)} collective-permute-done((bf16[128,768]{1,0:T(8,128)(2,1)S(1)}, bf16[128,768]{1,0:T(8,128)(2,1)S(1)}, u32[]{:S(2)}, u32[]{:S(2)}) %collective-permute-start.2) | collective-permute-done | bytes 196640 | tf_op jit(solution)/shard_map/ppermute | solution.py:249
  50.7 0.0 collective-permute-done.3
  50.7 0.1 collective-permute-start.4
  50.8 0.1 pad_add_fusion.place
  50.9 2.8 %collective-permute-done.4.near_b = bf16[768,768]{1,0:T(8,128)(2,1)S(1)} collective-permute-done((bf16[768,768]{1,0:T(8,128)(2,1)S(1)}, bf16[768,768]{1,0:T(8,128)(2,1)S(1)}, u32[]{:S(2)}, u32[]{:S(2)}) %collective-permute-start.4) | collective-permute-done | bytes 1179680 | tf_op jit(solution)/shard_map/ppermute | solution.py:249
  53.7 0.0 copy-done.6
  53.7 0.0 copy-done.8
  53.7 2.6 %shard_map.93 = (bf16[8,128,384]{2,1,0:T(8,128)(2,1)S(1)}, f32[3,128,1536]{2,1,0:T(8,128)S(1)}) custom-call(s32[3]{0:T(128)S(1)} %pad_add_fusion.place, s32[32,32]{1,0:T(8,128)S(1)} %copy-done.8, bf16[128,384]{1,0:T(8,128)(2,1)S(1)} %copy-done.6, bf16[768,768]{1,0:T(8,128)(2,1)S(1)} %constant_dynamic-update-slice_fusion.2.near_a, ...), custom_call_target="tpu_custom_call" | custom-call | flops 301989888 | bytes 8388608 | tf_op jit(solution)/shard_map/pallas_call | solution.py:71
  56.3 0.0 copy-start.3
  56.3 1.5 copy-done.3
  57.8 0.0 copy-start.5
  57.8 29.4 %all_to_all.15.rows_in = bf16[8,128,384]{2,1,0:T(8,128)(2,1)} all-to-all(bf16[8,128,384]{2,1,0:T(8,128)(2,1)S(1)} %get-tuple-element.14.attn), channel_id=1, replica_groups=mesh['z'=8,'xl'=2,'core'=2,'y'=4,'xh'=2] {'y','xh'}, dimensions={0} | all-to-all | bytes 1572864 | tf_op jit(solution)/shard_map/all_to_all | solution.py:273
  87.2 4.4 %all-gather.2.cloned.1.call-done.weight = bf16[3072,1280]{1,0:T(8,128)(2,1)} async-done(((bf16[96,1280]{1,0:T(8,128)(2,1)}), bf16[3072,1280]{1,0:T(8,128)(2,1)}) %all-gather.2.cloned.1.call-update) | async-done | bytes 7864336 | tf_op jit(solution)/shard_map/all_gather | solution.py:263
  91.6 0.0 copy-done.5
  91.6 0.0 copy-start
  91.6 3.2 %copy-done = bf16[3072,1280]{1,0:T(8,128)(2,1)S(1)} copy-done((bf16[3072,1280]{1,0:T(8,128)(2,1)S(1)}, bf16[3072,1280]{1,0:T(8,128)(2,1)}, u32[]{:S(2)}) %copy-start) | copy-done | bytes 7864344
  94.8 0.0 copy-start.2
  94.8 1.1 copy-done.2
  96.0 0.0 copy-start.1
  96.0 3.8 %shard_map.94 = (f32[128,1280]{1,0:T(8,128)S(1)}, f32[128,1280]{1,0:T(8,128)S(1)}, f32[32,24,128]{2,1,0:T(8,128)S(1)}) custom-call(bf16[8,128,384]{2,1,0:T(8,128)(2,1)S(1)} %copy-done.2, bf16[3072,1280]{1,0:T(8,128)(2,1)S(1)} %copy-done, bf16[128,1280]{1,0:T(8,128)(2,1)S(1)} %copy-done.5), custom_call_target="tpu_custom_call" | custom-call | flops 1006632960 | bytes 7864320 | tf_op jit(solution)/shard_map/pallas_call | solution.py:119
  99.8 20.5 %all_to_all.16.sums = f32[32,24,128]{2,1,0:T(8,128)S(1)} all-to-all(f32[32,24,128]{2,1,0:T(8,128)S(1)} %get-tuple-element.17), channel_id=1, replica_groups=mesh['z'=8,'xl'=2,'core'=2,'y'=4,'xh'=2] {'z','xl','core'}, dimensions={0} | all-to-all | bytes 786432 | tf_op jit(solution)/shard_map/all_to_all | solution.py:275
  120.4 0.0 copy-done.1
  120.4 0.0 copy-start.4
  120.4 4.3 %shard_map.95 = (bf16[8,128,384]{2,1,0:T(8,128)(2,1)S(1)}, bf16[128,1280]{1,0:T(8,128)(2,1)}) custom-call(f32[128,1280]{1,0:T(8,128)S(1)} %get-tuple-element.15.act, f32[128,1280]{1,0:T(8,128)S(1)} %get-tuple-element.16.slope, bf16[128,1280]{1,0:T(8,128)(2,1)S(1)} %copy-done.5, f32[32,24,128]{2,1,0:T(8,128)S(1)} %all_to_all.16.sums, ...), custom_call_target="tpu_custom_call" | custom-call | flops 1006632960 | bytes 7864320 | tf_op jit(solution)/shard_map/pallas_call | solution.py:167
  124.7 0.0 copy-start.7
  124.7 19.7 %all_to_all.17.partial = bf16[8,128,384]{2,1,0:T(8,128)(2,1)S(1)} all-to-all(bf16[8,128,384]{2,1,0:T(8,128)(2,1)S(1)} %get-tuple-element.20), channel_id=1, replica_groups=mesh['z'=8,'xl'=2,'core'=2,'y'=4,'xh'=2] {'y','xh'}, dimensions={0} | all-to-all | bytes 1572864 | tf_op jit(solution)/shard_map/all_to_all | solution.py:277
  144.4 0.0 copy-done.4
  144.4 0.0 copy-done.7
  144.4 2.7 %shard_map.96 = (f32[128,384]{1,0:T(8,128)}, bf16[768,768]{1,0:T(8,128)(2,1)S(1)}, bf16[768,768]{1,0:T(8,128)(2,1)S(1)}) custom-call(bf16[128,384]{1,0:T(8,128)(2,1)S(1)} %copy-done.7, bf16[768,768]{1,0:T(8,128)(2,1)S(1)} %constant_dynamic-update-slice_fusion.2.near_a, bf16[768,768]{1,0:T(8,128)(2,1)S(1)} %collective-permute-done.4.near_b, ...), custom_call_target="tpu_custom_call" | custom-call | flops 603979776 | bytes 8388608 | tf_op jit(solution)/shard_map/pallas_call | solution.py:220
  147.1 0.0 collective-permute-start.5
  147.1 2.8 %collective-permute-done.5 = bf16[768,768]{1,0:T(8,128)(2,1)S(1)} collective-permute-done((bf16[768,768]{1,0:T(8,128)(2,1)S(1)}, bf16[768,768]{1,0:T(8,128)(2,1)S(1)}, u32[]{:S(2)}, u32[]{:S(2)}) %collective-permute-start.5) | collective-permute-done | bytes 1179680 | tf_op jit(solution)/shard_map/ppermute | solution.py:249
  149.9 0.3 convert_add_fusion
  150.2 0.1 slice.45
  150.3 0.8 collective-permute-start.6
  151.1 14.6 %collective-permute-done.6 = bf16[384,768]{1,0:T(8,128)(2,1)S(1)} collective-permute-done((bf16[384,768]{1,0:T(8,128)(2,1)S(1)}, bf16[384,768]{1,0:T(8,128)(2,1)S(1)}, u32[]{:S(2)}, u32[]{:S(2)}) %collective-permute-start.6) | collective-permute-done | bytes 589856 | tf_op jit(solution)/shard_map/ppermute | solution.py:249
  165.7 0.1 fusion.1
  165.9 0.1 collective-permute-start.7
  166.0 2.0 %collective-permute-start.8 = (bf16[128,768]{1,0:T(8,128)(2,1)S(1)}, bf16[128,768]{1,0:T(8,128)(2,1)S(1)}, u32[]{:S(2)}, u32[]{:S(2)}) collective-permute-start(bf16[128,768]{1,0:T(8,128)(2,1)S(1)} %get-tuple-element.27), channel_id=1, source_target_pairs={{0,32},{32,64},{64,96},{96,128},{128,160},{160,192},{192,224},{224... | collective-permute-start | bytes 589832 | tf_op jit(solution)/shard_map/ppermute | solution.py:253
  168.0 4.1 %collective-permute-done.7 = bf16[128,768]{1,0:T(8,128)(2,1)S(1)} collective-permute-done((bf16[128,768]{1,0:T(8,128)(2,1)S(1)}, bf16[128,768]{1,0:T(8,128)(2,1)S(1)}, u32[]{:S(2)}, u32[]{:S(2)}) %collective-permute-start.7) | collective-permute-done | bytes 196640 | tf_op jit(solution)/shard_map/ppermute | solution.py:257
  172.1 1.3 collective-permute-done.8
  173.4 0.1 fusion
  173.5 0.8 fusion.3
  (6 shorter events, 0.1 us)
Async XLA Ops:
  7.2 84.4 %all-gather.2.cloned.1.call-start = ((), (), s32[]{:S(2)}) async-start(), calls=%async_computation.3 | async-start | bytes 8110080 | tf_op jit(solution)/shard_map/all_gather | solution.py:263
  9.7 10.1 %collective-permute-start.1 = (bf16[128,768]{1,0:T(8,128)(2,1)S(1)}, bf16[128,768]{1,0:T(8,128)(2,1)S(1)}, u32[]{:S(2)}, u32[]{:S(2)}) collective-permute-start(bf16[128,768]{1,0:T(8,128)(2,1)S(1)} %get-tuple-element.30), channel_id=1, source_target_pairs={{0,224},{32,0},{64,32},{96,64},{128,96},{160,128},{192,160},{224,1... | collective-permute-start | bytes 589832 | tf_op jit(solution)/shard_map/ppermute | solution.py:257
  15.7 7.6 %collective-permute-start = (bf16[128,768]{1,0:T(8,128)(2,1)S(1)}, bf16[128,768]{1,0:T(8,128)(2,1)S(1)}, u32[]{:S(2)}, u32[]{:S(2)}) collective-permute-start(bf16[128,768]{1,0:T(8,128)(2,1)S(1)} %get-tuple-element.30), channel_id=1, source_target_pairs={{0,32},{32,64},{64,96},{96,128},{128,160},{160,192},{192,224},{224... | collective-permute-start | bytes 589832 | tf_op jit(solution)/shard_map/ppermute | solution.py:253
  23.3 30.4 %copy-start.6 = (bf16[128,384]{1,0:T(8,128)(2,1)S(1)}, bf16[128,384]{1,0:T(8,128)(2,1)}, u32[]{:S(2)}) copy-start(bf16[128,384]{1,0:T(8,128)(2,1)} %query.3) | copy-start | bytes 294916
  23.3 30.4 %copy-start.8 = (s32[32,32]{1,0:T(8,128)S(1)}, s32[32,32]{1,0:T(8,128)}, u32[]{:S(2)}) copy-start(s32[32,32]{1,0:T(8,128)} %mask.1) | copy-start | bytes 12292
  23.3 27.4 %collective-permute-start.3 = (bf16[256,768]{1,0:T(8,128)(2,1)S(1)}, bf16[256,768]{1,0:T(8,128)(2,1)S(1)}, u32[]{:S(2)}, u32[]{:S(2)}) collective-permute-start(bf16[256,768]{1,0:T(8,128)(2,1)S(1)} %pad_maximum_fusion), channel_id=1, source_target_pairs={{0,16},{16,0},{1,17},{17,1},{2,18},{18,2},{3,19},{19,3},{4,20},{20... | collective-permute-start | bytes 1179656 | tf_op jit(solution)/shard_map/ppermute | solution.py:249
  23.9 26.7 %collective-permute-start.2 = (bf16[128,768]{1,0:T(8,128)(2,1)S(1)}, bf16[128,768]{1,0:T(8,128)(2,1)S(1)}, u32[]{:S(2)}, u32[]{:S(2)}) collective-permute-start(bf16[128,768]{1,0:T(8,128)(2,1)S(1)} %get-tuple-element.30), channel_id=1, source_target_pairs={{0,16},{16,0},{1,17},{17,1},{2,18},{18,2},{3,19},{19,3},{4,20},{20... | collective-permute-start | bytes 589832 | tf_op jit(solution)/shard_map/ppermute | solution.py:249
  50.7 2.9 %collective-permute-start.4 = (bf16[768,768]{1,0:T(8,128)(2,1)S(1)}, bf16[768,768]{1,0:T(8,128)(2,1)S(1)}, u32[]{:S(2)}, u32[]{:S(2)}) collective-permute-start(bf16[768,768]{1,0:T(8,128)(2,1)S(1)} %constant_dynamic-update-slice_fusion.2.near_a), channel_id=1, source_target_pairs={{0,8},{8,0},{1,9},{9,1},{2,10},{10,2},{3,11},{11,3},{4,12},{12,4},... | collective-permute-start | bytes 3538952 | tf_op jit(solution)/shard_map/ppermute | solution.py:249
  56.3 1.5 copy-start.3
  57.8 33.8 %copy-start.5 = (bf16[128,1280]{1,0:T(8,128)(2,1)S(1)}, bf16[128,1280]{1,0:T(8,128)(2,1)}, u32[]{:S(2)}) copy-start(bf16[128,1280]{1,0:T(8,128)(2,1)} %cot.3) | copy-start | bytes 983044
  91.6 3.2 %copy-start = (bf16[3072,1280]{1,0:T(8,128)(2,1)S(1)}, bf16[3072,1280]{1,0:T(8,128)(2,1)}, u32[]{:S(2)}) copy-start(bf16[3072,1280]{1,0:T(8,128)(2,1)} %all-gather.2.cloned.1.call-done.weight) | copy-start | bytes 23592964
  94.8 1.1 copy-start.2
  96.0 24.4 %copy-start.1 = (bf16[3072,1280]{1,0:T(8,128)(2,1)S(1)}, bf16[3072,1280]{1,0:T(8,128)(2,1)}, u32[]{:S(2)}) copy-start(bf16[3072,1280]{1,0:T(8,128)(2,1)} %all-gather.2.cloned.1.call-done.weight) | copy-start | bytes 23592964
  120.4 24.0 %copy-start.4 = (f32[3,128,1536]{2,1,0:T(8,128)S(1)}, f32[3,128,1536]{2,1,0:T(8,128)}, u32[]{:S(2)}) copy-start(f32[3,128,1536]{2,1,0:T(8,128)} %copy-done.3) | copy-start | bytes 7077892
  124.7 19.7 %copy-start.7 = (bf16[128,384]{1,0:T(8,128)(2,1)S(1)}, bf16[128,384]{1,0:T(8,128)(2,1)}, u32[]{:S(2)}) copy-start(bf16[128,384]{1,0:T(8,128)(2,1)} %query.3) | copy-start | bytes 294916
  147.1 2.8 %collective-permute-start.5 = (bf16[768,768]{1,0:T(8,128)(2,1)S(1)}, bf16[768,768]{1,0:T(8,128)(2,1)S(1)}, u32[]{:S(2)}, u32[]{:S(2)}) collective-permute-start(bf16[768,768]{1,0:T(8,128)(2,1)S(1)} %get-tuple-element.23), channel_id=1, source_target_pairs={{0,8},{8,0},{1,9},{9,1},{2,10},{10,2},{3,11},{11,3},{4,12},{12,4},... | collective-permute-start | bytes 3538952 | tf_op jit(solution)/shard_map/ppermute | solution.py:249
  150.3 15.5 %collective-permute-start.6 = (bf16[384,768]{1,0:T(8,128)(2,1)S(1)}, bf16[384,768]{1,0:T(8,128)(2,1)S(1)}, u32[]{:S(2)}, u32[]{:S(2)}) collective-permute-start(bf16[384,768]{1,0:T(8,128)(2,1)S(1)} %slice.45), channel_id=1, source_target_pairs={{0,16},{16,0},{1,17},{17,1},{2,18},{18,2},{3,19},{19,3},{4,20},{20... | collective-permute-start | bytes 1769480 | tf_op jit(solution)/shard_map/ppermute | solution.py:249
  165.9 6.2 %collective-permute-start.7 = (bf16[128,768]{1,0:T(8,128)(2,1)S(1)}, bf16[128,768]{1,0:T(8,128)(2,1)S(1)}, u32[]{:S(2)}, u32[]{:S(2)}) collective-permute-start(bf16[128,768]{1,0:T(8,128)(2,1)S(1)} %get-tuple-element.26), channel_id=1, source_target_pairs={{0,224},{32,0},{64,32},{96,64},{128,96},{160,128},{192,160},{224,1... | collective-permute-start | bytes 589832 | tf_op jit(solution)/shard_map/ppermute | solution.py:257
  166.0 7.4 %collective-permute-start.8 = (bf16[128,768]{1,0:T(8,128)(2,1)S(1)}, bf16[128,768]{1,0:T(8,128)(2,1)S(1)}, u32[]{:S(2)}, u32[]{:S(2)}) collective-permute-start(bf16[128,768]{1,0:T(8,128)(2,1)S(1)} %get-tuple-element.27), channel_id=1, source_target_pairs={{0,32},{32,64},{64,96},{96,128},{128,160},{160,192},{192,224},{224... | collective-permute-start | bytes 589832 | tf_op jit(solution)/shard_map/ppermute | solution.py:253
Sparse Core Ops, SparseCore 0:
  9.9 81.6 all-gather.1

commit v2 on v1

--- a/solution.py
+++ b/solution.py
@@ -81,107 +81,97 @@
     )(place, mask, query, near_a, near_b)
 
 
-def up_kernel(rows_in, weight, cot, act_out, slope_out, sums, total):
-    step = pl.program_id(0)
-    part = dot(rows_in[0], weight[...])
-
-    @pl.when(step == 0)
-    def _():
-        total[...] = part
-
-    @pl.when(step > 0)
-    def _():
-        total[...] += part
-
-    @pl.when(step == pl.num_programs(0) - 1)
-    def _():
-        width = total.shape[1]
-        chunks = width // 128
-        for r in range(chunks):
-            cols = slice(r * 128, (r + 1) * 128)
-            v = total[:, cols]
-            t = jnp.tanh(ROOT * (v + CUBIC * (v * v * v)))
-            act = 0.5 * v * (1.0 + t)
-            act_out[:, cols] = act
-            slope_out[:, cols] = 0.5 * (1.0 + t) + 0.5 * v * (1.0 - t * t) * (ROOT * (1.0 + 3.0 * CUBIC * (v * v)))
-            power = jnp.sum(act * act, axis=0, keepdims=True)
-            pull = jnp.sum(act * cot[:, cols].astype(jnp.float32), axis=0, keepdims=True)
-            sums[:, r : r + 1, :] = jnp.broadcast_to(power[None], (sums.shape[0], 1, 128))
-            sums[:, chunks + r : chunks + r + 1, :] = jnp.broadcast_to(pull[None], (sums.shape[0], 1, 128))
-        rest = sums.shape[1] - 2 * chunks
-        sums[:, 2 * chunks :, :] = jnp.zeros((sums.shape[0], rest, 128), jnp.float32)
+def up_kernel(rows_in, weight, cot, act_out, slope_out, sums, held, total, arrived):
+    parts, rows, depth = rows_in.shape
+    width = held.shape[1]
+    piece = weight.shape[3]
+    copies = []
+    for part in range(parts):
+        for core in range(2):
+            for xl in range(2):
+                where = part * depth + (2 * xl + core) * piece
+                copies.append(
+                    pltpu.make_async_copy(
+                        weight.at[part, core, xl], held.at[pl.ds(where, piece), :], arrived.at[part, 2 * core + xl]
+                    )
+                )
+    for copy in copies:
+        copy.start()
+    for part in range(parts):
+        for copy in copies[4 * part : 4 * part + 4]:
+            copy.wait()
+        term = dot(rows_in[part], held[part * depth : (part + 1) * depth, :])
+        if part == 0:
+            total[...] = term
+        else:
+            total[...] += term
+    chunks = width // 128
+    power, pull = [], []
+    for r in range(chunks):
+        cols = slice(r * 128, (r + 1) * 128)
+        v = total[:, cols]
+        t = jnp.tanh(ROOT * (v + CUBIC * (v * v * v)))
+        act = 0.5 * v * (1.0 + t)
+        act_out[:, cols] = act
+        slope_out[:, cols] = 0.5 * (1.0 + t) + 0.5 * v * (1.0 - t * t) * (ROOT * (1.0 + 3.0 * CUBIC * (v * v)))
+        power.append(jnp.sum(act * act, axis=0, keepdims=True))
+        pull.append(jnp.sum(act * cot[:, cols].astype(jnp.float32), axis=0, keepdims=True))
+    lines = power + pull + [jnp.zeros((sums.shape[1] - 2 * chunks, 128), jnp.float32)]
+    sums[...] = jnp.broadcast_to(jnp.concatenate(lines, axis=0).astype(jnp.bfloat16)[None], sums.shape)
 
 
 def up(rows_in, weight, cot, copies):
     parts, rows, depth = rows_in.shape
     width = weight.shape[1]
     lines = -(-2 * (width // 128) // 8) * 8
+    in_vmem = pl.BlockSpec(memory_space=VMEM)
     return pl.pallas_call(
         up_kernel,
-        grid=(parts,),
         out_shape=(
             jax.ShapeDtypeStruct((rows, width), jnp.float32),
             jax.ShapeDtypeStruct((rows, width), jnp.float32),
-            jax.ShapeDtypeStruct((copies, lines, 128), jnp.float32),
-        ),
-        in_specs=[
-            pl.BlockSpec((1, rows, depth), lambda i: (i, 0, 0)),
-            pl.BlockSpec((depth, width), lambda i: (i, 0)),
-            pl.BlockSpec((rows, width), lambda i: (0, 0)),
-        ],
-        out_specs=(
-            pl.BlockSpec((rows, width), lambda i: (0, 0)),
-            pl.BlockSpec((rows, width), lambda i: (0, 0)),
-            pl.BlockSpec((copies, lines, 128), lambda i: (0, 0, 0)),
-        ),
-        scratch_shapes=[pltpu.VMEM((rows, width), jnp.float32)],
-        compiler_params=pltpu.CompilerParams(vmem_limit_bytes=24 << 20),
+            jax.ShapeDtypeStruct((copies, lines, 128), jnp.bfloat16),
+            VMEM(weight.shape, jnp.bfloat16),
+        ),
+        in_specs=[in_vmem, pl.BlockSpec(memory_space=pltpu.HBM), in_vmem],
+        out_specs=(in_vmem,) * 4,
+        scratch_shapes=[pltpu.VMEM((rows, width), jnp.float32), pltpu.SemaphoreType.DMA((parts, 4))],
+        compiler_params=pltpu.CompilerParams(vmem_limit_bytes=40 << 20),
         cost_estimate=pl.CostEstimate(
             flops=2 * rows * width * parts * depth, bytes_accessed=weight.size * 2, transcendentals=rows * width
         ),
-    )(rows_in, weight, cot)
+    )(rows_in, weight.reshape(parts, 2, 2, depth // 4, width), cot)
 
 
 def down_kernel(act, slope, cot, sums, weight, out, scaled, grad):
-    @pl.when(pl.program_id(0) == 0)
-    def _():
-        chunks = act.shape[1] // 128
-        total = jnp.sum(sums[...], axis=0)
-        for r in range(chunks):
-            cols = slice(r * 128, (r + 1) * 128)
-            a = act[:, cols]
-            c = cot[:, cols].astype(jnp.float32)
-            inv = lax.rsqrt(total[r : r + 1, :] * (1.0 / TOKENS) + EPSILON)
-            pull = total[chunks + r : chunks + r + 1, :]
-            scaled[:, cols] = (a * inv).astype(jnp.bfloat16)
-            back = pull * -0.5 * inv * inv * inv * (2.0 / TOKENS)
-            grad[:, cols] = ((c * inv + back * a) * slope[:, cols]).astype(jnp.bfloat16)
-
-    out[0] = dot(grad[...], weight[...], NT).astype(jnp.bfloat16)
+    chunks = act.shape[1] // 128
+    total = jnp.sum(sums[...].astype(jnp.float32), axis=0)
+    for r in range(chunks):
+        cols = slice(r * 128, (r + 1) * 128)
+        a = act[:, cols]
+        c = cot[:, cols].astype(jnp.float32)
+        inv = lax.rsqrt(total[r : r + 1, :] * (1.0 / TOKENS) + EPSILON)
+        pull = total[chunks + r : chunks + r + 1, :]
+        scaled[:, cols] = (a * inv).astype(jnp.bfloat16)
+        back = pull * -0.5 * inv * inv * inv * (2.0 / TOKENS)
+        grad[:, cols] = ((c * inv + back * a) * slope[:, cols]).astype(jnp.bfloat16)
+    parts, _, depth = out.shape
+    for part in range(parts):
+        out[part] = dot(grad[...], weight[part * depth : (part + 1) * depth, :], NT).astype(jnp.bfloat16)
 
 
 def down(act, slope, cot, sums, weight, parts):
     rows, width = act.shape
     depth = weight.shape[0] // parts
-    whole = lambda i: (0, 0)
+    in_vmem = pl.BlockSpec(memory_space=VMEM)
     return pl.pallas_call(
         down_kernel,
-        grid=(parts,),
         out_shape=(
             jax.ShapeDtypeStruct((parts, rows, depth), jnp.bfloat16),
             jax.ShapeDtypeStruct((rows, width), jnp.bfloat16),
         ),
-        in_specs=[
-            pl.BlockSpec((rows, width), whole),
-            pl.BlockSpec((rows, width), whole),
-            pl.BlockSpec((rows, width), whole),
-            pl.BlockSpec(sums.shape, lambda i: (0, 0, 0)),
-            pl.BlockSpec((depth, width), lambda i: (i, 0)),
-        ],
-        out_specs=(
-            pl.BlockSpec((1, rows, depth), lambda i: (i, 0, 0)),
-            pl.BlockSpec((rows, width), whole),
-        ),
+        in_specs=[in_vmem] * 5,
+        out_specs=(in_vmem,) * 2,
         scratch_shapes=[pltpu.VMEM((rows, width), jnp.bfloat16)],
         compiler_params=pltpu.CompilerParams(vmem_limit_bytes=24 << 20),
         cost_estimate=pl.CostEstimate(
@@ -259,8 +249,12 @@
 
 def body(query, key, value, tile_mask, weight, cot):
     rows, width = query.shape
-    place = jnp.stack([lax.axis_index("z"), lax.axis_index("xl"), lax.axis_index("core")]).astype(jnp.int32)
-    full_weight = lax.all_gather(weight, SEQ, axis=0, tiled=True)
+    f32, bf16 = jnp.float32, jnp.bfloat16
+    xl = lax.axis_index("xl")
+    place = jnp.stack([lax.axis_index("z"), xl, lax.axis_index("core")]).astype(jnp.int32)
+    other = swap(weight, "xl")
+    pair = jnp.concatenate([jnp.where(xl == 0, weight, other), jnp.where(xl == 0, other, weight)], axis=0)
+    full_weight = lax.all_gather(pair, ("z", "core"), axis=0, tiled=True)
     own = jnp.concatenate([key, value], axis=1)
     from_low = up_plane(own)
     from_high = down_plane(own)
@@ -271,17 +265,15 @@
     copies = lax.axis_size(FSDP)
     attn, probs = attend(place, tile_mask, query, near_a, near_b, copies)
     full_rows = lax.all_to_all(attn, FSDP, 0, 0)
-    act, slope, sums = up(full_rows, full_weight, cot, lax.axis_size(SEQ))
+    act, slope, sums, held = up(full_rows, full_weight, cot, lax.axis_size(SEQ))
     sums = lax.all_to_all(sums, SEQ, 0, 0)
-    back, scaled = down(act, slope, cot, sums, full_weight, copies)
+    back, scaled = down(act, slope, cot, sums, held, copies)
     partial = lax.all_to_all(back, FSDP, 0, 0)
     grad_query, grad_a, grad_b = backward(query, near_a, near_b, attn, probs, partial)
-    f32 = jnp.float32
-    grad_a = grad_a.astype(f32) + swap(grad_b, "core").astype(f32)
-    side = grad_a[3 * rows :].astype(jnp.bfloat16)
-    mine = grad_a[: 3 * rows] + swap(side, "xl").astype(f32)
-    far = mine[rows:].astype(jnp.bfloat16)
-    grad_own = mine[:rows] + down_plane(far[:rows]).astype(f32) + up_plane(far[rows:]).astype(f32)
+    both = (grad_a.astype(f32) + swap(grad_b, "core").astype(f32)).reshape(2, len(NEAR) // 2, rows, 2 * width)
+    to_low, to_high = both[:, 1].astype(bf16), both[:, 2].astype(bf16)
+    here = both[:, 0] + down_plane(to_low).astype(f32) + up_plane(to_high).astype(f32)
+    grad_own = here[0] + swap(here[1].astype(bf16), "xl").astype(f32)
     return scaled, grad_query, grad_own[:, :width], grad_own[:, width:]
 
 

time: 181 us -> 151 us (0.83)
  waiting for transfers between devices: 63.5 us -> 46.5 us
  blocking collectives: 69.6 us -> 56.8 us
  local copies, waits for them, and re-layouts: 8.62 us -> 3.64 us
  starting transfers between devices: 11.1 us -> 14.2 us
    ppermute x5 -> x6, waiting for transfers between devices: 45.4 us -> 26.3 us  [swap(): return lax.ppermute(value, axis, [(0, 1), (1, 0)])]
    all_to_all x1, blocking collectives: 29.4 us -> 20.7 us  [body(): full_rows = lax.all_to_all(attn, FSDP, 0, 0)]
    ppermute x2, waiting for transfers between devices: 8.25 us -> 12.4 us  [down_plane(): lax.ppermute(value, 'z', [(i, (i - 1) % PLANES) for i in range(PLANES)])]
    all_to_all x1, blocking collectives: 20.5 us -> 16.4 us  [body(): sums = lax.all_to_all(sums, SEQ, 0, 0)]
    unnamed x22, local copies, waits for them, and re-layouts: 6.81 us -> 2.7 us
    ppermute x5 -> x6, starting transfers between devices: 3.05 us -> 6.09 us  [swap(): return lax.ppermute(value, axis, [(0, 1), (1, 0)])]
  transfers between devices with their start and end apart: 10 -> 11, of which waited for: 9 -> 10; matrix products, arithmetic and copies ran while one was open for 1% -> 0% of each run, Pallas kernels for 1% -> 2%
where the time goes in v2:
time: 151 us; the launch traced here: 150 us
  blocking collectives  56.8 us (38%)
  waiting for transfers between devices  46.5 us (31%)
  starting transfers between devices  14.2 us (9%)
  between operations  14.2 us (9%)
  Pallas kernels  12.6 us (8%)
  local copies, waits for them, and re-layouts  3.64 us (2%)
  other arithmetic  2.31 us (2%)
    ppermute x6, waiting for transfers between devices, swap(): return lax.ppermute(value, axis, [(0, 1), (1, 0)])  26.3 us
    all_to_all x1, blocking collectives, body(): full_rows = lax.all_to_all(attn, FSDP, 0, 0)  20.7 us
    all_to_all x1, blocking collectives, body(): partial = lax.all_to_all(back, FSDP, 0, 0)  19.6 us
    all_to_all x1, blocking collectives, body(): sums = lax.all_to_all(sums, SEQ, 0, 0)  16.4 us
    ppermute x2, waiting for transfers between devices, down_plane(): lax.ppermute(value, 'z', [(i, (i - 1) % PLANES) for i in range(PLANES)])  12.4 us
    ppermute x2, starting transfers between devices, down_plane(): lax.ppermute(value, 'z', [(i, (i - 1) % PLANES) for i in range(PLANES)])  6.37 us
    ppermute x6, starting transfers between devices, swap(): return lax.ppermute(value, axis, [(0, 1), (1, 0)])  6.09 us
    ppermute x2, waiting for transfers between devices, up_plane(): lax.ppermute(value, 'z', [(i, (i + 1) % PLANES) for i in range(PLANES)])  4.89 us
  transfers between devices with their start and end apart: 11, of which 10 were waited for; matrix products, arithmetic and copies ran while one was open for 0% of the time, Pallas kernels for 2%

profile of v2, /device:TPU:2, one launch (start us, length us, event | category | flops | bytes accessed | tf_op | source)
XLA Modules:
  0.0 150.2 jit_solution(2776047685140208142)
XLA Ops:
  7.2 0.0 all-gather.2.cloned.1.call-start
  7.2 2.4 %collective-permute-start.5 = (bf16[96,1280]{1,0:T(8,128)(2,1)}, bf16[96,1280]{1,0:T(8,128)(2,1)S(1)}, u32[]{:S(2)}, u32[]{:S(2)}) collective-permute-start(bf16[96,1280]{1,0:T(8,128)(2,1)} %param.10), channel_id=1, source_target_pairs={{0,16},{16,0},{1,17},{17,1},{2,18},{18,2},{3,19},{19,3},{4,20},{20... | collective-permute-start | bytes 737288 | tf_op jit(solution)/shard_map/ppermute | solution.py:239
  9.6 0.0 copy-start.7
  9.6 0.0 copy-start.8
  9.6 5.6 %collective-permute-done.5 = bf16[96,1280]{1,0:T(8,128)(2,1)S(1)} collective-permute-done((bf16[96,1280]{1,0:T(8,128)(2,1)}, bf16[96,1280]{1,0:T(8,128)(2,1)S(1)}, u32[]{:S(2)}, u32[]{:S(2)}) %collective-permute-start.5) | collective-permute-done | bytes 245792 | tf_op jit(solution)/shard_map/ppermute | solution.py:239
  15.2 1.0 broadcast_select_fusion.1
  16.2 0.8 pad_maximum_fusion
  17.0 0.0 all-gather.2.cloned.1.call-update
  17.0 0.0 copy-done.7
  17.1 0.0 copy-done.8
  17.1 5.9 %collective-permute-start.1 = (bf16[128,768]{1,0:T(8,128)(2,1)S(1)}, bf16[128,768]{1,0:T(8,128)(2,1)S(1)}, u32[]{:S(2)}, u32[]{:S(2)}) collective-permute-start(bf16[128,768]{1,0:T(8,128)(2,1)S(1)} %get-tuple-element.32), channel_id=1, source_target_pairs={{0,224},{32,0},{64,32},{96,64},{128,96},{160,128},{192,160},{224,1... | collective-permute-start | bytes 589832 | tf_op jit(solution)/shard_map/ppermute | solution.py:247
  23.0 0.0 collective-permute-start
  23.0 3.3 %collective-permute-done.1 = bf16[128,768]{1,0:T(8,128)(2,1)S(1)} collective-permute-done((bf16[128,768]{1,0:T(8,128)(2,1)S(1)}, bf16[128,768]{1,0:T(8,128)(2,1)S(1)}, u32[]{:S(2)}, u32[]{:S(2)}) %collective-permute-start.1) | collective-permute-done | bytes 196640 | tf_op jit(solution)/shard_map/ppermute | solution.py:247
  26.3 3.6 %collective-permute-done = bf16[128,768]{1,0:T(8,128)(2,1)S(1)} collective-permute-done((bf16[128,768]{1,0:T(8,128)(2,1)S(1)}, bf16[128,768]{1,0:T(8,128)(2,1)S(1)}, u32[]{:S(2)}, u32[]{:S(2)}) %collective-permute-start) | collective-permute-done | bytes 196640 | tf_op jit(solution)/shard_map/ppermute | solution.py:243
  30.0 0.0 copy-start.4
  30.0 0.0 copy-start.6
  30.0 0.6 collective-permute-start.3
  30.6 1.5 collective-permute-start.2
  32.1 10.7 %collective-permute-done.2 = bf16[128,768]{1,0:T(8,128)(2,1)S(1)} collective-permute-done((bf16[128,768]{1,0:T(8,128)(2,1)S(1)}, bf16[128,768]{1,0:T(8,128)(2,1)S(1)}, u32[]{:S(2)}, u32[]{:S(2)}) %collective-permute-start.2) | collective-permute-done | bytes 196640 | tf_op jit(solution)/shard_map/ppermute | solution.py:239
  42.8 0.0 collective-permute-done.3
  42.9 0.1 collective-permute-start.4
  43.0 0.1 pad_add_fusion.place
  43.1 2.8 %collective-permute-done.4.near_b = bf16[768,768]{1,0:T(8,128)(2,1)S(1)} collective-permute-done((bf16[768,768]{1,0:T(8,128)(2,1)S(1)}, bf16[768,768]{1,0:T(8,128)(2,1)S(1)}, u32[]{:S(2)}, u32[]{:S(2)}) %collective-permute-start.4) | collective-permute-done | bytes 1179680 | tf_op jit(solution)/shard_map/ppermute | solution.py:239
  45.8 0.0 copy-done.4
  45.8 0.0 copy-done.6
  45.8 2.6 %shard_map.93 = (bf16[8,128,384]{2,1,0:T(8,128)(2,1)S(1)}, f32[3,128,1536]{2,1,0:T(8,128)S(1)}) custom-call(s32[3]{0:T(128)S(1)} %pad_add_fusion.place, s32[32,32]{1,0:T(8,128)S(1)} %copy-done.6, bf16[128,384]{1,0:T(8,128)(2,1)S(1)} %copy-done.4, bf16[768,768]{1,0:T(8,128)(2,1)S(1)} %constant_dynamic-update-slice_fusion.2.near_a, ...), custom_call_target="tpu_custom_call" | custom-call | flops 301989888 | bytes 8388608 | tf_op jit(solution)/shard_map/pallas_call | solution.py:71
  48.5 0.0 copy-start.1
  48.5 1.5 copy-done.1
  50.0 0.0 copy-start.3
  50.0 20.7 %all_to_all.15.rows_in = bf16[8,128,384]{2,1,0:T(8,128)(2,1)} all-to-all(bf16[8,128,384]{2,1,0:T(8,128)(2,1)S(1)} %get-tuple-element.15.attn), channel_id=1, replica_groups=mesh['z'=8,'xl'=2,'core'=2,'y'=4,'xh'=2] {'y','xh'}, dimensions={0} | all-to-all | bytes 1572864 | tf_op jit(solution)/shard_map/all_to_all | solution.py:267
  70.7 2.9 %all-gather.2.cloned.1.call-done = bf16[3072,1280]{1,0:T(8,128)(2,1)} async-done(((bf16[192,1280]{1,0:T(8,128)(2,1)}), bf16[3072,1280]{1,0:T(8,128)(2,1)}) %all-gather.2.cloned.1.call-update) | async-done | bytes 7864336 | tf_op jit(solution)/shard_map/all_gather | solution.py:257
  73.6 0.0 copy-done.3
  73.6 0.0 copy-start
  73.6 1.1 copy-done
  74.7 4.4 %shard_map.94 = (f32[128,1280]{1,0:T(8,128)S(1)}, f32[128,1280]{1,0:T(8,128)S(1)}, bf16[32,24,128]{2,1,0:T(8,128)(2,1)S(1)}, bf16[3072,1280]{1,0:T(8,128)(2,1)S(1)}) custom-call(bf16[8,128,384]{2,1,0:T(8,128)(2,1)S(1)} %copy-done, bf16[8,2,2,96,1280]{4,3,2,1,0:T(8,128)(2,1)} %bitcast.21, bf16[128,1280]{1,0:T(8,128)(2,1)S(1)} %copy-done.3), custom_call_target="tpu_custom_call" | custom-call | flops 1006632960 | bytes 7864320 | tf_op jit(solution)/shard_map/pallas_call | solution.py:128
  79.1 16.4 %all_to_all.16.sums = bf16[32,24,128]{2,1,0:T(8,128)(2,1)S(1)} all-to-all(bf16[32,24,128]{2,1,0:T(8,128)(2,1)S(1)} %get-tuple-element.18), channel_id=1, replica_groups=mesh['z'=8,'xl'=2,'core'=2,'y'=4,'xh'=2] {'z','xl','core'}, dimensions={0} | all-to-all | bytes 393216 | tf_op jit(solution)/shard_map/all_to_all | solution.py:269
  95.5 0.0 copy-start.2
  95.5 3.0 %shard_map.95 = (bf16[8,128,384]{2,1,0:T(8,128)(2,1)S(1)}, bf16[128,1280]{1,0:T(8,128)(2,1)}) custom-call(f32[128,1280]{1,0:T(8,128)S(1)} %get-tuple-element.16.act, f32[128,1280]{1,0:T(8,128)S(1)} %get-tuple-element.17.slope, bf16[128,1280]{1,0:T(8,128)(2,1)S(1)} %copy-done.3, bf16[32,24,128]{2,1,0:T(8,128)(2,1)S(1)} %all_to_all.16.sums, ...), custom_call_target="tpu_custom_call" | custom-call | flops 1006632960 | bytes 7864320 | tf_op jit(solution)/shard_map/pallas_call | solution.py:167
  98.4 0.0 copy-start.5
  98.4 19.6 %all_to_all.17.partial = bf16[8,128,384]{2,1,0:T(8,128)(2,1)S(1)} all-to-all(bf16[8,128,384]{2,1,0:T(8,128)(2,1)S(1)} %get-tuple-element.22), channel_id=1, replica_groups=mesh['z'=8,'xl'=2,'core'=2,'y'=4,'xh'=2] {'y','xh'}, dimensions={0} | all-to-all | bytes 1572864 | tf_op jit(solution)/shard_map/all_to_all | solution.py:271
  118.1 0.0 copy-done.2
  118.1 0.0 copy-done.5
  118.1 2.7 %shard_map.96 = (f32[128,384]{1,0:T(8,128)}, bf16[768,768]{1,0:T(8,128)(2,1)S(1)}, bf16[768,768]{1,0:T(8,128)(2,1)S(1)}) custom-call(bf16[128,384]{1,0:T(8,128)(2,1)S(1)} %copy-done.5, bf16[768,768]{1,0:T(8,128)(2,1)S(1)} %constant_dynamic-update-slice_fusion.2.near_a, bf16[768,768]{1,0:T(8,128)(2,1)S(1)} %collective-permute-done.4.near_b, ...), custom_call_target="tpu_custom_call" | custom-call | flops 603979776 | bytes 8388608 | tf_op jit(solution)/shard_map/pallas_call | solution.py:210
  120.7 0.0 collective-permute-start.6
  120.7 2.8 %collective-permute-done.6 = bf16[768,768]{1,0:T(8,128)(2,1)S(1)} collective-permute-done((bf16[768,768]{1,0:T(8,128)(2,1)S(1)}, bf16[768,768]{1,0:T(8,128)(2,1)S(1)}, u32[]{:S(2)}, u32[]{:S(2)}) %collective-permute-start.6) | collective-permute-done | bytes 1179680 | tf_op jit(solution)/shard_map/ppermute | solution.py:239
  123.6 0.2 convert_add_fusion
  123.8 0.1 slice_bitcast_fusion.3
  123.9 0.4 collective-permute-start.7
  124.4 1.7 %collective-permute-start.8 = (bf16[2,128,768]{2,1,0:T(8,128)(2,1)S(1)}, bf16[2,128,768]{2,1,0:T(8,128)(2,1)S(1)}, u32[]{:S(2)}, u32[]{:S(2)}) collective-permute-start(bf16[2,128,768]{2,1,0:T(8,128)(2,1)S(1)} %get-tuple-element.27), channel_id=1, source_target_pairs={{0,32},{32,64},{64,96},{96,128},{128,160},{160,192},{192,224},{224... | collective-permute-start | bytes 1179656 | tf_op jit(solution)/shard_map/ppermute | solution.py:243
  126.0 9.1 %collective-permute-done.7 = bf16[2,128,768]{2,1,0:T(8,128)(2,1)S(1)} collective-permute-done((bf16[2,128,768]{2,1,0:T(8,128)(2,1)S(1)}, bf16[2,128,768]{2,1,0:T(8,128)(2,1)S(1)}, u32[]{:S(2)}, u32[]{:S(2)}) %collective-permute-start.7) | collective-permute-done | bytes 393248 | tf_op jit(solution)/shard_map/ppermute | solution.py:247
  135.1 1.3 collective-permute-done.8
  136.4 0.1 fusion.1
  136.6 1.5 %collective-permute-start.9 = (bf16[128,768]{1,0:T(8,128)(2,1)S(1)}, bf16[128,768]{1,0:T(8,128)(2,1)S(1)}, u32[]{:S(2)}, u32[]{:S(2)}) collective-permute-start(bf16[128,768]{1,0:T(8,128)(2,1)S(1)} %fusion.3), channel_id=1, source_target_pairs={{0,16},{16,0},{1,17},{17,1},{2,18},{18,2},{3,19},{19,3},{4,20},{20... | collective-permute-start | bytes 589832 | tf_op jit(solution)/shard_map/ppermute | solution.py:239
  138.1 4.4 %collective-permute-done.9 = bf16[128,768]{1,0:T(8,128)(2,1)S(1)} collective-permute-done((bf16[128,768]{1,0:T(8,128)(2,1)S(1)}, bf16[128,768]{1,0:T(8,128)(2,1)S(1)}, u32[]{:S(2)}, u32[]{:S(2)}) %collective-permute-start.9) | collective-permute-done | bytes 196640 | tf_op jit(solution)/shard_map/ppermute | solution.py:239
  142.5 0.8 fusion.4
  (9 shorter events, 0.2 us)
Async XLA Ops:
  7.2 66.4 %all-gather.2.cloned.1.call-start = ((), (), s32[]{:S(2)}) async-start(), calls=%async_computation.3 | async-start | bytes 8355840 | tf_op jit(solution)/shard_map/all_gather | solution.py:257
  7.2 8.0 %collective-permute-start.5 = (bf16[96,1280]{1,0:T(8,128)(2,1)}, bf16[96,1280]{1,0:T(8,128)(2,1)S(1)}, u32[]{:S(2)}, u32[]{:S(2)}) collective-permute-start(bf16[96,1280]{1,0:T(8,128)(2,1)} %param.10), channel_id=1, source_target_pairs={{0,16},{16,0},{1,17},{17,1},{2,18},{18,2},{3,19},{19,3},{4,20},{20... | collective-permute-start | bytes 737288 | tf_op jit(solution)/shard_map/ppermute | solution.py:239
  9.6 7.5 %copy-start.7 = (bf16[128,384]{1,0:T(8,128)(2,1)S(1)}, bf16[128,384]{1,0:T(8,128)(2,1)}, u32[]{:S(2)}) copy-start(bf16[128,384]{1,0:T(8,128)(2,1)} %param.7) | copy-start | bytes 294916
  9.6 7.5 %copy-start.8 = (bf16[128,384]{1,0:T(8,128)(2,1)S(1)}, bf16[128,384]{1,0:T(8,128)(2,1)}, u32[]{:S(2)}) copy-start(bf16[128,384]{1,0:T(8,128)(2,1)} %param.8) | copy-start | bytes 294916
  17.1 9.2 %collective-permute-start.1 = (bf16[128,768]{1,0:T(8,128)(2,1)S(1)}, bf16[128,768]{1,0:T(8,128)(2,1)S(1)}, u32[]{:S(2)}, u32[]{:S(2)}) collective-permute-start(bf16[128,768]{1,0:T(8,128)(2,1)S(1)} %get-tuple-element.32), channel_id=1, source_target_pairs={{0,224},{32,0},{64,32},{96,64},{128,96},{160,128},{192,160},{224,1... | collective-permute-start | bytes 589832 | tf_op jit(solution)/shard_map/ppermute | solution.py:247
  23.0 6.9 %collective-permute-start = (bf16[128,768]{1,0:T(8,128)(2,1)S(1)}, bf16[128,768]{1,0:T(8,128)(2,1)S(1)}, u32[]{:S(2)}, u32[]{:S(2)}) collective-permute-start(bf16[128,768]{1,0:T(8,128)(2,1)S(1)} %get-tuple-element.32), channel_id=1, source_target_pairs={{0,32},{32,64},{64,96},{96,128},{128,160},{160,192},{192,224},{224... | collective-permute-start | bytes 589832 | tf_op jit(solution)/shard_map/ppermute | solution.py:243
  30.0 15.9 %copy-start.4 = (bf16[128,384]{1,0:T(8,128)(2,1)S(1)}, bf16[128,384]{1,0:T(8,128)(2,1)}, u32[]{:S(2)}) copy-start(bf16[128,384]{1,0:T(8,128)(2,1)} %query.3) | copy-start | bytes 294916
  30.0 15.9 %copy-start.6 = (s32[32,32]{1,0:T(8,128)S(1)}, s32[32,32]{1,0:T(8,128)}, u32[]{:S(2)}) copy-start(s32[32,32]{1,0:T(8,128)} %mask.1) | copy-start | bytes 12292
  30.0 12.9 %collective-permute-start.3 = (bf16[256,768]{1,0:T(8,128)(2,1)S(1)}, bf16[256,768]{1,0:T(8,128)(2,1)S(1)}, u32[]{:S(2)}, u32[]{:S(2)}) collective-permute-start(bf16[256,768]{1,0:T(8,128)(2,1)S(1)} %pad_maximum_fusion.1), channel_id=1, source_target_pairs={{0,16},{16,0},{1,17},{17,1},{2,18},{18,2},{3,19},{19,3},{4,20},{20... | collective-permute-start | bytes 1179656 | tf_op jit(solution)/shard_map/ppermute | solution.py:239
  30.6 12.2 %collective-permute-start.2 = (bf16[128,768]{1,0:T(8,128)(2,1)S(1)}, bf16[128,768]{1,0:T(8,128)(2,1)S(1)}, u32[]{:S(2)}, u32[]{:S(2)}) collective-permute-start(bf16[128,768]{1,0:T(8,128)(2,1)S(1)} %get-tuple-element.32), channel_id=1, source_target_pairs={{0,16},{16,0},{1,17},{17,1},{2,18},{18,2},{3,19},{19,3},{4,20},{20... | collective-permute-start | bytes 589832 | tf_op jit(solution)/shard_map/ppermute | solution.py:239
  42.9 2.9 %collective-permute-start.4 = (bf16[768,768]{1,0:T(8,128)(2,1)S(1)}, bf16[768,768]{1,0:T(8,128)(2,1)S(1)}, u32[]{:S(2)}, u32[]{:S(2)}) collective-permute-start(bf16[768,768]{1,0:T(8,128)(2,1)S(1)} %constant_dynamic-update-slice_fusion.2.near_a), channel_id=1, source_target_pairs={{0,8},{8,0},{1,9},{9,1},{2,10},{10,2},{3,11},{11,3},{4,12},{12,4},... | collective-permute-start | bytes 3538952 | tf_op jit(solution)/shard_map/ppermute | solution.py:239
  48.5 1.5 copy-start.1
  50.0 23.6 %copy-start.3 = (bf16[128,1280]{1,0:T(8,128)(2,1)S(1)}, bf16[128,1280]{1,0:T(8,128)(2,1)}, u32[]{:S(2)}) copy-start(bf16[128,1280]{1,0:T(8,128)(2,1)} %cot.3) | copy-start | bytes 983044
  73.6 1.1 copy-start
  95.5 22.6 %copy-start.2 = (f32[3,128,1536]{2,1,0:T(8,128)S(1)}, f32[3,128,1536]{2,1,0:T(8,128)}, u32[]{:S(2)}) copy-start(f32[3,128,1536]{2,1,0:T(8,128)} %copy-done.1) | copy-start | bytes 7077892
  98.4 19.6 %copy-start.5 = (bf16[128,384]{1,0:T(8,128)(2,1)S(1)}, bf16[128,384]{1,0:T(8,128)(2,1)}, u32[]{:S(2)}) copy-start(bf16[128,384]{1,0:T(8,128)(2,1)} %query.3) | copy-start | bytes 294916
  120.7 2.8 %collective-permute-start.6 = (bf16[768,768]{1,0:T(8,128)(2,1)S(1)}, bf16[768,768]{1,0:T(8,128)(2,1)S(1)}, u32[]{:S(2)}, u32[]{:S(2)}) collective-permute-start(bf16[768,768]{1,0:T(8,128)(2,1)S(1)} %get-tuple-element.25), channel_id=1, source_target_pairs={{0,8},{8,0},{1,9},{9,1},{2,10},{10,2},{3,11},{11,3},{4,12},{12,4},... | collective-permute-start | bytes 3538952 | tf_op jit(solution)/shard_map/ppermute | solution.py:239
  123.9 11.2 %collective-permute-start.7 = (bf16[2,128,768]{2,1,0:T(8,128)(2,1)S(1)}, bf16[2,128,768]{2,1,0:T(8,128)(2,1)S(1)}, u32[]{:S(2)}, u32[]{:S(2)}) collective-permute-start(bf16[2,128,768]{2,1,0:T(8,128)(2,1)S(1)} %get-tuple-element.26), channel_id=1, source_target_pairs={{0,224},{32,0},{64,32},{96,64},{128,96},{160,128},{192,160},{224,1... | collective-permute-start | bytes 1179656 | tf_op jit(solution)/shard_map/ppermute | solution.py:247
  124.4 12.1 %collective-permute-start.8 = (bf16[2,128,768]{2,1,0:T(8,128)(2,1)S(1)}, bf16[2,128,768]{2,1,0:T(8,128)(2,1)S(1)}, u32[]{:S(2)}, u32[]{:S(2)}) collective-permute-start(bf16[2,128,768]{2,1,0:T(8,128)(2,1)S(1)} %get-tuple-element.27), channel_id=1, source_target_pairs={{0,32},{32,64},{64,96},{96,128},{128,160},{160,192},{192,224},{224... | collective-permute-start | bytes 1179656 | tf_op jit(solution)/shard_map/ppermute | solution.py:243
  136.6 5.9 %collective-permute-start.9 = (bf16[128,768]{1,0:T(8,128)(2,1)S(1)}, bf16[128,768]{1,0:T(8,128)(2,1)S(1)}, u32[]{:S(2)}, u32[]{:S(2)}) collective-permute-start(bf16[128,768]{1,0:T(8,128)(2,1)S(1)} %fusion.3), channel_id=1, source_target_pairs={{0,16},{16,0},{1,17},{17,1},{2,18},{18,2},{3,19},{19,3},{4,20},{20... | collective-permute-start | bytes 589832 | tf_op jit(solution)/shard_map/ppermute | solution.py:239
Sparse Core Ops, SparseCore 0:
  17.1 56.3 all-gather.1

commit v3 on v2

v3 whole, which is shorter than its diff:
```python
import functools

import jax
import jax.numpy as jnp
from jax import lax
from jax.experimental import pallas as pl
from jax.experimental.pallas import tpu as pltpu
from jax.sharding import Mesh, PartitionSpec as P

HD = 128
TILE = 128
TOKENS = 4096
EPSILON = 1e-05
MASKED = -1e30
ROOT = 0.7978845608028654
CUBIC = 0.044715
PLANES = 8
NEAR = ((0, 0), (1, 0), (0, -1), (1, -1), (0, 1), (1, 1))
SEQ = ("z", "xl", "core")
FSDP = ("y", "xh")
WIDE = ("xl", "y", "xh")
NT = (((1,), (1,)), ((), ()))
TN = (((0,), (0,)), ((), ()))
VMEM = pltpu.VMEM
SMEM = pltpu.SMEM


def dot(a, b, dims=(((1,), (0,)), ((), ()))):
    return lax.dot_general(a, b, dims, preferred_element_type=jnp.float32)


def attend_kernel(place, mask, query, near_a, near_b, out, plain, probs):
    z, xl, core = place[0], place[1], place[2]
    me = 4 * z + 2 * xl + core

    def bias_row(other_core):
        parts = []
        for dx, dz in NEAR:
            plane = z + dz
            inside = (plane >= 0) & (plane < PLANES)
            tile = 4 * jnp.clip(plane, 0, PLANES - 1) + 2 * (xl if dx == 0 else 1 - xl) + (1 - core if other_core else core)
            value = jnp.where(inside & (mask[me, tile] > 0), 0.0, MASKED).astype(jnp.float32)
            parts.append(jnp.full((1, TILE), value, jnp.float32))
        return jnp.concatenate(parts, axis=1)

    bias_a, bias_b = bias_row(False), bias_row(True)
    width = near_a.shape[1] // 2
    half = near_a.shape[0]
    scale = HD ** (-0.5)
    for head in range(width // HD):
        cols = slice(head * HD, (head + 1) * HD)
        vcols = slice(width + head * HD, width + (head + 1) * HD)
        q = query[:, cols]
        s_a = dot(q, near_a[:, cols], NT) * scale + bias_a
        s_b = dot(q, near_b[:, cols], NT) * scale + bias_b
        top = jnp.maximum(jnp.max(s_a, axis=1, keepdims=True), jnp.max(s_b, axis=1, keepdims=True))
        e_a = jnp.exp(s_a - top)
        e_b = jnp.exp(s_b - top)
        inv = 1.0 / (jnp.sum(e_a, axis=1, keepdims=True) + jnp.sum(e_b, axis=1, keepdims=True))
        p_a = e_a * inv
        p_b = e_b * inv
        probs[head, :, :half] = p_a
        probs[head, :, half:] = p_b
        mixed = dot(p_a.astype(jnp.bfloat16), near_a[:, vcols]) + dot(p_b.astype(jnp.bfloat16), near_b[:, vcols])
        mixed = mixed.astype(jnp.bfloat16)
        plain[:, cols] = mixed
        turned = mixed.astype(jnp.float32).T.astype(jnp.bfloat16)
        _, copies, lines, tokens = out.shape
        start = head * HD
        while start < (head + 1) * HD:
            side, low = divmod(start, lines)
            stop = min((head + 1) * HD, (side + 1) * lines)
            piece = turned[start - head * HD : stop - head * HD]
            out[side, :, low : low + stop - start, :] = jnp.broadcast_to(piece[None], (copies,) + piece.shape)
            start = stop


def attend(place, mask, query, near_a, near_b, copies):
    rows, width = query.shape
    heads = width // HD
    keys = 2 * near_a.shape[0]
    return pl.pallas_call(
        attend_kernel,
        out_shape=(
            jax.ShapeDtypeStruct((2, copies, width // 2, rows), jnp.bfloat16),
            jax.ShapeDtypeStruct((rows, width), jnp.bfloat16),
            jax.ShapeDtypeStruct((heads, rows, keys), jnp.float32),
        ),
        in_specs=[pl.BlockSpec(memory_space=SMEM)] * 2 + [pl.BlockSpec(memory_space=VMEM)] * 3,
        out_specs=(pl.BlockSpec(memory_space=VMEM),) * 3,
        compiler_params=pltpu.CompilerParams(vmem_limit_bytes=24 << 20),
        cost_estimate=pl.CostEstimate(flops=4 * rows * keys * width, bytes_accessed=8 << 20, transcendentals=heads * rows * keys),
    )(place, mask, query, near_a, near_b)


def up_kernel(place, rows_in, weight, cot, mine, theirs, held, cot_out, total, arrived):
    parts, depth, _ = weight.shape
    rows = rows_in.shape[2]
    own = place[1]
    copies = [pltpu.make_async_copy(weight.at[part], held.at[part], arrived.at[part]) for part in range(parts)]
    copies.append(pltpu.make_async_copy(cot, cot_out, arrived.at[parts]))
    for copy in copies:
        copy.start()
    group = 4
    for first in range(0, parts, group):
        for copy in copies[first : first + group]:
            copy.wait()
        near = rows_in[pl.ds(own * parts + first, group)].reshape(group * depth, rows)
        far = rows_in[pl.ds((1 - own) * parts + first, group)].reshape(group * depth, rows)
        held_rows = held[first : first + group].reshape(group * depth, held.shape[2])
        term = dot(jnp.concatenate([near, far], axis=1), held_rows, TN)
        if first == 0:
            total[...] = term
        elif first + group < parts:
            total[...] += term
        else:
            term = total[...] + term
            mine[...] = term[:rows]
            theirs[...] = term[rows:].astype(jnp.bfloat16)
    copies[parts].wait()


def up(place, rows_in, weight, cot):
    sides, depth, rows = rows_in.shape
    parts = sides // 2
    width = weight.shape[1]
    in_vmem = pl.BlockSpec(memory_space=VMEM)
    in_hbm = pl.BlockSpec(memory_space=pltpu.HBM)
    return pl.pallas_call(
        up_kernel,
        out_shape=(
            jax.ShapeDtypeStruct((rows, width), jnp.float32),
            jax.ShapeDtypeStruct((rows, width), jnp.bfloat16),
            VMEM((parts, depth, width), jnp.bfloat16),
            VMEM(cot.shape, jnp.bfloat16),
        ),
        in_specs=[pl.BlockSpec(memory_space=SMEM), in_vmem, in_hbm, in_hbm],
        out_specs=(in_vmem,) * 4,
        scratch_shapes=[pltpu.VMEM((2 * rows, width), jnp.float32), pltpu.SemaphoreType.DMA((parts + 1,))],
        compiler_params=pltpu.CompilerParams(vmem_limit_bytes=46 << 20),
        cost_estimate=pl.CostEstimate(
            flops=4 * rows * width * parts * depth, bytes_accessed=weight.size * 2, transcendentals=0
        ),
    )(place, rows_in, weight.reshape(parts, depth, width), cot)


def middle_kernel(mine, got, cot, act_out, pull_out, push_out, pair, sums):
    chunks = mine.shape[1] // 128
    power, pull = [], []
    for r in range(chunks):
        cols = slice(r * 128, (r + 1) * 128)
        v = mine[:, cols] + got[:, cols].astype(jnp.float32)
        t = jnp.tanh(ROOT * (v + CUBIC * (v * v * v)))
        act = 0.5 * v * (1.0 + t)
        slope = 0.5 * (1.0 + t) + 0.5 * v * (1.0 - t * t) * (ROOT * (1.0 + 3.0 * CUBIC * (v * v)))
        c = cot[:, cols].astype(jnp.float32)
        act_out[:, cols] = act
        pull_out[:, cols] = c * slope
        push_out[:, cols] = act * slope
        pair[0, :, cols] = (c * slope).astype(jnp.bfloat16)
        pair[1, :, cols] = (act * slope).astype(jnp.bfloat16)
        power.append(jnp.sum(act * act, axis=0, keepdims=True))
        pull.append(jnp.sum(act * c, axis=0, keepdims=True))
    lines = power + pull + [jnp.zeros((sums.shape[1] - 2 * chunks, 128), jnp.float32)]
    sums[...] = jnp.broadcast_to(jnp.concatenate(lines, axis=0).astype(jnp.bfloat16)[None], sums.shape)


def middle(mine, got, cot, copies):
    rows, width = mine.shape
    lines = -(-2 * (width // 128) // 8) * 8
    in_vmem = pl.BlockSpec(memory_space=VMEM)
    wide = jax.ShapeDtypeStruct((rows, width), jnp.float32)
    return pl.pallas_call(
        middle_kernel,
        out_shape=(
            wide,
            wide,
            wide,
            jax.ShapeDtypeStruct((2, rows, width), jnp.bfloat16),
            jax.ShapeDtypeStruct((copies, lines, 128), jnp.bfloat16),
        ),
        in_specs=[in_vmem] * 3,
        out_specs=(in_vmem,) * 5,
        compiler_params=pltpu.CompilerParams(vmem_limit_bytes=24 << 20),
        cost_estimate=pl.CostEstimate(flops=40 * rows * width, bytes_accessed=4 << 20, transcendentals=rows * width),
    )(mine, got, cot)


def down_kernel(place, act, pull, push, pair, sums, weight, out, scaled, grad):
    rows, width = act.shape
    chunks = width // 128
    own = place[1]
    total = jnp.sum(sums[...].astype(jnp.float32), axis=0)
    for r in range(chunks):
        cols = slice(r * 128, (r + 1) * 128)
        inv = lax.rsqrt(total[r : r + 1, :] * (1.0 / TOKENS) + EPSILON)
        back = total[chunks + r : chunks + r + 1, :] * -0.5 * inv * inv * inv * (2.0 / TOKENS)
        scaled[:, cols] = (act[:, cols] * inv).astype(jnp.bfloat16)
        grad[:rows, cols] = (pull[:, cols] * inv + back * push[:, cols]).astype(jnp.bfloat16)
        far = pair[0, :, cols].astype(jnp.float32) * inv + back * pair[1, :, cols].astype(jnp.float32)
        grad[rows:, cols] = far.astype(jnp.bfloat16)
    parts, depth, _ = weight.shape
    group = 4
    for first in range(0, parts, group):
        term = dot(weight[first : first + group].reshape(group * depth, width), grad[...], NT).astype(jnp.bfloat16)
        out[pl.ds(own * parts + first, group)] = term[:, :rows].reshape(group, depth, rows)
        out[pl.ds((1 - own) * parts + first, group)] = term[:, rows:].reshape(group, depth, rows)


def down(place, act, pull, push, pair, sums, weight):
    rows, width = act.shape
    parts, depth, _ = weight.shape
    in_vmem = pl.BlockSpec(memory_space=VMEM)
    return pl.pallas_call(
        down_kernel,
        out_shape=(
            jax.ShapeDtypeStruct((2 * parts, depth, rows), jnp.bfloat16),
            jax.ShapeDtypeStruct((rows, width), jnp.bfloat16),
        ),
        in_specs=[pl.BlockSpec(memory_space=SMEM)] + [in_vmem] * 6,
        out_specs=(in_vmem,) * 2,
        scratch_shapes=[pltpu.VMEM((2 * rows, width), jnp.bfloat16)],
        compiler_params=pltpu.CompilerParams(vmem_limit_bytes=24 << 20),
        cost_estimate=pl.CostEstimate(
            flops=4 * rows * width * parts * depth, bytes_accessed=weight.size * 2, transcendentals=0
        ),
    )(place, act, pull, push, pair, sums, weight)


def backward_kernel(query, near_a, near_b, attn, probs, partial, grad_query, grad_a, grad_b):
    width = query.shape[1]
    half = near_a.shape[0]
    scale = HD ** (-0.5)
    parts = partial.shape[0] // 2
    sides = []
    for side in range(2):
        total = partial[side * parts].astype(jnp.float32)
        for i in range(1, parts):
            total = total + partial[side * parts + i].astype(jnp.float32)
        sides.append(total)
    turned = jnp.concatenate(sides, axis=0)
    for head in range(width // HD):
        cols = slice(head * HD, (head + 1) * HD)
        vcols = slice(width + head * HD, width + (head + 1) * HD)
        g = turned[cols].T.astype(jnp.bfloat16)
        delta = jnp.sum(g.astype(jnp.float32) * attn[:, cols].astype(jnp.float32), axis=1, keepdims=True)
        q = query[:, cols]
        out = None
        for side, (near, result) in enumerate(((near_a, grad_a), (near_b, grad_b))):
            p = probs[head, :, side * half : (side + 1) * half]
            d = (p * (dot(g, near[:, vcols], NT) - delta)).astype(jnp.bfloat16)
            term = dot(d, near[:, cols])
            out = term if out is None else out + term
            result[:, cols] = (dot(d, q, TN) * scale).astype(jnp.bfloat16)
            result[:, vcols] = dot(p.astype(jnp.bfloat16), g, TN).astype(jnp.bfloat16)
        grad_query[:, cols] = out * scale


def backward(query, near_a, near_b, attn, probs, partial):
    rows, width = query.shape
    in_vmem = pl.BlockSpec(memory_space=VMEM)
    return pl.pallas_call(
        backward_kernel,
        out_shape=(
            jax.ShapeDtypeStruct((rows, width), jnp.float32),
            jax.ShapeDtypeStruct(near_a.shape, jnp.bfloat16),
            jax.ShapeDtypeStruct(near_b.shape, jnp.bfloat16),
        ),
        in_specs=[in_vmem] * 6,
        out_specs=(in_vmem,) * 3,
        compiler_params=pltpu.CompilerParams(vmem_limit_bytes=24 << 20),
        cost_estimate=pl.CostEstimate(
            flops=8 * rows * 2 * near_a.shape[0] * width, bytes_accessed=8 << 20, transcendentals=0
        ),
    )(query, near_a, near_b, attn, probs, partial)


def swap(value, axis):
    return lax.ppermute(value, axis, [(0, 1), (1, 0)])


def up_plane(value):
    return lax.ppermute(value, "z", [(i, (i + 1) % PLANES) for i in range(PLANES)])


def down_plane(value):
    return lax.ppermute(value, "z", [(i, (i - 1) % PLANES) for i in range(PLANES)])


def body(query, key, value, tile_mask, weight, cot):
    rows, width = query.shape
    f32, bf16 = jnp.float32, jnp.bfloat16
    place = jnp.stack([lax.axis_index("z"), lax.axis_index("xl"), lax.axis_index("core")]).astype(jnp.int32)
    half_weight = lax.all_gather(weight, ("z", "core"), axis=0, tiled=True)
    own = jnp.concatenate([key, value], axis=1)
    own = jnp.concatenate([own, swap(own, "xl")], axis=0)
    near_a = jnp.concatenate([own, up_plane(own), down_plane(own)], axis=0)
    near_b = swap(near_a, "core")
    attn_out, attn, probs = attend(place, tile_mask, query, near_a, near_b, lax.axis_size(FSDP))
    sides, copies, depth, _ = attn_out.shape
    rows_in = lax.all_to_all(attn_out.reshape(sides * copies, depth, rows), WIDE, 0, 0)
    mine, theirs, held, cot = up(place, rows_in, half_weight, cot)
    act, pull, push, pair, sums = middle(mine, swap(theirs, "xl"), cot, lax.axis_size(SEQ))
    pair = swap(pair, "xl")
    sums = lax.all_to_all(sums, SEQ, 0, 0)
    back, scaled = down(place, act, pull, push, pair, sums, held)
    partial = lax.all_to_all(back, WIDE, 0, 0)
    grad_query, grad_a, grad_b = backward(query, near_a, near_b, attn, probs, partial)
    both = (grad_a.astype(f32) + swap(grad_b, "core").astype(f32)).reshape(3, 2, rows, 2 * width)
    to_low, to_high = both[1].astype(bf16), both[2].astype(bf16)
    here = both[0] + down_plane(to_low).astype(f32) + up_plane(to_high).astype(f32)
    grad_own = here[0] + swap(here[1].astype(bf16), "xl").astype(f32)
    return scaled, grad_query, grad_own[:, :width], grad_own[:, width:]


def solution(mesh):
    fine = Mesh(mesh.devices.reshape(PLANES, 2, 2, 4, 2), SEQ + FSDP)
    both = P(SEQ, FSDP)
    return jax.shard_map(
        body,
        mesh=fine,
        in_specs=(both, both, both, P(), both, both),
        out_specs=(both,) * 4,
        check_vma=False,
    )
```

time: 151 us -> 153 us (1.013)
  waiting for transfers between devices: 46.5 us -> 49.9 us
  blocking collectives: 56.8 us -> 53.6 us
  starting transfers between devices: 14.2 us -> 16.5 us
  other arithmetic: 2.31 us -> 0.69 us
    ppermute x2, waiting for transfers between devices: 4.89 us -> 15.2 us  [up_plane(): lax.ppermute(value, 'z', [(i, (i + 1) % PLANES) for i in range(PLANES)])]
    ppermute x6, waiting for transfers between devices: 26.3 us -> 21.2 us  [swap(): return lax.ppermute(value, axis, [(0, 1), (1, 0)])]
    all_gather x1, waiting for transfers between devices: 2.86 us -> 0.01 us  [body(): half_weight = lax.all_gather(weight, ('z', 'core'), axis=0, tiled=True)]
    ppermute x2, starting transfers between devices: 6.37 us -> 9.16 us  [down_plane(): lax.ppermute(value, 'z', [(i, (i - 1) % PLANES) for i in range(PLANES)])]
    all_to_all x1, blocking collectives: 16.4 us -> 14.6 us  [body(): sums = lax.all_to_all(sums, SEQ, 0, 0)]
    ppermute x2, starting transfers between devices: 1.67 us -> 0.09 us  [up_plane(): lax.ppermute(value, 'z', [(i, (i + 1) % PLANES) for i in range(PLANES)])]
    unnamed x22 -> x11, local copies, waits for them, and re-layouts: 2.7 us -> 3.31 us
    pallas_call x3 -> x4, Pallas kernels: 8.25 us -> 8.74 us  [the longest x1 2.72 us: attend(): pl.pallas_call(attend_kernel, out_shape=(jax.ShapeDtypeStruct((2, copies,...]
  transfers between devices with their start and end apart: 11 -> 11, of which waited for: 10 -> 8; matrix products, arithmetic and copies ran while one was open for 0% -> 1% of each run, Pallas kernels for 2% -> 2%
where the time goes in v3:
time: 153 us; the launch traced here: 152 us
  blocking collectives  53.6 us (35%)
  waiting for transfers between devices  49.9 us (33%)
  starting transfers between devices  16.5 us (11%)
  between operations  14.2 us (9%)
  Pallas kernels  12.3 us (8%)
  local copies, waits for them, and re-layouts  5.12 us (3%)
    ppermute x6, waiting for transfers between devices, swap(): return lax.ppermute(value, axis, [(0, 1), (1, 0)])  21.2 us
    all_to_all x1, blocking collectives, body(): lax.all_to_all(attn_out.reshape(sides * copies, depth, rows), WIDE, 0, 0)  20.7 us
    all_to_all x1, blocking collectives, body(): partial = lax.all_to_all(back, WIDE, 0, 0)  18.2 us
    ppermute x2, waiting for transfers between devices, up_plane(): lax.ppermute(value, 'z', [(i, (i + 1) % PLANES) for i in range(PLANES)])  15.2 us
    all_to_all x1, blocking collectives, body(): sums = lax.all_to_all(sums, SEQ, 0, 0)  14.6 us
    ppermute x2, waiting for transfers between devices, down_plane(): lax.ppermute(value, 'z', [(i, (i - 1) % PLANES) for i in range(PLANES)])  12.8 us
    ppermute x2, starting transfers between devices, down_plane(): lax.ppermute(value, 'z', [(i, (i - 1) % PLANES) for i in range(PLANES)])  9.16 us
    ppermute x6, starting transfers between devices, swap(): return lax.ppermute(value, axis, [(0, 1), (1, 0)])  7.18 us
  transfers between devices with their start and end apart: 11, of which 8 were waited for; matrix products, arithmetic and copies ran while one was open for 1% of the time, Pallas kernels for 2%

profile of v3, /device:TPU:2, one launch (start us, length us, event | category | flops | bytes accessed | tf_op | source)
XLA Modules:
  0.0 152.3 jit_solution(16010079643647599607)
XLA Ops:
  7.2 0.0 all-gather.2.cloned.1.call-start
  7.2 0.7 all-gather.2.cloned.1.call-update
  7.9 0.9 constant_dynamic-update-slice_fusion.1
  8.8 0.9 constant_dynamic-update-slice_fusion
  9.7 2.4 %collective-permute-start = (bf16[128,768]{1,0:T(8,128)(2,1)S(1)}, bf16[128,768]{1,0:T(8,128)(2,1)S(1)}, u32[]{:S(2)}, u32[]{:S(2)}) collective-permute-start(bf16[128,768]{1,0:T(8,128)(2,1)S(1)} %constant_dynamic-update-slice_fusion), channel_id=1, source_target_pairs={{0,16},{16,0},{1,17},{17,1},{2,18},{18,2},{3,19},{19,3},{4,20},{20... | collective-permute-start | bytes 589832 | tf_op jit(solution)/shard_map/ppermute | solution.py:279
  12.1 4.4 %collective-permute-done = bf16[128,768]{1,0:T(8,128)(2,1)S(1)} collective-permute-done((bf16[128,768]{1,0:T(8,128)(2,1)S(1)}, bf16[128,768]{1,0:T(8,128)(2,1)S(1)}, u32[]{:S(2)}, u32[]{:S(2)}) %collective-permute-start) | collective-permute-done | bytes 196640 | tf_op jit(solution)/shard_map/ppermute | solution.py:279
  16.5 0.0 copy-start.2
  16.5 0.0 copy-start.4
  16.5 5.9 %collective-permute-start.2 = (bf16[256,768]{1,0:T(8,128)(2,1)S(1)}, bf16[256,768]{1,0:T(8,128)(2,1)S(1)}, u32[]{:S(2)}, u32[]{:S(2)}) collective-permute-start(bf16[256,768]{1,0:T(8,128)(2,1)S(1)} %pad_maximum_fusion.1), channel_id=1, source_target_pairs={{0,224},{32,0},{64,32},{96,64},{128,96},{160,128},{192,160},{224,1... | collective-permute-start | bytes 1179656 | tf_op jit(solution)/shard_map/ppermute | solution.py:287
  22.4 0.0 collective-permute-start.1
  22.4 12.8 %collective-permute-done.2 = bf16[256,768]{1,0:T(8,128)(2,1)S(1)} collective-permute-done((bf16[256,768]{1,0:T(8,128)(2,1)S(1)}, bf16[256,768]{1,0:T(8,128)(2,1)S(1)}, u32[]{:S(2)}, u32[]{:S(2)}) %collective-permute-start.2) | collective-permute-done | bytes 393248 | tf_op jit(solution)/shard_map/ppermute | solution.py:287
  35.2 6.2 %collective-permute-done.1 = bf16[256,768]{1,0:T(8,128)(2,1)S(1)} collective-permute-done((bf16[256,768]{1,0:T(8,128)(2,1)S(1)}, bf16[256,768]{1,0:T(8,128)(2,1)S(1)}, u32[]{:S(2)}, u32[]{:S(2)}) %collective-permute-start.1) | collective-permute-done | bytes 393248 | tf_op jit(solution)/shard_map/ppermute | solution.py:283
  41.4 0.1 pad_maximum_fusion.near_a
  41.4 0.1 collective-permute-start.3
  41.6 0.1 pad_add_fusion.place
  41.6 2.8 %collective-permute-done.3.near_b = bf16[768,768]{1,0:T(8,128)(2,1)S(1)} collective-permute-done((bf16[768,768]{1,0:T(8,128)(2,1)S(1)}, bf16[768,768]{1,0:T(8,128)(2,1)S(1)}, u32[]{:S(2)}, u32[]{:S(2)}) %collective-permute-start.3) | collective-permute-done | bytes 1179680 | tf_op jit(solution)/shard_map/ppermute | solution.py:279
  44.4 0.0 copy-done.2
  44.4 0.0 copy-done.4
  44.4 2.7 %shard_map.93 = (bf16[2,8,192,128]{3,2,1,0:T(8,128)(2,1)S(1)}, bf16[128,384]{1,0:T(8,128)(2,1)S(1)}, f32[3,128,1536]{2,1,0:T(8,128)S(1)}) custom-call(s32[3]{0:T(128)S(1)} %pad_add_fusion.place, s32[32,32]{1,0:T(8,128)S(1)} %copy-done.4, bf16[128,384]{1,0:T(8,128)(2,1)S(1)} %copy-done.2, bf16[768,768]{1,0:T(8,128)(2,1)S(1)} %pad_maximum_fusion.near_a, ...), custom_call_target="tpu_custom_call" | custom-call | flops 301989888 | bytes 8388608 | tf_op jit(solution)/shard_map/pallas_call | solution.py:82
  47.1 0.0 copy-start
  47.1 1.4 copy-done
  48.5 20.7 %all_to_all.15.rows_in = bf16[16,192,128]{2,1,0:T(8,128)(2,1)S(1)} all-to-all(bf16[16,192,128]{2,1,0:T(8,128)(2,1)S(1)} %bitcast.14), channel_id=1, replica_groups=mesh['z'=8,'xl'=2,'core'=2,'y'=4,'xh'=2] {'xl','y','xh'}, dimensions={0} | all-to-all | bytes 1572864 | tf_op jit(solution)/shard_map/all_to_all | solution.py:301
  69.3 0.0 all-gather.2.cloned.1.call-done
  69.3 0.0 copy-start.3
  69.3 1.0 copy-done.3
  70.3 3.6 %shard_map.94 = (f32[128,1280]{1,0:T(8,128)S(1)}, bf16[128,1280]{1,0:T(8,128)(2,1)S(1)}, bf16[8,192,1280]{2,1,0:T(8,128)(2,1)S(1)}, bf16[128,1280]{1,0:T(8,128)(2,1)S(1)}) custom-call(s32[3]{0:T(128)S(1)} %pad_add_fusion.place, bf16[16,192,128]{2,1,0:T(8,128)(2,1)S(1)} %all_to_all.15.rows_in, bf16[8,192,1280]{2,1,0:T(8,128)(2,1)} %bitcast.15, ...), custom_call_target="tpu_custom_call" | custom-call | flops 1006632960 | bytes 3932160 | tf_op jit(solution)/shard_map/pallas_call | solution.py:129
  73.9 1.5 %collective-permute-start.4 = (bf16[128,1280]{1,0:T(8,128)(2,1)S(1)}, bf16[128,1280]{1,0:T(8,128)(2,1)S(1)}, u32[]{:S(2)}, u32[]{:S(2)}) collective-permute-start(bf16[128,1280]{1,0:T(8,128)(2,1)S(1)} %get-tuple-element.23), channel_id=1, source_target_pairs={{0,16},{16,0},{1,17},{17,1},{2,18},{18,2},{3,19},{19,3},{4,20},{20... | collective-permute-start | bytes 983048 | tf_op jit(solution)/shard_map/ppermute | solution.py:279
  75.4 6.6 %collective-permute-done.4.got = bf16[128,1280]{1,0:T(8,128)(2,1)S(1)} collective-permute-done((bf16[128,1280]{1,0:T(8,128)(2,1)S(1)}, bf16[128,1280]{1,0:T(8,128)(2,1)S(1)}, u32[]{:S(2)}, u32[]{:S(2)}) %collective-permute-start.4) | collective-permute-done | bytes 327712 | tf_op jit(solution)/shard_map/ppermute | solution.py:279
  82.0 0.7 shard_map.95
  82.7 1.6 %collective-permute-start.5 = (bf16[2,128,1280]{2,1,0:T(8,128)(2,1)S(1)}, bf16[2,128,1280]{2,1,0:T(8,128)(2,1)S(1)}, u32[]{:S(2)}, u32[]{:S(2)}) collective-permute-start(bf16[2,128,1280]{2,1,0:T(8,128)(2,1)S(1)} %get-tuple-element.28), channel_id=1, source_target_pairs={{0,16},{16,0},{1,17},{17,1},{2,18},{18,2},{3,19},{19,3},{4,20},{20... | collective-permute-start | bytes 1966088 | tf_op jit(solution)/shard_map/ppermute | solution.py:279
  84.4 14.6 %all_to_all.16.sums = bf16[32,24,128]{2,1,0:T(8,128)(2,1)S(1)} all-to-all(bf16[32,24,128]{2,1,0:T(8,128)(2,1)S(1)} %get-tuple-element.29), channel_id=1, replica_groups=mesh['z'=8,'xl'=2,'core'=2,'y'=4,'xh'=2] {'z','xl','core'}, dimensions={0} | all-to-all | bytes 393216 | tf_op jit(solution)/shard_map/all_to_all | solution.py:305
  99.0 0.0 collective-permute-done.5.pair
  99.0 0.0 copy-start.1
  99.0 2.6 %shard_map.96 = (bf16[16,192,128]{2,1,0:T(8,128)(2,1)S(1)}, bf16[128,1280]{1,0:T(8,128)(2,1)}) custom-call(s32[3]{0:T(128)S(1)} %pad_add_fusion.place, f32[128,1280]{1,0:T(8,128)S(1)} %get-tuple-element.25.act, f32[128,1280]{1,0:T(8,128)S(1)} %get-tuple-element.26.pull, f32[128,1280]{1,0:T(8,128)S(1)} %get-tuple-element.27.push, ...), custom_call_target="tpu_custom_call" | custom-call | flops 1006632960 | bytes 3932160 | tf_op jit(solution)/shard_map/pallas_call | solution.py:214
  101.6 18.2 %all_to_all.17.partial = bf16[16,192,128]{2,1,0:T(8,128)(2,1)S(1)} all-to-all(bf16[16,192,128]{2,1,0:T(8,128)(2,1)S(1)} %get-tuple-element.34), channel_id=1, replica_groups=mesh['z'=8,'xl'=2,'core'=2,'y'=4,'xh'=2] {'xl','y','xh'}, dimensions={0} | all-to-all | bytes 1572864 | tf_op jit(solution)/shard_map/all_to_all | solution.py:307
  119.8 0.0 copy-done.1
  119.8 2.7 %shard_map.97 = (f32[128,384]{1,0:T(8,128)}, bf16[768,768]{1,0:T(8,128)(2,1)S(1)}, bf16[768,768]{1,0:T(8,128)(2,1)S(1)}) custom-call(bf16[128,384]{1,0:T(8,128)(2,1)S(1)} %copy-done.2, bf16[768,768]{1,0:T(8,128)(2,1)S(1)} %pad_maximum_fusion.near_a, bf16[768,768]{1,0:T(8,128)(2,1)S(1)} %collective-permute-done.3.near_b, ...), custom_call_target="tpu_custom_call" | custom-call | flops 603979776 | bytes 8388608 | tf_op jit(solution)/shard_map/pallas_call | solution.py:262
  122.5 0.0 collective-permute-start.6
  122.5 2.8 %collective-permute-done.6 = bf16[768,768]{1,0:T(8,128)(2,1)S(1)} collective-permute-done((bf16[768,768]{1,0:T(8,128)(2,1)S(1)}, bf16[768,768]{1,0:T(8,128)(2,1)S(1)}, u32[]{:S(2)}, u32[]{:S(2)}) %collective-permute-start.6) | collective-permute-done | bytes 1179680 | tf_op jit(solution)/shard_map/ppermute | solution.py:279
  125.4 0.4 convert_add_fusion
  125.7 0.1 fusion.3
  125.8 0.1 collective-permute-start.8
  125.9 3.2 %collective-permute-start.7 = (bf16[2,128,768]{2,1,0:T(8,128)(2,1)S(1)}, bf16[2,128,768]{2,1,0:T(8,128)(2,1)S(1)}, u32[]{:S(2)}, u32[]{:S(2)}) collective-permute-start(bf16[2,128,768]{2,1,0:T(8,128)(2,1)S(1)} %bitcast.17), channel_id=1, source_target_pairs={{0,224},{32,0},{64,32},{96,64},{128,96},{160,128},{192,160},{224,1... | collective-permute-start | bytes 1179656 | tf_op jit(solution)/shard_map/ppermute | solution.py:287
  129.1 0.1 slice.34
  129.2 9.1 %collective-permute-done.8 = bf16[2,128,768]{2,1,0:T(8,128)(2,1)S(1)} collective-permute-done((bf16[2,128,768]{2,1,0:T(8,128)(2,1)S(1)}, bf16[2,128,768]{2,1,0:T(8,128)(2,1)S(1)}, u32[]{:S(2)}, u32[]{:S(2)}) %collective-permute-start.8) | collective-permute-done | bytes 393248 | tf_op jit(solution)/shard_map/ppermute | solution.py:283
  138.2 0.0 collective-permute-done.7
  138.2 0.1 convert_add_fusion.1
  138.4 1.5 %collective-permute-start.9 = (bf16[128,768]{1,0:T(8,128)(2,1)S(1)}, bf16[128,768]{1,0:T(8,128)(2,1)S(1)}, u32[]{:S(2)}, u32[]{:S(2)}) collective-permute-start(bf16[128,768]{1,0:T(8,128)(2,1)S(1)} %fusion.1), channel_id=1, source_target_pairs={{0,16},{16,0},{1,17},{17,1},{2,18},{18,2},{3,19},{19,3},{4,20},{20... | collective-permute-start | bytes 589832 | tf_op jit(solution)/shard_map/ppermute | solution.py:279
  139.9 4.7 %collective-permute-done.9 = bf16[128,768]{1,0:T(8,128)(2,1)S(1)} collective-permute-done((bf16[128,768]{1,0:T(8,128)(2,1)S(1)}, bf16[128,768]{1,0:T(8,128)(2,1)S(1)}, u32[]{:S(2)}, u32[]{:S(2)}) %collective-permute-start.9) | collective-permute-done | bytes 196640 | tf_op jit(solution)/shard_map/ppermute | solution.py:279
  144.6 0.8 fusion.4
  (3 shorter events, 0.1 us)
Async XLA Ops:
  7.2 62.1 %all-gather.2.cloned.1.call-start = ((), (), s32[]{:S(2)}) async-start(), calls=%async_computation.3 | async-start | bytes 4177920 | tf_op jit(solution)/shard_map/all_gather | solution.py:294
  9.7 6.7 %collective-permute-start = (bf16[128,768]{1,0:T(8,128)(2,1)S(1)}, bf16[128,768]{1,0:T(8,128)(2,1)S(1)}, u32[]{:S(2)}, u32[]{:S(2)}) collective-permute-start(bf16[128,768]{1,0:T(8,128)(2,1)S(1)} %constant_dynamic-update-slice_fusion), channel_id=1, source_target_pairs={{0,16},{16,0},{1,17},{17,1},{2,18},{18,2},{3,19},{19,3},{4,20},{20... | collective-permute-start | bytes 589832 | tf_op jit(solution)/shard_map/ppermute | solution.py:279
  16.5 27.9 %copy-start.2 = (bf16[128,384]{1,0:T(8,128)(2,1)S(1)}, bf16[128,384]{1,0:T(8,128)(2,1)}, u32[]{:S(2)}) copy-start(bf16[128,384]{1,0:T(8,128)(2,1)} %query.3) | copy-start | bytes 294916
  16.5 27.9 %copy-start.4 = (s32[32,32]{1,0:T(8,128)S(1)}, s32[32,32]{1,0:T(8,128)}, u32[]{:S(2)}) copy-start(s32[32,32]{1,0:T(8,128)} %mask.1) | copy-start | bytes 12292
  16.5 18.7 %collective-permute-start.2 = (bf16[256,768]{1,0:T(8,128)(2,1)S(1)}, bf16[256,768]{1,0:T(8,128)(2,1)S(1)}, u32[]{:S(2)}, u32[]{:S(2)}) collective-permute-start(bf16[256,768]{1,0:T(8,128)(2,1)S(1)} %pad_maximum_fusion.1), channel_id=1, source_target_pairs={{0,224},{32,0},{64,32},{96,64},{128,96},{160,128},{192,160},{224,1... | collective-permute-start | bytes 1179656 | tf_op jit(solution)/shard_map/ppermute | solution.py:287
  22.4 18.9 %collective-permute-start.1 = (bf16[256,768]{1,0:T(8,128)(2,1)S(1)}, bf16[256,768]{1,0:T(8,128)(2,1)S(1)}, u32[]{:S(2)}, u32[]{:S(2)}) collective-permute-start(bf16[256,768]{1,0:T(8,128)(2,1)S(1)} %pad_maximum_fusion.1), channel_id=1, source_target_pairs={{0,32},{32,64},{64,96},{96,128},{128,160},{160,192},{192,224},{224... | collective-permute-start | bytes 1179656 | tf_op jit(solution)/shard_map/ppermute | solution.py:283
  41.4 2.9 %collective-permute-start.3 = (bf16[768,768]{1,0:T(8,128)(2,1)S(1)}, bf16[768,768]{1,0:T(8,128)(2,1)S(1)}, u32[]{:S(2)}, u32[]{:S(2)}) collective-permute-start(bf16[768,768]{1,0:T(8,128)(2,1)S(1)} %pad_maximum_fusion.near_a), channel_id=1, source_target_pairs={{0,8},{8,0},{1,9},{9,1},{2,10},{10,2},{3,11},{11,3},{4,12},{12,4},... | collective-permute-start | bytes 3538952 | tf_op jit(solution)/shard_map/ppermute | solution.py:279
  47.1 1.4 copy-start
  69.3 1.0 copy-start.3
  73.9 8.1 %collective-permute-start.4 = (bf16[128,1280]{1,0:T(8,128)(2,1)S(1)}, bf16[128,1280]{1,0:T(8,128)(2,1)S(1)}, u32[]{:S(2)}, u32[]{:S(2)}) collective-permute-start(bf16[128,1280]{1,0:T(8,128)(2,1)S(1)} %get-tuple-element.23), channel_id=1, source_target_pairs={{0,16},{16,0},{1,17},{17,1},{2,18},{18,2},{3,19},{19,3},{4,20},{20... | collective-permute-start | bytes 983048 | tf_op jit(solution)/shard_map/ppermute | solution.py:279
  82.7 16.3 %collective-permute-start.5 = (bf16[2,128,1280]{2,1,0:T(8,128)(2,1)S(1)}, bf16[2,128,1280]{2,1,0:T(8,128)(2,1)S(1)}, u32[]{:S(2)}, u32[]{:S(2)}) collective-permute-start(bf16[2,128,1280]{2,1,0:T(8,128)(2,1)S(1)} %get-tuple-element.28), channel_id=1, source_target_pairs={{0,16},{16,0},{1,17},{17,1},{2,18},{18,2},{3,19},{19,3},{4,20},{20... | collective-permute-start | bytes 1966088 | tf_op jit(solution)/shard_map/ppermute | solution.py:279
  99.0 20.8 %copy-start.1 = (f32[3,128,1536]{2,1,0:T(8,128)S(1)}, f32[3,128,1536]{2,1,0:T(8,128)}, u32[]{:S(2)}) copy-start(f32[3,128,1536]{2,1,0:T(8,128)} %copy-done) | copy-start | bytes 7077892
  122.5 2.8 %collective-permute-start.6 = (bf16[768,768]{1,0:T(8,128)(2,1)S(1)}, bf16[768,768]{1,0:T(8,128)(2,1)S(1)}, u32[]{:S(2)}, u32[]{:S(2)}) collective-permute-start(bf16[768,768]{1,0:T(8,128)(2,1)S(1)} %get-tuple-element.37), channel_id=1, source_target_pairs={{0,8},{8,0},{1,9},{9,1},{2,10},{10,2},{3,11},{11,3},{4,12},{12,4},... | collective-permute-start | bytes 3538952 | tf_op jit(solution)/shard_map/ppermute | solution.py:279
  125.8 12.4 %collective-permute-start.8 = (bf16[2,128,768]{2,1,0:T(8,128)(2,1)S(1)}, bf16[2,128,768]{2,1,0:T(8,128)(2,1)S(1)}, u32[]{:S(2)}, u32[]{:S(2)}) collective-permute-start(bf16[2,128,768]{2,1,0:T(8,128)(2,1)S(1)} %bitcast.18), channel_id=1, source_target_pairs={{0,32},{32,64},{64,96},{96,128},{128,160},{160,192},{192,224},{224... | collective-permute-start | bytes 1179656 | tf_op jit(solution)/shard_map/ppermute | solution.py:283
  125.9 12.4 %collective-permute-start.7 = (bf16[2,128,768]{2,1,0:T(8,128)(2,1)S(1)}, bf16[2,128,768]{2,1,0:T(8,128)(2,1)S(1)}, u32[]{:S(2)}, u32[]{:S(2)}) collective-permute-start(bf16[2,128,768]{2,1,0:T(8,128)(2,1)S(1)} %bitcast.17), channel_id=1, source_target_pairs={{0,224},{32,0},{64,32},{96,64},{128,96},{160,128},{192,160},{224,1... | collective-permute-start | bytes 1179656 | tf_op jit(solution)/shard_map/ppermute | solution.py:287
  138.4 6.2 %collective-permute-start.9 = (bf16[128,768]{1,0:T(8,128)(2,1)S(1)}, bf16[128,768]{1,0:T(8,128)(2,1)S(1)}, u32[]{:S(2)}, u32[]{:S(2)}) collective-permute-start(bf16[128,768]{1,0:T(8,128)(2,1)S(1)} %fusion.1), channel_id=1, source_target_pairs={{0,16},{16,0},{1,17},{17,1},{2,18},{18,2},{3,19},{19,3},{4,20},{20... | collective-permute-start | bytes 589832 | tf_op jit(solution)/shard_map/ppermute | solution.py:279
Sparse Core Ops, SparseCore 0:
  9.8 46.8 all-gather.1

commit v4 on v3

--- a/solution.py
+++ b/solution.py
@@ -15,6 +15,7 @@
 ROOT = 0.7978845608028654
 CUBIC = 0.044715
 PLANES = 8
+GROUP = 4
 NEAR = ((0, 0), (1, 0), (0, -1), (1, -1), (0, 1), (1, 1))
 SEQ = ("z", "xl", "core")
 FSDP = ("y", "xh")
@@ -29,7 +30,7 @@
     return lax.dot_general(a, b, dims, preferred_element_type=jnp.float32)
 
 
-def attend_kernel(place, mask, query, near_a, near_b, out, plain, probs):
+def attend_kernel(place, mask, query, near_a, near_b, cot, out, plain, probs, cot_out, kept, sent):
     z, xl, core = place[0], place[1], place[2]
     me = 4 * z + 2 * xl + core
 
@@ -59,8 +60,9 @@
         inv = 1.0 / (jnp.sum(e_a, axis=1, keepdims=True) + jnp.sum(e_b, axis=1, keepdims=True))
         p_a = e_a * inv
         p_b = e_b * inv
-        probs[head, :, :half] = p_a
-        probs[head, :, half:] = p_b
+        kept[head, :, :half] = p_a
+        kept[head, :, half:] = p_b
+        pltpu.make_async_copy(kept.at[head], probs.at[head], sent.at[head]).start()
         mixed = dot(p_a.astype(jnp.bfloat16), near_a[:, vcols]) + dot(p_b.astype(jnp.bfloat16), near_b[:, vcols])
         mixed = mixed.astype(jnp.bfloat16)
         plain[:, cols] = mixed
@@ -73,75 +75,92 @@
             piece = turned[start - head * HD : stop - head * HD]
             out[side, :, low : low + stop - start, :] = jnp.broadcast_to(piece[None], (copies,) + piece.shape)
             start = stop
-
-
-def attend(place, mask, query, near_a, near_b, copies):
+    cot_out[...] = cot[...]
+    for head in range(width // HD):
+        pltpu.make_async_copy(kept.at[head], probs.at[head], sent.at[head]).wait()
+
+
+def attend(place, mask, query, near_a, near_b, cot, copies):
     rows, width = query.shape
     heads = width // HD
     keys = 2 * near_a.shape[0]
+    in_vmem = pl.BlockSpec(memory_space=VMEM)
     return pl.pallas_call(
         attend_kernel,
         out_shape=(
             jax.ShapeDtypeStruct((2, copies, width // 2, rows), jnp.bfloat16),
             jax.ShapeDtypeStruct((rows, width), jnp.bfloat16),
-            jax.ShapeDtypeStruct((heads, rows, keys), jnp.float32),
-        ),
-        in_specs=[pl.BlockSpec(memory_space=SMEM)] * 2 + [pl.BlockSpec(memory_space=VMEM)] * 3,
-        out_specs=(pl.BlockSpec(memory_space=VMEM),) * 3,
-        compiler_params=pltpu.CompilerParams(vmem_limit_bytes=24 << 20),
+            pltpu.HBM((heads, rows, keys), jnp.float32),
+            jax.ShapeDtypeStruct(cot.shape, cot.dtype),
+        ),
+        in_specs=[pl.BlockSpec(memory_space=SMEM)] * 2 + [in_vmem] * 4,
+        out_specs=(in_vmem, in_vmem, pl.BlockSpec(memory_space=pltpu.HBM), in_vmem),
+        scratch_shapes=[pltpu.VMEM((heads, rows, keys), jnp.float32), pltpu.SemaphoreType.DMA((heads,))],
+        compiler_params=pltpu.CompilerParams(vmem_limit_bytes=16 << 20),
         cost_estimate=pl.CostEstimate(flops=4 * rows * keys * width, bytes_accessed=8 << 20, transcendentals=heads * rows * keys),
-    )(place, mask, query, near_a, near_b)
-
-
-def up_kernel(place, rows_in, weight, cot, mine, theirs, held, cot_out, total, arrived):
-    parts, depth, _ = weight.shape
+    )(place, mask, query, near_a, near_b, cot)
+
+
+def up_far_kernel(place, rows_in, weight, theirs, held, arrived):
+    parts, depth, width = held.shape
     rows = rows_in.shape[2]
-    own = place[1]
+    other = 1 - place[1]
     copies = [pltpu.make_async_copy(weight.at[part], held.at[part], arrived.at[part]) for part in range(parts)]
-    copies.append(pltpu.make_async_copy(cot, cot_out, arrived.at[parts]))
     for copy in copies:
         copy.start()
-    group = 4
-    for first in range(0, parts, group):
-        for copy in copies[first : first + group]:
+    total = None
+    for first in range(0, parts, GROUP):
+        for copy in copies[first : first + GROUP]:
             copy.wait()
-        near = rows_in[pl.ds(own * parts + first, group)].reshape(group * depth, rows)
-        far = rows_in[pl.ds((1 - own) * parts + first, group)].reshape(group * depth, rows)
-        held_rows = held[first : first + group].reshape(group * depth, held.shape[2])
-        term = dot(jnp.concatenate([near, far], axis=1), held_rows, TN)
-        if first == 0:
-            total[...] = term
-        elif first + group < parts:
-            total[...] += term
-        else:
-            term = total[...] + term
-            mine[...] = term[:rows]
-            theirs[...] = term[rows:].astype(jnp.bfloat16)
-    copies[parts].wait()
-
-
-def up(place, rows_in, weight, cot):
+        far = rows_in[pl.ds(other * parts + first, GROUP)].reshape(GROUP * depth, rows)
+        term = dot(far, held[first : first + GROUP].reshape(GROUP * depth, width), TN)
+        total = term if total is None else total + term
+    theirs[...] = total.astype(jnp.bfloat16)
+
+
+def up_far(place, rows_in, weight):
     sides, depth, rows = rows_in.shape
     parts = sides // 2
     width = weight.shape[1]
     in_vmem = pl.BlockSpec(memory_space=VMEM)
     in_hbm = pl.BlockSpec(memory_space=pltpu.HBM)
     return pl.pallas_call(
-        up_kernel,
-        out_shape=(
-            jax.ShapeDtypeStruct((rows, width), jnp.float32),
+        up_far_kernel,
+        out_shape=(
             jax.ShapeDtypeStruct((rows, width), jnp.bfloat16),
             VMEM((parts, depth, width), jnp.bfloat16),
-            VMEM(cot.shape, jnp.bfloat16),
-        ),
-        in_specs=[pl.BlockSpec(memory_space=SMEM), in_vmem, in_hbm, in_hbm],
-        out_specs=(in_vmem,) * 4,
-        scratch_shapes=[pltpu.VMEM((2 * rows, width), jnp.float32), pltpu.SemaphoreType.DMA((parts + 1,))],
+        ),
+        in_specs=[pl.BlockSpec(memory_space=SMEM), in_vmem, in_hbm],
+        out_specs=(in_vmem,) * 2,
+        scratch_shapes=[pltpu.SemaphoreType.DMA((parts,))],
         compiler_params=pltpu.CompilerParams(vmem_limit_bytes=46 << 20),
         cost_estimate=pl.CostEstimate(
-            flops=4 * rows * width * parts * depth, bytes_accessed=weight.size * 2, transcendentals=0
-        ),
-    )(place, rows_in, weight.reshape(parts, depth, width), cot)
+            flops=2 * rows * width * parts * depth, bytes_accessed=weight.size * 2, transcendentals=0
+        ),
+    )(place, rows_in, weight.reshape(parts, depth, width))
+
+
+def up_near_kernel(place, rows_in, held, mine):
+    parts, depth, width = held.shape
+    rows = rows_in.shape[2]
+    near = rows_in[pl.ds(place[1] * parts, parts)].reshape(parts * depth, rows)
+    mine[...] = dot(near, held[...].reshape(parts * depth, width), TN)
+
+
+def up_near(place, rows_in, held):
+    parts, depth, width = held.shape
+    rows = rows_in.shape[2]
+    in_vmem = pl.BlockSpec(memory_space=VMEM)
+    return pl.pallas_call(
+        up_near_kernel,
+        out_shape=jax.ShapeDtypeStruct((rows, width), jnp.float32),
+        in_specs=[pl.BlockSpec(memory_space=SMEM), in_vmem, in_vmem],
+        out_specs=in_vmem,
+        compiler_params=pltpu.CompilerParams(vmem_limit_bytes=16 << 20),
+        cost_estimate=pl.CostEstimate(
+            flops=2 * rows * width * parts * depth, bytes_accessed=held.size * 2, transcendentals=0
+        ),
+    )(place, rows_in, held)
 
 
 def middle_kernel(mine, got, cot, act_out, pull_out, push_out, pair, sums):
@@ -181,7 +200,7 @@
         ),
         in_specs=[in_vmem] * 3,
         out_specs=(in_vmem,) * 5,
-        compiler_params=pltpu.CompilerParams(vmem_limit_bytes=24 << 20),
+        compiler_params=pltpu.CompilerParams(vmem_limit_bytes=16 << 20),
         cost_estimate=pl.CostEstimate(flops=40 * rows * width, bytes_accessed=4 << 20, transcendentals=rows * width),
     )(mine, got, cot)
 
@@ -220,7 +239,7 @@
         in_specs=[pl.BlockSpec(memory_space=SMEM)] + [in_vmem] * 6,
         out_specs=(in_vmem,) * 2,
         scratch_shapes=[pltpu.VMEM((2 * rows, width), jnp.bfloat16)],
-        compiler_params=pltpu.CompilerParams(vmem_limit_bytes=24 << 20),
+        compiler_params=pltpu.CompilerParams(vmem_limit_bytes=16 << 20),
         cost_estimate=pl.CostEstimate(
             flops=4 * rows * width * parts * depth, bytes_accessed=weight.size * 2, transcendentals=0
         ),
@@ -268,7 +287,7 @@
         ),
         in_specs=[in_vmem] * 6,
         out_specs=(in_vmem,) * 3,
-        compiler_params=pltpu.CompilerParams(vmem_limit_bytes=24 << 20),
+        compiler_params=pltpu.CompilerParams(vmem_limit_bytes=16 << 20),
         cost_estimate=pl.CostEstimate(
             flops=8 * rows * 2 * near_a.shape[0] * width, bytes_accessed=8 << 20, transcendentals=0
         ),
@@ -292,15 +311,20 @@
     f32, bf16 = jnp.float32, jnp.bfloat16
     place = jnp.stack([lax.axis_index("z"), lax.axis_index("xl"), lax.axis_index("core")]).astype(jnp.int32)
     half_weight = lax.all_gather(weight, ("z", "core"), axis=0, tiled=True)
-    own = jnp.concatenate([key, value], axis=1)
-    own = jnp.concatenate([own, swap(own, "xl")], axis=0)
-    near_a = jnp.concatenate([own, up_plane(own), down_plane(own)], axis=0)
+    own = lax.pad(key, jnp.zeros((), bf16), ((0, 0, 0), (0, width, 0)))
+    own = own + lax.pad(value, jnp.zeros((), bf16), ((0, 0, 0), (width, 0, 0)))
+    from_low, from_high = up_plane(own), down_plane(own)
+    own_x = swap(own, "xl")
+    far_x = swap(jnp.concatenate([from_low, from_high], axis=0), "xl")
+    near_a = jnp.concatenate([own, own_x, from_low, far_x[:rows], from_high, far_x[rows:]], axis=0)
     near_b = swap(near_a, "core")
-    attn_out, attn, probs = attend(place, tile_mask, query, near_a, near_b, lax.axis_size(FSDP))
+    attn_out, attn, probs, cot = attend(place, tile_mask, query, near_a, near_b, cot, lax.axis_size(FSDP))
     sides, copies, depth, _ = attn_out.shape
     rows_in = lax.all_to_all(attn_out.reshape(sides * copies, depth, rows), WIDE, 0, 0)
-    mine, theirs, held, cot = up(place, rows_in, half_weight, cot)
-    act, pull, push, pair, sums = middle(mine, swap(theirs, "xl"), cot, lax.axis_size(SEQ))
+    theirs, held = up_far(place, rows_in, half_weight)
+    got = swap(theirs, "xl")
+    mine = up_near(place, rows_in, held)
+    act, pull, push, pair, sums = middle(mine, got, cot, lax.axis_size(SEQ))
     pair = swap(pair, "xl")
     sums = lax.all_to_all(sums, SEQ, 0, 0)
     back, scaled = down(place, act, pull, push, pair, sums, held)

time: 153 us -> 142 us (0.928)
  waiting for transfers between devices: 49.9 us -> 41.4 us
  local copies, waits for them, and re-layouts: 5.12 us -> 1.71 us
  Pallas kernels: 12.3 us -> 14.1 us
    ppermute x2, waiting for transfers between devices: 12.8 us -> 3.62 us  [down_plane(): lax.ppermute(value, 'z', [(i, (i - 1) % PLANES) for i in range(PLANES)])]
    ppermute x6 -> x7, waiting for transfers between devices: 21.2 us -> 24.6 us  [swap(): return lax.ppermute(value, axis, [(0, 1), (1, 0)])]
    ppermute x2, waiting for transfers between devices: 15.2 us -> 12.5 us  [up_plane(): lax.ppermute(value, 'z', [(i, (i + 1) % PLANES) for i in range(PLANES)])]
    unnamed x11 -> x16, local copies, waits for them, and re-layouts: 3.31 us -> 0.8 us
    ppermute x6 -> x7, starting transfers between devices: 7.18 us -> 5.99 us  [swap(): return lax.ppermute(value, axis, [(0, 1), (1, 0)])]
    pallas_call x1 -> x2, Pallas kernels: 3.61 us -> 4.66 us  [the longest x1 3.39 us: up_far(): pl.pallas_call(up_far_kernel, out_shape=(jax.ShapeDtypeStruct((rows, widt...]
  transfers between devices with their start and end apart: 11 -> 12, of which waited for: 8 -> 8; matrix products, arithmetic and copies ran while one was open for 1% -> 1% of each run, Pallas kernels for 2% -> 3%
where the time goes in v4:
time: 142 us
  blocking collectives  53.4 us (38%)
  waiting for transfers between devices  41.4 us (29%)
  starting transfers between devices  15.3 us (11%)
  between operations  14.2 us (10%)
  Pallas kernels  14.1 us (10%)
  local copies, waits for them, and re-layouts  1.71 us (1%)
  other arithmetic  1.5 us (1%)
    ppermute x7, waiting for transfers between devices, swap(): return lax.ppermute(value, axis, [(0, 1), (1, 0)])  24.6 us
    all_to_all x1, blocking collectives, body(): lax.all_to_all(attn_out.reshape(sides * copies, depth, rows), WIDE, 0, 0)  20.6 us
    all_to_all x1, blocking collectives, body(): partial = lax.all_to_all(back, WIDE, 0, 0)  17.7 us
    all_to_all x1, blocking collectives, body(): sums = lax.all_to_all(sums, SEQ, 0, 0)  15.2 us
    ppermute x2, waiting for transfers between devices, up_plane(): lax.ppermute(value, 'z', [(i, (i + 1) % PLANES) for i in range(PLANES)])  12.5 us
    ppermute x2, starting transfers between devices, down_plane(): lax.ppermute(value, 'z', [(i, (i - 1) % PLANES) for i in range(PLANES)])  7.78 us
    ppermute x7, starting transfers between devices, swap(): return lax.ppermute(value, axis, [(0, 1), (1, 0)])  5.99 us
    ppermute x2, waiting for transfers between devices, down_plane(): lax.ppermute(value, 'z', [(i, (i - 1) % PLANES) for i in range(PLANES)])  3.62 us
  transfers between devices with their start and end apart: 12, of which 8 were waited for; matrix products, arithmetic and copies ran while one was open for 1% of the time, Pallas kernels for 3%

profile of v4, /device:TPU:2, one launch (start us, length us, event | category | flops | bytes accessed | tf_op | source)
XLA Modules:
  0.0 141.6 jit_solution(18311764340783097090)
XLA Ops:
  7.2 0.0 all-gather.2.cloned.1.call-start
  7.2 0.7 all-gather.2.cloned.1.call-update
  7.9 1.0 pad_add_fusion
  8.9 5.9 %collective-permute-start.2 = (bf16[128,768]{1,0:T(8,128)(2,1)S(1)}, bf16[128,768]{1,0:T(8,128)(2,1)S(1)}, u32[]{:S(2)}, u32[]{:S(2)}) collective-permute-start(bf16[128,768]{1,0:T(8,128)(2,1)S(1)} %get-tuple-element.42), channel_id=1, source_target_pairs={{0,224},{32,0},{64,32},{96,64},{128,96},{160,128},{192,160},{224,1... | collective-permute-start | bytes 589832 | tf_op jit(solution)/shard_map/ppermute | solution.py:306
  14.8 0.0 collective-permute-start.1
  14.8 0.5 collective-permute-start
  15.3 3.6 %collective-permute-done.2 = bf16[128,768]{1,0:T(8,128)(2,1)S(1)} collective-permute-done((bf16[128,768]{1,0:T(8,128)(2,1)S(1)}, bf16[128,768]{1,0:T(8,128)(2,1)S(1)}, u32[]{:S(2)}, u32[]{:S(2)}) %collective-permute-start.2) | collective-permute-done | bytes 196640 | tf_op jit(solution)/shard_map/ppermute | solution.py:306
  19.0 3.4 %collective-permute-done.1 = bf16[128,768]{1,0:T(8,128)(2,1)S(1)} collective-permute-done((bf16[128,768]{1,0:T(8,128)(2,1)S(1)}, bf16[128,768]{1,0:T(8,128)(2,1)S(1)}, u32[]{:S(2)}, u32[]{:S(2)}) %collective-permute-start.1) | collective-permute-done | bytes 196640 | tf_op jit(solution)/shard_map/ppermute | solution.py:302
  22.4 0.0 copy-start.1
  22.4 0.0 copy-start.2
  22.4 0.0 copy-start.5
  22.4 0.6 collective-permute-start.3
  23.1 0.0 collective-permute-done
  23.1 9.1 %collective-permute-done.3 = bf16[256,768]{1,0:T(8,128)(2,1)S(1)} collective-permute-done((bf16[256,768]{1,0:T(8,128)(2,1)S(1)}, bf16[256,768]{1,0:T(8,128)(2,1)S(1)}, u32[]{:S(2)}, u32[]{:S(2)}) %collective-permute-start.3) | collective-permute-done | bytes 393248 | tf_op jit(solution)/shard_map/ppermute | solution.py:298
  32.3 0.1 collective-permute-start.4
  32.4 0.1 pad_add_fusion.1.place
  32.4 2.8 %collective-permute-done.4.near_b = bf16[768,768]{1,0:T(8,128)(2,1)S(1)} collective-permute-done((bf16[768,768]{1,0:T(8,128)(2,1)S(1)}, bf16[768,768]{1,0:T(8,128)(2,1)S(1)}, u32[]{:S(2)}, u32[]{:S(2)}) %collective-permute-start.4) | collective-permute-done | bytes 1179680 | tf_op jit(solution)/shard_map/ppermute | solution.py:298
  35.2 0.0 copy-done.1
  35.2 0.0 copy-done.2
  35.2 0.0 copy-done.5
  35.2 3.4 %shard_map.93 = (bf16[2,8,192,128]{3,2,1,0:T(8,128)(2,1)S(1)}, bf16[128,384]{1,0:T(8,128)(2,1)S(1)}, f32[3,128,1536]{2,1,0:T(8,128)}, bf16[128,1280]{1,0:T(8,128)(2,1)S(1)}) custom-call(s32[3]{0:T(128)S(1)} %pad_add_fusion.1.place, s32[32,32]{1,0:T(8,128)S(1)} %copy-done.5, bf16[128,384]{1,0:T(8,128)(2,1)S(1)} %copy-done.1, ...), custom_call_target="tpu_custom_call" | custom-call | flops 301989888 | bytes 8388608 | tf_op jit(solution)/shard_map/pallas_call | solution.py:88
  38.6 0.0 copy-start.3
  38.6 0.7 copy-done.3
  39.3 20.6 %all_to_all.15.rows_in = bf16[16,192,128]{2,1,0:T(8,128)(2,1)S(1)} all-to-all(bf16[16,192,128]{2,1,0:T(8,128)(2,1)S(1)} %bitcast.14), channel_id=1, replica_groups=mesh['z'=8,'xl'=2,'core'=2,'y'=4,'xh'=2] {'xl','y','xh'}, dimensions={0} | all-to-all | bytes 1572864 | tf_op jit(solution)/shard_map/all_to_all | solution.py:323
  59.9 0.0 all-gather.2.cloned.1.call-done
  59.9 3.4 %shard_map.94 = (bf16[128,1280]{1,0:T(8,128)(2,1)S(1)}, bf16[8,192,1280]{2,1,0:T(8,128)(2,1)S(1)}) custom-call(s32[3]{0:T(128)S(1)} %pad_add_fusion.1.place, bf16[16,192,128]{2,1,0:T(8,128)(2,1)S(1)} %all_to_all.15.rows_in, bf16[8,192,1280]{2,1,0:T(8,128)(2,1)} %bitcast.15), custom_call_target="tpu_custom_call" | custom-call | flops 503316480 | bytes 3932160 | tf_op jit(solution)/shard_map/pallas_call | solution.py:127
  63.3 1.5 %collective-permute-start.5 = (bf16[128,1280]{1,0:T(8,128)(2,1)S(1)}, bf16[128,1280]{1,0:T(8,128)(2,1)S(1)}, u32[]{:S(2)}, u32[]{:S(2)}) collective-permute-start(bf16[128,1280]{1,0:T(8,128)(2,1)S(1)} %get-tuple-element.22), channel_id=1, source_target_pairs={{0,16},{16,0},{1,17},{17,1},{2,18},{18,2},{3,19},{19,3},{4,20},{20... | collective-permute-start | bytes 983048 | tf_op jit(solution)/shard_map/ppermute | solution.py:298
  64.9 0.0 copy-start.4
  64.9 1.3 shard_map.95.mine
  66.2 5.3 %collective-permute-done.5.got = bf16[128,1280]{1,0:T(8,128)(2,1)S(1)} collective-permute-done((bf16[128,1280]{1,0:T(8,128)(2,1)S(1)}, bf16[128,1280]{1,0:T(8,128)(2,1)S(1)}, u32[]{:S(2)}, u32[]{:S(2)}) %collective-permute-start.5) | collective-permute-done | bytes 327712 | tf_op jit(solution)/shard_map/ppermute | solution.py:298
  71.5 0.0 copy-done.4
  71.5 0.7 shard_map.96
  72.2 1.6 %collective-permute-start.6 = (bf16[2,128,1280]{2,1,0:T(8,128)(2,1)S(1)}, bf16[2,128,1280]{2,1,0:T(8,128)(2,1)S(1)}, u32[]{:S(2)}, u32[]{:S(2)}) collective-permute-start(bf16[2,128,1280]{2,1,0:T(8,128)(2,1)S(1)} %get-tuple-element.27), channel_id=1, source_target_pairs={{0,16},{16,0},{1,17},{17,1},{2,18},{18,2},{3,19},{19,3},{4,20},{20... | collective-permute-start | bytes 1966088 | tf_op jit(solution)/shard_map/ppermute | solution.py:298
  73.8 15.2 %all_to_all.16.sums = bf16[32,24,128]{2,1,0:T(8,128)(2,1)S(1)} all-to-all(bf16[32,24,128]{2,1,0:T(8,128)(2,1)S(1)} %get-tuple-element.28), channel_id=1, replica_groups=mesh['z'=8,'xl'=2,'core'=2,'y'=4,'xh'=2] {'z','xl','core'}, dimensions={0} | all-to-all | bytes 393216 | tf_op jit(solution)/shard_map/all_to_all | solution.py:329
  89.0 0.0 collective-permute-done.6.pair
  89.0 0.0 copy-start
  89.0 2.6 %shard_map.97 = (bf16[16,192,128]{2,1,0:T(8,128)(2,1)S(1)}, bf16[128,1280]{1,0:T(8,128)(2,1)}) custom-call(s32[3]{0:T(128)S(1)} %pad_add_fusion.1.place, f32[128,1280]{1,0:T(8,128)S(1)} %get-tuple-element.24.act, f32[128,1280]{1,0:T(8,128)S(1)} %get-tuple-element.25.pull, f32[128,1280]{1,0:T(8,128)S(1)} %get-tuple-element.26.push, ...), custom_call_target="tpu_custom_call" | custom-call | flops 1006632960 | bytes 3932160 | tf_op jit(solution)/shard_map/pallas_call | solution.py:233
  91.6 17.7 %all_to_all.17.partial = bf16[16,192,128]{2,1,0:T(8,128)(2,1)S(1)} all-to-all(bf16[16,192,128]{2,1,0:T(8,128)(2,1)S(1)} %get-tuple-element.32), channel_id=1, replica_groups=mesh['z'=8,'xl'=2,'core'=2,'y'=4,'xh'=2] {'xl','y','xh'}, dimensions={0} | all-to-all | bytes 1572864 | tf_op jit(solution)/shard_map/all_to_all | solution.py:331
  109.3 0.0 copy-done
  109.3 2.7 %shard_map.98 = (f32[128,384]{1,0:T(8,128)}, bf16[768,768]{1,0:T(8,128)(2,1)S(1)}, bf16[768,768]{1,0:T(8,128)(2,1)S(1)}) custom-call(bf16[128,384]{1,0:T(8,128)(2,1)S(1)} %copy-done.1, bf16[768,768]{1,0:T(8,128)(2,1)S(1)} %slice_dynamic-update-slice_fusion.near_a, bf16[768,768]{1,0:T(8,128)(2,1)S(1)} %collective-permute-done.4.near_b, ...), custom_call_target="tpu_custom_call" | custom-call | flops 603979776 | bytes 8388608 | tf_op jit(solution)/shard_map/pallas_call | solution.py:281
  112.0 0.0 collective-permute-start.7
  112.0 2.8 %collective-permute-done.7 = bf16[768,768]{1,0:T(8,128)(2,1)S(1)} collective-permute-done((bf16[768,768]{1,0:T(8,128)(2,1)S(1)}, bf16[768,768]{1,0:T(8,128)(2,1)S(1)}, u32[]{:S(2)}, u32[]{:S(2)}) %collective-permute-start.7) | collective-permute-done | bytes 1179680 | tf_op jit(solution)/shard_map/ppermute | solution.py:298
  114.8 0.3 convert_add_fusion
  115.1 0.1 fusion.3
  115.2 1.5 %collective-permute-start.9 = (bf16[2,128,768]{2,1,0:T(8,128)(2,1)S(1)}, bf16[2,128,768]{2,1,0:T(8,128)(2,1)S(1)}, u32[]{:S(2)}, u32[]{:S(2)}) collective-permute-start(bf16[2,128,768]{2,1,0:T(8,128)(2,1)S(1)} %bitcast.18), channel_id=1, source_target_pairs={{0,32},{32,64},{64,96},{96,128},{128,160},{160,192},{192,224},{224... | collective-permute-start | bytes 1179656 | tf_op jit(solution)/shard_map/ppermute | solution.py:302
  116.6 1.8 %collective-permute-start.8 = (bf16[2,128,768]{2,1,0:T(8,128)(2,1)S(1)}, bf16[2,128,768]{2,1,0:T(8,128)(2,1)S(1)}, u32[]{:S(2)}, u32[]{:S(2)}) collective-permute-start(bf16[2,128,768]{2,1,0:T(8,128)(2,1)S(1)} %bitcast.17), channel_id=1, source_target_pairs={{0,224},{32,0},{64,32},{96,64},{128,96},{160,128},{192,160},{224,1... | collective-permute-start | bytes 1179656 | tf_op jit(solution)/shard_map/ppermute | solution.py:306
  118.5 0.1 slice.44
  118.5 9.1 %collective-permute-done.9 = bf16[2,128,768]{2,1,0:T(8,128)(2,1)S(1)} collective-permute-done((bf16[2,128,768]{2,1,0:T(8,128)(2,1)S(1)}, bf16[2,128,768]{2,1,0:T(8,128)(2,1)S(1)}, u32[]{:S(2)}, u32[]{:S(2)}) %collective-permute-start.9) | collective-permute-done | bytes 393248 | tf_op jit(solution)/shard_map/ppermute | solution.py:302
  127.6 0.0 collective-permute-done.8
  127.6 0.1 convert_add_fusion.1
  127.8 1.5 %collective-permute-start.10 = (bf16[128,768]{1,0:T(8,128)(2,1)S(1)}, bf16[128,768]{1,0:T(8,128)(2,1)S(1)}, u32[]{:S(2)}, u32[]{:S(2)}) collective-permute-start(bf16[128,768]{1,0:T(8,128)(2,1)S(1)} %fusion.1), channel_id=1, source_target_pairs={{0,16},{16,0},{1,17},{17,1},{2,18},{18,2},{3,19},{19,3},{4,20},{20... | collective-permute-start | bytes 589832 | tf_op jit(solution)/shard_map/ppermute | solution.py:298
  129.3 4.7 %collective-permute-done.10 = bf16[128,768]{1,0:T(8,128)(2,1)S(1)} collective-permute-done((bf16[128,768]{1,0:T(8,128)(2,1)S(1)}, bf16[128,768]{1,0:T(8,128)(2,1)S(1)}, u32[]{:S(2)}, u32[]{:S(2)}) %collective-permute-start.10) | collective-permute-done | bytes 196640 | tf_op jit(solution)/shard_map/ppermute | solution.py:298
  134.0 0.8 fusion.4
  (8 shorter events, 0.2 us)
Async XLA Ops:
  7.2 52.8 %all-gather.2.cloned.1.call-start = ((), (), s32[]{:S(2)}) async-start(), calls=%async_computation.3 | async-start | bytes 4177920 | tf_op jit(solution)/shard_map/all_gather | solution.py:313
  8.9 10.1 %collective-permute-start.2 = (bf16[128,768]{1,0:T(8,128)(2,1)S(1)}, bf16[128,768]{1,0:T(8,128)(2,1)S(1)}, u32[]{:S(2)}, u32[]{:S(2)}) collective-permute-start(bf16[128,768]{1,0:T(8,128)(2,1)S(1)} %get-tuple-element.42), channel_id=1, source_target_pairs={{0,224},{32,0},{64,32},{96,64},{128,96},{160,128},{192,160},{224,1... | collective-permute-start | bytes 589832 | tf_op jit(solution)/shard_map/ppermute | solution.py:306
  14.8 7.6 %collective-permute-start.1 = (bf16[128,768]{1,0:T(8,128)(2,1)S(1)}, bf16[128,768]{1,0:T(8,128)(2,1)S(1)}, u32[]{:S(2)}, u32[]{:S(2)}) collective-permute-start(bf16[128,768]{1,0:T(8,128)(2,1)S(1)} %get-tuple-element.42), channel_id=1, source_target_pairs={{0,32},{32,64},{64,96},{96,128},{128,160},{160,192},{192,224},{224... | collective-permute-start | bytes 589832 | tf_op jit(solution)/shard_map/ppermute | solution.py:302
  14.8 8.3 %collective-permute-start = (bf16[128,768]{1,0:T(8,128)(2,1)S(1)}, bf16[128,768]{1,0:T(8,128)(2,1)S(1)}, u32[]{:S(2)}, u32[]{:S(2)}) collective-permute-start(bf16[128,768]{1,0:T(8,128)(2,1)S(1)} %get-tuple-element.42), channel_id=1, source_target_pairs={{0,16},{16,0},{1,17},{17,1},{2,18},{18,2},{3,19},{19,3},{4,20},{20... | collective-permute-start | bytes 589832 | tf_op jit(solution)/shard_map/ppermute | solution.py:298
  22.4 12.8 %copy-start.1 = (bf16[128,384]{1,0:T(8,128)(2,1)S(1)}, bf16[128,384]{1,0:T(8,128)(2,1)}, u32[]{:S(2)}) copy-start(bf16[128,384]{1,0:T(8,128)(2,1)} %query.3) | copy-start | bytes 294916
  22.4 12.8 %copy-start.2 = (bf16[128,1280]{1,0:T(8,128)(2,1)S(1)}, bf16[128,1280]{1,0:T(8,128)(2,1)}, u32[]{:S(2)}) copy-start(bf16[128,1280]{1,0:T(8,128)(2,1)} %cot.1) | copy-start | bytes 983044
  22.4 12.8 %copy-start.5 = (s32[32,32]{1,0:T(8,128)S(1)}, s32[32,32]{1,0:T(8,128)}, u32[]{:S(2)}) copy-start(s32[32,32]{1,0:T(8,128)} %mask.1) | copy-start | bytes 12292
  22.4 9.8 %collective-permute-start.3 = (bf16[256,768]{1,0:T(8,128)(2,1)S(1)}, bf16[256,768]{1,0:T(8,128)(2,1)S(1)}, u32[]{:S(2)}, u32[]{:S(2)}) collective-permute-start(bf16[256,768]{1,0:T(8,128)(2,1)S(1)} %pad_maximum_fusion), channel_id=1, source_target_pairs={{0,16},{16,0},{1,17},{17,1},{2,18},{18,2},{3,19},{19,3},{4,20},{20... | collective-permute-start | bytes 1179656 | tf_op jit(solution)/shard_map/ppermute | solution.py:298
  32.3 2.9 %collective-permute-start.4 = (bf16[768,768]{1,0:T(8,128)(2,1)S(1)}, bf16[768,768]{1,0:T(8,128)(2,1)S(1)}, u32[]{:S(2)}, u32[]{:S(2)}) collective-permute-start(bf16[768,768]{1,0:T(8,128)(2,1)S(1)} %slice_dynamic-update-slice_fusion.near_a), channel_id=1, source_target_pairs={{0,8},{8,0},{1,9},{9,1},{2,10},{10,2},{3,11},{11,3},{4,12},{12,4},... | collective-permute-start | bytes 3538952 | tf_op jit(solution)/shard_map/ppermute | solution.py:298
  38.6 0.7 copy-start.3
  63.3 8.1 %collective-permute-start.5 = (bf16[128,1280]{1,0:T(8,128)(2,1)S(1)}, bf16[128,1280]{1,0:T(8,128)(2,1)S(1)}, u32[]{:S(2)}, u32[]{:S(2)}) collective-permute-start(bf16[128,1280]{1,0:T(8,128)(2,1)S(1)} %get-tuple-element.22), channel_id=1, source_target_pairs={{0,16},{16,0},{1,17},{17,1},{2,18},{18,2},{3,19},{19,3},{4,20},{20... | collective-permute-start | bytes 983048 | tf_op jit(solution)/shard_map/ppermute | solution.py:298
  64.9 6.6 %copy-start.4 = (bf16[128,1280]{1,0:T(8,128)(2,1)S(1)}, bf16[128,1280]{1,0:T(8,128)(2,1)}, u32[]{:S(2)}) copy-start(bf16[128,1280]{1,0:T(8,128)(2,1)} %copy-done.3) | copy-start | bytes 983044
  72.2 16.8 %collective-permute-start.6 = (bf16[2,128,1280]{2,1,0:T(8,128)(2,1)S(1)}, bf16[2,128,1280]{2,1,0:T(8,128)(2,1)S(1)}, u32[]{:S(2)}, u32[]{:S(2)}) collective-permute-start(bf16[2,128,1280]{2,1,0:T(8,128)(2,1)S(1)} %get-tuple-element.27), channel_id=1, source_target_pairs={{0,16},{16,0},{1,17},{17,1},{2,18},{18,2},{3,19},{19,3},{4,20},{20... | collective-permute-start | bytes 1966088 | tf_op jit(solution)/shard_map/ppermute | solution.py:298
  89.0 20.3 %copy-start = (f32[3,128,1536]{2,1,0:T(8,128)S(1)}, f32[3,128,1536]{2,1,0:T(8,128)}, u32[]{:S(2)}) copy-start(f32[3,128,1536]{2,1,0:T(8,128)} %get-tuple-element.31.probs) | copy-start | bytes 7077892
  112.0 2.8 %collective-permute-start.7 = (bf16[768,768]{1,0:T(8,128)(2,1)S(1)}, bf16[768,768]{1,0:T(8,128)(2,1)S(1)}, u32[]{:S(2)}, u32[]{:S(2)}) collective-permute-start(bf16[768,768]{1,0:T(8,128)(2,1)S(1)} %get-tuple-element.35), channel_id=1, source_target_pairs={{0,8},{8,0},{1,9},{9,1},{2,10},{10,2},{3,11},{11,3},{4,12},{12,4},... | collective-permute-start | bytes 3538952 | tf_op jit(solution)/shard_map/ppermute | solution.py:298
  115.2 12.4 %collective-permute-start.9 = (bf16[2,128,768]{2,1,0:T(8,128)(2,1)S(1)}, bf16[2,128,768]{2,1,0:T(8,128)(2,1)S(1)}, u32[]{:S(2)}, u32[]{:S(2)}) collective-permute-start(bf16[2,128,768]{2,1,0:T(8,128)(2,1)S(1)} %bitcast.18), channel_id=1, source_target_pairs={{0,32},{32,64},{64,96},{96,128},{128,160},{160,192},{192,224},{224... | collective-permute-start | bytes 1179656 | tf_op jit(solution)/shard_map/ppermute | solution.py:302
  116.6 11.0 %collective-permute-start.8 = (bf16[2,128,768]{2,1,0:T(8,128)(2,1)S(1)}, bf16[2,128,768]{2,1,0:T(8,128)(2,1)S(1)}, u32[]{:S(2)}, u32[]{:S(2)}) collective-permute-start(bf16[2,128,768]{2,1,0:T(8,128)(2,1)S(1)} %bitcast.17), channel_id=1, source_target_pairs={{0,224},{32,0},{64,32},{96,64},{128,96},{160,128},{192,160},{224,1... | collective-permute-start | bytes 1179656 | tf_op jit(solution)/shard_map/ppermute | solution.py:306
  127.8 6.2 %collective-permute-start.10 = (bf16[128,768]{1,0:T(8,128)(2,1)S(1)}, bf16[128,768]{1,0:T(8,128)(2,1)S(1)}, u32[]{:S(2)}, u32[]{:S(2)}) collective-permute-start(bf16[128,768]{1,0:T(8,128)(2,1)S(1)} %fusion.1), channel_id=1, source_target_pairs={{0,16},{16,0},{1,17},{17,1},{2,18},{18,2},{3,19},{19,3},{4,20},{20... | collective-permute-start | bytes 589832 | tf_op jit(solution)/shard_map/ppermute | solution.py:298
Sparse Core Ops, SparseCore 0:
  9.8 44.7 all-gather.1

commit v5 on v4

--- a/solution.py
+++ b/solution.py
@@ -15,7 +15,7 @@
 ROOT = 0.7978845608028654
 CUBIC = 0.044715
 PLANES = 8
-GROUP = 4
+GROUP = 2
 NEAR = ((0, 0), (1, 0), (0, -1), (1, -1), (0, 1), (1, 1))
 SEQ = ("z", "xl", "core")
 FSDP = ("y", "xh")
@@ -30,7 +30,7 @@
     return lax.dot_general(a, b, dims, preferred_element_type=jnp.float32)
 
 
-def attend_kernel(place, mask, query, near_a, near_b, cot, out, plain, probs, cot_out, kept, sent):
+def attend_kernel(place, mask, query, near_a, near_b, out, plain, probs, kept, sent):
     z, xl, core = place[0], place[1], place[2]
     me = 4 * z + 2 * xl + core
 
@@ -58,12 +58,12 @@
         e_a = jnp.exp(s_a - top)
         e_b = jnp.exp(s_b - top)
         inv = 1.0 / (jnp.sum(e_a, axis=1, keepdims=True) + jnp.sum(e_b, axis=1, keepdims=True))
-        p_a = e_a * inv
-        p_b = e_b * inv
+        p_a = (e_a * inv).astype(jnp.bfloat16)
+        p_b = (e_b * inv).astype(jnp.bfloat16)
         kept[head, :, :half] = p_a
         kept[head, :, half:] = p_b
         pltpu.make_async_copy(kept.at[head], probs.at[head], sent.at[head]).start()
-        mixed = dot(p_a.astype(jnp.bfloat16), near_a[:, vcols]) + dot(p_b.astype(jnp.bfloat16), near_b[:, vcols])
+        mixed = dot(p_a, near_a[:, vcols]) + dot(p_b, near_b[:, vcols])
         mixed = mixed.astype(jnp.bfloat16)
         plain[:, cols] = mixed
         turned = mixed.astype(jnp.float32).T.astype(jnp.bfloat16)
@@ -75,12 +75,11 @@
             piece = turned[start - head * HD : stop - head * HD]
             out[side, :, low : low + stop - start, :] = jnp.broadcast_to(piece[None], (copies,) + piece.shape)
             start = stop
-    cot_out[...] = cot[...]
     for head in range(width // HD):
         pltpu.make_async_copy(kept.at[head], probs.at[head], sent.at[head]).wait()
 
 
-def attend(place, mask, query, near_a, near_b, cot, copies):
+def attend(place, mask, query, near_a, near_b, copies):
     rows, width = query.shape
     heads = width // HD
     keys = 2 * near_a.shape[0]
@@ -90,15 +89,14 @@
         out_shape=(
             jax.ShapeDtypeStruct((2, copies, width // 2, rows), jnp.bfloat16),
             jax.ShapeDtypeStruct((rows, width), jnp.bfloat16),
-            pltpu.HBM((heads, rows, keys), jnp.float32),
-            jax.ShapeDtypeStruct(cot.shape, cot.dtype),
-        ),
-        in_specs=[pl.BlockSpec(memory_space=SMEM)] * 2 + [in_vmem] * 4,
-        out_specs=(in_vmem, in_vmem, pl.BlockSpec(memory_space=pltpu.HBM), in_vmem),
-        scratch_shapes=[pltpu.VMEM((heads, rows, keys), jnp.float32), pltpu.SemaphoreType.DMA((heads,))],
+            pltpu.HBM((heads, rows, keys), jnp.bfloat16),
+        ),
+        in_specs=[pl.BlockSpec(memory_space=SMEM)] * 2 + [in_vmem] * 3,
+        out_specs=(in_vmem, in_vmem, pl.BlockSpec(memory_space=pltpu.HBM)),
+        scratch_shapes=[pltpu.VMEM((heads, rows, keys), jnp.bfloat16), pltpu.SemaphoreType.DMA((heads,))],
         compiler_params=pltpu.CompilerParams(vmem_limit_bytes=16 << 20),
         cost_estimate=pl.CostEstimate(flops=4 * rows * keys * width, bytes_accessed=8 << 20, transcendentals=heads * rows * keys),
-    )(place, mask, query, near_a, near_b, cot)
+    )(place, mask, query, near_a, near_b)
 
 
 def up_far_kernel(place, rows_in, weight, theirs, held, arrived):
@@ -267,11 +265,11 @@
         out = None
         for side, (near, result) in enumerate(((near_a, grad_a), (near_b, grad_b))):
             p = probs[head, :, side * half : (side + 1) * half]
-            d = (p * (dot(g, near[:, vcols], NT) - delta)).astype(jnp.bfloat16)
+            d = (p.astype(jnp.float32) * (dot(g, near[:, vcols], NT) - delta)).astype(jnp.bfloat16)
             term = dot(d, near[:, cols])
             out = term if out is None else out + term
             result[:, cols] = (dot(d, q, TN) * scale).astype(jnp.bfloat16)
-            result[:, vcols] = dot(p.astype(jnp.bfloat16), g, TN).astype(jnp.bfloat16)
+            result[:, vcols] = dot(p, g, TN).astype(jnp.bfloat16)
         grad_query[:, cols] = out * scale
 
 
@@ -304,6 +302,13 @@
 
 def down_plane(value):
     return lax.ppermute(value, "z", [(i, (i - 1) % PLANES) for i in range(PLANES)])
+
+
+def shifted(value, planes, xl):
+    pairs = [
+        (2 * i + j, 2 * ((i + planes) % PLANES) + (j + xl) % 2) for i in range(PLANES) for j in range(2)
+    ]
+    return lax.ppermute(value, ("z", "xl"), pairs)
 
 
 def body(query, key, value, tile_mask, weight, cot):
@@ -318,7 +323,7 @@
     far_x = swap(jnp.concatenate([from_low, from_high], axis=0), "xl")
     near_a = jnp.concatenate([own, own_x, from_low, far_x[:rows], from_high, far_x[rows:]], axis=0)
     near_b = swap(near_a, "core")
-    attn_out, attn, probs, cot = attend(place, tile_mask, query, near_a, near_b, cot, lax.axis_size(FSDP))
+    attn_out, attn, probs = attend(place, tile_mask, query, near_a, near_b, lax.axis_size(FSDP))
     sides, copies, depth, _ = attn_out.shape
     rows_in = lax.all_to_all(attn_out.reshape(sides * copies, depth, rows), WIDE, 0, 0)
     theirs, held = up_far(place, rows_in, half_weight)
@@ -330,10 +335,13 @@
     back, scaled = down(place, act, pull, push, pair, sums, held)
     partial = lax.all_to_all(back, WIDE, 0, 0)
     grad_query, grad_a, grad_b = backward(query, near_a, near_b, attn, probs, partial)
-    both = (grad_a.astype(f32) + swap(grad_b, "core").astype(f32)).reshape(3, 2, rows, 2 * width)
-    to_low, to_high = both[1].astype(bf16), both[2].astype(bf16)
-    here = both[0] + down_plane(to_low).astype(f32) + up_plane(to_high).astype(f32)
-    grad_own = here[0] + swap(here[1].astype(bf16), "xl").astype(f32)
+    both = grad_a.astype(f32) + swap(grad_b, "core").astype(f32)
+    blocks = [both[i * rows : (i + 1) * rows] for i in range(6)]
+    moves = ((1, 0, 1), (3, -1, 1), (5, 1, 1), (2, -1, 0), (4, 1, 0))
+    arrived = [shifted(blocks[i].astype(bf16), planes, xl) for i, planes, xl in moves]
+    grad_own = blocks[0]
+    for block in arrived:
+        grad_own = grad_own + block.astype(f32)
     return scaled, grad_query, grad_own[:, :width], grad_own[:, width:]
 
 

time: 142 us -> 140 us (0.986)
  waiting for transfers between devices: 41.4 us -> 36.1 us
  starting transfers between devices: 15.3 us -> 19.3 us
    ppermute x2 -> x1, waiting for transfers between devices: 12.5 us -> 3.41 us  [up_plane(): lax.ppermute(value, 'z', [(i, (i + 1) % PLANES) for i in range(PLANES)])]
    ppermute x0 -> x5, starting transfers between devices: none -> 8.91 us  [shifted(): return lax.ppermute(value, ('z', 'xl'), pairs)]
    ppermute x0 -> x5, waiting for transfers between devices: none -> 8.34 us  [shifted(): return lax.ppermute(value, ('z', 'xl'), pairs)]
    ppermute x7 -> x6, waiting for transfers between devices: 24.6 us -> 20 us  [swap(): return lax.ppermute(value, axis, [(0, 1), (1, 0)])]
    ppermute x2 -> x1, starting transfers between devices: 7.78 us -> 5.93 us  [down_plane(): lax.ppermute(value, 'z', [(i, (i - 1) % PLANES) for i in range(PLANES)])]
    ppermute x7 -> x6, starting transfers between devices: 5.99 us -> 4.41 us  [swap(): return lax.ppermute(value, axis, [(0, 1), (1, 0)])]
    ppermute x2 -> x1, starting transfers between devices: 1.47 us -> 0.01 us  [up_plane(): lax.ppermute(value, 'z', [(i, (i + 1) % PLANES) for i in range(PLANES)])]
    ppermute x2 -> x1, waiting for transfers between devices: 3.62 us -> 3.62 us  [down_plane(): lax.ppermute(value, 'z', [(i, (i - 1) % PLANES) for i in range(PLANES)])]
  transfers between devices with their start and end apart: 12 -> 14, of which waited for: 8 -> 10; matrix products, arithmetic and copies ran while one was open for 1% -> 1% of each run, Pallas kernels for 3% -> 3%
where the time goes in v5:
time: 140 us; the launch traced here: 139 us
  blocking collectives  53.6 us (38%)
  waiting for transfers between devices  36.1 us (26%)
  starting transfers between devices  19.3 us (14%)
  between operations  14.2 us (10%)
  Pallas kernels  13.9 us (10%)
  other arithmetic  1.48 us (1%)
    all_to_all x1, blocking collectives, body(): lax.all_to_all(attn_out.reshape(sides * copies, depth, rows), WIDE, 0, 0)  20.6 us
    ppermute x6, waiting for transfers between devices, swap(): return lax.ppermute(value, axis, [(0, 1), (1, 0)])  20 us
    all_to_all x1, blocking collectives, body(): partial = lax.all_to_all(back, WIDE, 0, 0)  17.8 us
    all_to_all x1, blocking collectives, body(): sums = lax.all_to_all(sums, SEQ, 0, 0)  15.1 us
    ppermute x5, starting transfers between devices, shifted(): return lax.ppermute(value, ('z', 'xl'), pairs)  8.91 us
    ppermute x5, waiting for transfers between devices, shifted(): return lax.ppermute(value, ('z', 'xl'), pairs)  8.34 us
    ppermute x1, starting transfers between devices, down_plane(): lax.ppermute(value, 'z', [(i, (i - 1) % PLANES) for i in range(PLANES)])  5.93 us
    ppermute x6, starting transfers between devices, swap(): return lax.ppermute(value, axis, [(0, 1), (1, 0)])  4.41 us
  transfers between devices with their start and end apart: 14, of which 10 were waited for; matrix products, arithmetic and copies ran while one was open for 1% of the time, Pallas kernels for 3%

profile of v5, /device:TPU:2, one launch (start us, length us, event | category | flops | bytes accessed | tf_op | source)
XLA Modules:
  0.0 139.5 jit_solution(10772684924747191)
XLA Ops:
  7.2 0.0 all-gather.2.cloned.1.call-start
  7.2 0.7 all-gather.2.cloned.1.call-update
  7.9 1.0 pad_add_fusion
  8.9 5.9 %collective-permute-start.2 = (bf16[128,768]{1,0:T(8,128)(2,1)S(1)}, bf16[128,768]{1,0:T(8,128)(2,1)S(1)}, u32[]{:S(2)}, u32[]{:S(2)}) collective-permute-start(bf16[128,768]{1,0:T(8,128)(2,1)S(1)} %get-tuple-element.43), channel_id=1, source_target_pairs={{0,224},{32,0},{64,32},{96,64},{128,96},{160,128},{192,160},{224,1... | collective-permute-start | bytes 589832 | tf_op jit(solution)/shard_map/ppermute | solution.py:304
  14.8 0.0 collective-permute-start.1
  14.8 0.5 collective-permute-start
  15.3 3.6 %collective-permute-done.2 = bf16[128,768]{1,0:T(8,128)(2,1)S(1)} collective-permute-done((bf16[128,768]{1,0:T(8,128)(2,1)S(1)}, bf16[128,768]{1,0:T(8,128)(2,1)S(1)}, u32[]{:S(2)}, u32[]{:S(2)}) %collective-permute-start.2) | collective-permute-done | bytes 196640 | tf_op jit(solution)/shard_map/ppermute | solution.py:304
  19.0 3.4 %collective-permute-done.1 = bf16[128,768]{1,0:T(8,128)(2,1)S(1)} collective-permute-done((bf16[128,768]{1,0:T(8,128)(2,1)S(1)}, bf16[128,768]{1,0:T(8,128)(2,1)S(1)}, u32[]{:S(2)}, u32[]{:S(2)}) %collective-permute-start.1) | collective-permute-done | bytes 196640 | tf_op jit(solution)/shard_map/ppermute | solution.py:300
  22.4 0.0 copy-start.1
  22.4 0.0 copy-start.3
  22.4 0.6 collective-permute-start.3
  23.1 0.0 collective-permute-done
  23.1 9.1 %collective-permute-done.3 = bf16[256,768]{1,0:T(8,128)(2,1)S(1)} collective-permute-done((bf16[256,768]{1,0:T(8,128)(2,1)S(1)}, bf16[256,768]{1,0:T(8,128)(2,1)S(1)}, u32[]{:S(2)}, u32[]{:S(2)}) %collective-permute-start.3) | collective-permute-done | bytes 393248 | tf_op jit(solution)/shard_map/ppermute | solution.py:296
  32.2 0.1 collective-permute-start.4
  32.4 0.1 pad_add_fusion.1.place
  32.4 2.8 %collective-permute-done.4.near_b = bf16[768,768]{1,0:T(8,128)(2,1)S(1)} collective-permute-done((bf16[768,768]{1,0:T(8,128)(2,1)S(1)}, bf16[768,768]{1,0:T(8,128)(2,1)S(1)}, u32[]{:S(2)}, u32[]{:S(2)}) %collective-permute-start.4) | collective-permute-done | bytes 1179680 | tf_op jit(solution)/shard_map/ppermute | solution.py:296
  35.2 0.0 copy-done.1
  35.2 0.0 copy-done.3
  35.2 3.4 %shard_map.93 = (bf16[2,8,192,128]{3,2,1,0:T(8,128)(2,1)S(1)}, bf16[128,384]{1,0:T(8,128)(2,1)S(1)}, bf16[3,128,1536]{2,1,0:T(8,128)(2,1)}) custom-call(s32[3]{0:T(128)S(1)} %pad_add_fusion.1.place, s32[32,32]{1,0:T(8,128)S(1)} %copy-done.3, bf16[128,384]{1,0:T(8,128)(2,1)S(1)} %copy-done.1, bf16[768,768]{1,0:T(8,128)(2,1)S(1)} %slice_dynamic-update-slice_fusion.near_a, ...), custom_call_target="tpu_custom_call" | custom-call | flops 301989888 | bytes 8388608 | tf_op jit(solution)/shard_map/pallas_call | solution.py:87
  38.6 20.6 %all_to_all.15.rows_in = bf16[16,192,128]{2,1,0:T(8,128)(2,1)S(1)} all-to-all(bf16[16,192,128]{2,1,0:T(8,128)(2,1)S(1)} %bitcast.5), channel_id=1, replica_groups=mesh['z'=8,'xl'=2,'core'=2,'y'=4,'xh'=2] {'xl','y','xh'}, dimensions={0} | all-to-all | bytes 1572864 | tf_op jit(solution)/shard_map/all_to_all | solution.py:328
  59.3 0.0 all-gather.2.cloned.1.call-done
  59.3 3.2 %shard_map.94 = (bf16[128,1280]{1,0:T(8,128)(2,1)S(1)}, bf16[8,192,1280]{2,1,0:T(8,128)(2,1)S(1)}) custom-call(s32[3]{0:T(128)S(1)} %pad_add_fusion.1.place, bf16[16,192,128]{2,1,0:T(8,128)(2,1)S(1)} %all_to_all.15.rows_in, bf16[8,192,1280]{2,1,0:T(8,128)(2,1)} %bitcast.6), custom_call_target="tpu_custom_call" | custom-call | flops 503316480 | bytes 3932160 | tf_op jit(solution)/shard_map/pallas_call | solution.py:125
  62.5 1.5 %collective-permute-start.5 = (bf16[128,1280]{1,0:T(8,128)(2,1)S(1)}, bf16[128,1280]{1,0:T(8,128)(2,1)S(1)}, u32[]{:S(2)}, u32[]{:S(2)}) collective-permute-start(bf16[128,1280]{1,0:T(8,128)(2,1)S(1)} %get-tuple-element.21), channel_id=1, source_target_pairs={{0,16},{16,0},{1,17},{17,1},{2,18},{18,2},{3,19},{19,3},{4,20},{20... | collective-permute-start | bytes 983048 | tf_op jit(solution)/shard_map/ppermute | solution.py:296
  64.0 0.0 copy-start.2
  64.0 1.3 shard_map.95.mine
  65.3 5.3 %collective-permute-done.5.got = bf16[128,1280]{1,0:T(8,128)(2,1)S(1)} collective-permute-done((bf16[128,1280]{1,0:T(8,128)(2,1)S(1)}, bf16[128,1280]{1,0:T(8,128)(2,1)S(1)}, u32[]{:S(2)}, u32[]{:S(2)}) %collective-permute-start.5) | collective-permute-done | bytes 327712 | tf_op jit(solution)/shard_map/ppermute | solution.py:296
  70.6 0.0 copy-done.2
  70.6 0.7 shard_map.96
  71.4 1.6 %collective-permute-start.6 = (bf16[2,128,1280]{2,1,0:T(8,128)(2,1)S(1)}, bf16[2,128,1280]{2,1,0:T(8,128)(2,1)S(1)}, u32[]{:S(2)}, u32[]{:S(2)}) collective-permute-start(bf16[2,128,1280]{2,1,0:T(8,128)(2,1)S(1)} %get-tuple-element.25), channel_id=1, source_target_pairs={{0,16},{16,0},{1,17},{17,1},{2,18},{18,2},{3,19},{19,3},{4,20},{20... | collective-permute-start | bytes 1966088 | tf_op jit(solution)/shard_map/ppermute | solution.py:296
  73.0 15.1 %all_to_all.16.sums = bf16[32,24,128]{2,1,0:T(8,128)(2,1)S(1)} all-to-all(bf16[32,24,128]{2,1,0:T(8,128)(2,1)S(1)} %get-tuple-element.26), channel_id=1, replica_groups=mesh['z'=8,'xl'=2,'core'=2,'y'=4,'xh'=2] {'z','xl','core'}, dimensions={0} | all-to-all | bytes 393216 | tf_op jit(solution)/shard_map/all_to_all | solution.py:334
  88.1 0.0 collective-permute-done.6.pair
  88.1 2.6 %shard_map.97 = (bf16[16,192,128]{2,1,0:T(8,128)(2,1)S(1)}, bf16[128,1280]{1,0:T(8,128)(2,1)}) custom-call(s32[3]{0:T(128)S(1)} %pad_add_fusion.1.place, f32[128,1280]{1,0:T(8,128)S(1)} %get-tuple-element.22.act, f32[128,1280]{1,0:T(8,128)S(1)} %get-tuple-element.23.pull, f32[128,1280]{1,0:T(8,128)S(1)} %get-tuple-element.24.push, ...), custom_call_target="tpu_custom_call" | custom-call | flops 1006632960 | bytes 3932160 | tf_op jit(solution)/shard_map/pallas_call | solution.py:231
  90.7 0.0 copy-start
  90.7 17.8 %all_to_all.17.partial = bf16[16,192,128]{2,1,0:T(8,128)(2,1)S(1)} all-to-all(bf16[16,192,128]{2,1,0:T(8,128)(2,1)S(1)} %get-tuple-element.30), channel_id=1, replica_groups=mesh['z'=8,'xl'=2,'core'=2,'y'=4,'xh'=2] {'xl','y','xh'}, dimensions={0} | all-to-all | bytes 1572864 | tf_op jit(solution)/shard_map/all_to_all | solution.py:336
  108.6 0.0 copy-done
  108.6 2.7 %shard_map.98 = (f32[128,384]{1,0:T(8,128)}, bf16[768,768]{1,0:T(8,128)(2,1)S(1)}, bf16[768,768]{1,0:T(8,128)(2,1)S(1)}) custom-call(bf16[128,384]{1,0:T(8,128)(2,1)S(1)} %copy-done.1, bf16[768,768]{1,0:T(8,128)(2,1)S(1)} %slice_dynamic-update-slice_fusion.near_a, bf16[768,768]{1,0:T(8,128)(2,1)S(1)} %collective-permute-done.4.near_b, ...), custom_call_target="tpu_custom_call" | custom-call | flops 603979776 | bytes 8388608 | tf_op jit(solution)/shard_map/pallas_call | solution.py:279
  111.3 0.0 collective-permute-start.7
  111.3 2.8 %collective-permute-done.7 = bf16[768,768]{1,0:T(8,128)(2,1)S(1)} collective-permute-done((bf16[768,768]{1,0:T(8,128)(2,1)S(1)}, bf16[768,768]{1,0:T(8,128)(2,1)S(1)}, u32[]{:S(2)}, u32[]{:S(2)}) %collective-permute-start.7) | collective-permute-done | bytes 1179680 | tf_op jit(solution)/shard_map/ppermute | solution.py:296
  114.1 0.3 fusion.4
  114.4 0.1 fusion.5
  114.5 1.5 %collective-permute-start.8 = (bf16[128,768]{1,0:T(8,128)(2,1)S(1)}, bf16[128,768]{1,0:T(8,128)(2,1)S(1)}, u32[]{:S(2)}, u32[]{:S(2)}) collective-permute-start(bf16[128,768]{1,0:T(8,128)(2,1)S(1)} %get-tuple-element.36), channel_id=1, source_target_pairs={{0,16},{16,0},{32,48},{48,32},{64,80},{80,64},{96,112},{112,96},{1... | collective-permute-start | bytes 589832 | tf_op jit(solution)/shard_map/ppermute | solution.py:311
  116.0 2.3 %collective-permute-start.12 = (bf16[128,768]{1,0:T(8,128)(2,1)S(1)}, bf16[128,768]{1,0:T(8,128)(2,1)S(1)}, u32[]{:S(2)}, u32[]{:S(2)}) collective-permute-start(bf16[128,768]{1,0:T(8,128)(2,1)S(1)} %get-tuple-element.37), channel_id=1, source_target_pairs={{0,32},{16,48},{32,64},{48,80},{64,96},{80,112},{96,128},{112,144}... | collective-permute-start | bytes 589832 | tf_op jit(solution)/shard_map/ppermute | solution.py:311
  118.3 0.9 collective-permute-start.11
  119.3 1.1 collective-permute-start.10
  120.4 3.0 %collective-permute-start.9 = (bf16[128,768]{1,0:T(8,128)(2,1)S(1)}, bf16[128,768]{1,0:T(8,128)(2,1)S(1)}, u32[]{:S(2)}, u32[]{:S(2)}) collective-permute-start(bf16[128,768]{1,0:T(8,128)(2,1)S(1)} %get-tuple-element.40), channel_id=1, source_target_pairs={{0,240},{16,224},{32,16},{48,0},{64,48},{80,32},{96,80},{112,64},{... | collective-permute-start | bytes 589832 | tf_op jit(solution)/shard_map/ppermute | solution.py:311
  123.4 0.0 collective-permute-done.8
  123.4 1.6 %collective-permute-done.12 = bf16[128,768]{1,0:T(8,128)(2,1)S(1)} collective-permute-done((bf16[128,768]{1,0:T(8,128)(2,1)S(1)}, bf16[128,768]{1,0:T(8,128)(2,1)S(1)}, u32[]{:S(2)}, u32[]{:S(2)}) %collective-permute-start.12) | collective-permute-done | bytes 196640 | tf_op jit(solution)/shard_map/ppermute | solution.py:311
  125.0 1.2 collective-permute-done.11
  126.2 4.2 %collective-permute-done.10 = bf16[128,768]{1,0:T(8,128)(2,1)S(1)} collective-permute-done((bf16[128,768]{1,0:T(8,128)(2,1)S(1)}, bf16[128,768]{1,0:T(8,128)(2,1)S(1)}, u32[]{:S(2)}, u32[]{:S(2)}) %collective-permute-start.10) | collective-permute-done | bytes 196640 | tf_op jit(solution)/shard_map/ppermute | solution.py:311
  130.3 1.4 collective-permute-done.9
  131.7 0.1 fusion.3
  131.9 0.8 fusion.6
  (6 shorter events, 0.1 us)
Async XLA Ops:
  7.2 52.1 %all-gather.2.cloned.1.call-start = ((), (), s32[]{:S(2)}) async-start(), calls=%async_computation.3 | async-start | bytes 4177920 | tf_op jit(solution)/shard_map/all_gather | solution.py:318
  8.9 10.1 %collective-permute-start.2 = (bf16[128,768]{1,0:T(8,128)(2,1)S(1)}, bf16[128,768]{1,0:T(8,128)(2,1)S(1)}, u32[]{:S(2)}, u32[]{:S(2)}) collective-permute-start(bf16[128,768]{1,0:T(8,128)(2,1)S(1)} %get-tuple-element.43), channel_id=1, source_target_pairs={{0,224},{32,0},{64,32},{96,64},{128,96},{160,128},{192,160},{224,1... | collective-permute-start | bytes 589832 | tf_op jit(solution)/shard_map/ppermute | solution.py:304
  14.8 7.6 %collective-permute-start.1 = (bf16[128,768]{1,0:T(8,128)(2,1)S(1)}, bf16[128,768]{1,0:T(8,128)(2,1)S(1)}, u32[]{:S(2)}, u32[]{:S(2)}) collective-permute-start(bf16[128,768]{1,0:T(8,128)(2,1)S(1)} %get-tuple-element.43), channel_id=1, source_target_pairs={{0,32},{32,64},{64,96},{96,128},{128,160},{160,192},{192,224},{224... | collective-permute-start | bytes 589832 | tf_op jit(solution)/shard_map/ppermute | solution.py:300
  14.8 8.2 %collective-permute-start = (bf16[128,768]{1,0:T(8,128)(2,1)S(1)}, bf16[128,768]{1,0:T(8,128)(2,1)S(1)}, u32[]{:S(2)}, u32[]{:S(2)}) collective-permute-start(bf16[128,768]{1,0:T(8,128)(2,1)S(1)} %get-tuple-element.43), channel_id=1, source_target_pairs={{0,16},{16,0},{1,17},{17,1},{2,18},{18,2},{3,19},{19,3},{4,20},{20... | collective-permute-start | bytes 589832 | tf_op jit(solution)/shard_map/ppermute | solution.py:296
  22.4 12.8 %copy-start.1 = (bf16[128,384]{1,0:T(8,128)(2,1)S(1)}, bf16[128,384]{1,0:T(8,128)(2,1)}, u32[]{:S(2)}) copy-start(bf16[128,384]{1,0:T(8,128)(2,1)} %query.3) | copy-start | bytes 294916
  22.4 12.8 %copy-start.3 = (s32[32,32]{1,0:T(8,128)S(1)}, s32[32,32]{1,0:T(8,128)}, u32[]{:S(2)}) copy-start(s32[32,32]{1,0:T(8,128)} %mask.1) | copy-start | bytes 12292
  22.4 9.8 %collective-permute-start.3 = (bf16[256,768]{1,0:T(8,128)(2,1)S(1)}, bf16[256,768]{1,0:T(8,128)(2,1)S(1)}, u32[]{:S(2)}, u32[]{:S(2)}) collective-permute-start(bf16[256,768]{1,0:T(8,128)(2,1)S(1)} %pad_maximum_fusion), channel_id=1, source_target_pairs={{0,16},{16,0},{1,17},{17,1},{2,18},{18,2},{3,19},{19,3},{4,20},{20... | collective-permute-start | bytes 1179656 | tf_op jit(solution)/shard_map/ppermute | solution.py:296
  32.2 2.9 %collective-permute-start.4 = (bf16[768,768]{1,0:T(8,128)(2,1)S(1)}, bf16[768,768]{1,0:T(8,128)(2,1)S(1)}, u32[]{:S(2)}, u32[]{:S(2)}) collective-permute-start(bf16[768,768]{1,0:T(8,128)(2,1)S(1)} %slice_dynamic-update-slice_fusion.near_a), channel_id=1, source_target_pairs={{0,8},{8,0},{1,9},{9,1},{2,10},{10,2},{3,11},{11,3},{4,12},{12,4},... | collective-permute-start | bytes 3538952 | tf_op jit(solution)/shard_map/ppermute | solution.py:296
  62.5 8.1 %collective-permute-start.5 = (bf16[128,1280]{1,0:T(8,128)(2,1)S(1)}, bf16[128,1280]{1,0:T(8,128)(2,1)S(1)}, u32[]{:S(2)}, u32[]{:S(2)}) collective-permute-start(bf16[128,1280]{1,0:T(8,128)(2,1)S(1)} %get-tuple-element.21), channel_id=1, source_target_pairs={{0,16},{16,0},{1,17},{17,1},{2,18},{18,2},{3,19},{19,3},{4,20},{20... | collective-permute-start | bytes 983048 | tf_op jit(solution)/shard_map/ppermute | solution.py:296
  64.0 6.6 %copy-start.2 = (bf16[128,1280]{1,0:T(8,128)(2,1)S(1)}, bf16[128,1280]{1,0:T(8,128)(2,1)}, u32[]{:S(2)}) copy-start(bf16[128,1280]{1,0:T(8,128)(2,1)} %cot.1) | copy-start | bytes 983044
  71.4 16.7 %collective-permute-start.6 = (bf16[2,128,1280]{2,1,0:T(8,128)(2,1)S(1)}, bf16[2,128,1280]{2,1,0:T(8,128)(2,1)S(1)}, u32[]{:S(2)}, u32[]{:S(2)}) collective-permute-start(bf16[2,128,1280]{2,1,0:T(8,128)(2,1)S(1)} %get-tuple-element.25), channel_id=1, source_target_pairs={{0,16},{16,0},{1,17},{17,1},{2,18},{18,2},{3,19},{19,3},{4,20},{20... | collective-permute-start | bytes 1966088 | tf_op jit(solution)/shard_map/ppermute | solution.py:296
  90.7 17.8 %copy-start = (bf16[3,128,1536]{2,1,0:T(8,128)(2,1)S(1)}, bf16[3,128,1536]{2,1,0:T(8,128)(2,1)}, u32[]{:S(2)}) copy-start(bf16[3,128,1536]{2,1,0:T(8,128)(2,1)} %get-tuple-element.29.probs) | copy-start | bytes 3538948
  111.3 2.8 %collective-permute-start.7 = (bf16[768,768]{1,0:T(8,128)(2,1)S(1)}, bf16[768,768]{1,0:T(8,128)(2,1)S(1)}, u32[]{:S(2)}, u32[]{:S(2)}) collective-permute-start(bf16[768,768]{1,0:T(8,128)(2,1)S(1)} %get-tuple-element.33), channel_id=1, source_target_pairs={{0,8},{8,0},{1,9},{9,1},{2,10},{10,2},{3,11},{11,3},{4,12},{12,4},... | collective-permute-start | bytes 3538952 | tf_op jit(solution)/shard_map/ppermute | solution.py:296
  114.5 8.9 %collective-permute-start.8 = (bf16[128,768]{1,0:T(8,128)(2,1)S(1)}, bf16[128,768]{1,0:T(8,128)(2,1)S(1)}, u32[]{:S(2)}, u32[]{:S(2)}) collective-permute-start(bf16[128,768]{1,0:T(8,128)(2,1)S(1)} %get-tuple-element.36), channel_id=1, source_target_pairs={{0,16},{16,0},{32,48},{48,32},{64,80},{80,64},{96,112},{112,96},{1... | collective-permute-start | bytes 589832 | tf_op jit(solution)/shard_map/ppermute | solution.py:311
  116.0 9.0 %collective-permute-start.12 = (bf16[128,768]{1,0:T(8,128)(2,1)S(1)}, bf16[128,768]{1,0:T(8,128)(2,1)S(1)}, u32[]{:S(2)}, u32[]{:S(2)}) collective-permute-start(bf16[128,768]{1,0:T(8,128)(2,1)S(1)} %get-tuple-element.37), channel_id=1, source_target_pairs={{0,32},{16,48},{32,64},{48,80},{64,96},{80,112},{96,128},{112,144}... | collective-permute-start | bytes 589832 | tf_op jit(solution)/shard_map/ppermute | solution.py:311
  118.3 7.8 %collective-permute-start.11 = (bf16[128,768]{1,0:T(8,128)(2,1)S(1)}, bf16[128,768]{1,0:T(8,128)(2,1)S(1)}, u32[]{:S(2)}, u32[]{:S(2)}) collective-permute-start(bf16[128,768]{1,0:T(8,128)(2,1)S(1)} %get-tuple-element.38), channel_id=1, source_target_pairs={{0,224},{16,240},{32,0},{48,16},{64,32},{80,48},{96,64},{112,80},{... | collective-permute-start | bytes 589832 | tf_op jit(solution)/shard_map/ppermute | solution.py:311
  119.3 11.1 %collective-permute-start.10 = (bf16[128,768]{1,0:T(8,128)(2,1)S(1)}, bf16[128,768]{1,0:T(8,128)(2,1)S(1)}, u32[]{:S(2)}, u32[]{:S(2)}) collective-permute-start(bf16[128,768]{1,0:T(8,128)(2,1)S(1)} %get-tuple-element.39), channel_id=1, source_target_pairs={{0,48},{16,32},{32,80},{48,64},{64,112},{80,96},{96,144},{112,128}... | collective-permute-start | bytes 589832 | tf_op jit(solution)/shard_map/ppermute | solution.py:311
  120.4 11.4 %collective-permute-start.9 = (bf16[128,768]{1,0:T(8,128)(2,1)S(1)}, bf16[128,768]{1,0:T(8,128)(2,1)S(1)}, u32[]{:S(2)}, u32[]{:S(2)}) collective-permute-start(bf16[128,768]{1,0:T(8,128)(2,1)S(1)} %get-tuple-element.40), channel_id=1, source_target_pairs={{0,240},{16,224},{32,16},{48,0},{64,48},{80,32},{96,80},{112,64},{... | collective-permute-start | bytes 589832 | tf_op jit(solution)/shard_map/ppermute | solution.py:311
Sparse Core Ops, SparseCore 0:
  9.8 44.7 all-gather.1

commit v6 on v5

--- a/solution.py
+++ b/solution.py
@@ -244,52 +244,58 @@
     )(place, act, pull, push, pair, sums, weight)
 
 
-def backward_kernel(query, near_a, near_b, attn, probs, partial, grad_query, grad_a, grad_b):
+def backward_kernel(side, query, near, attn, probs, *refs):
+    if side == 1:
+        partial, grad_query, result, kept = refs
+        parts = partial.shape[0] // 2
+        halves = []
+        for x in range(2):
+            total = partial[x * parts].astype(jnp.float32)
+            for i in range(1, parts):
+                total = total + partial[x * parts + i].astype(jnp.float32)
+            halves.append(total)
+        turned = jnp.concatenate(halves, axis=0)
+    else:
+        kept, before, grad_query, result = refs
     width = query.shape[1]
-    half = near_a.shape[0]
+    half = near.shape[0]
     scale = HD ** (-0.5)
-    parts = partial.shape[0] // 2
-    sides = []
-    for side in range(2):
-        total = partial[side * parts].astype(jnp.float32)
-        for i in range(1, parts):
-            total = total + partial[side * parts + i].astype(jnp.float32)
-        sides.append(total)
-    turned = jnp.concatenate(sides, axis=0)
     for head in range(width // HD):
         cols = slice(head * HD, (head + 1) * HD)
         vcols = slice(width + head * HD, width + (head + 1) * HD)
-        g = turned[cols].T.astype(jnp.bfloat16)
+        if side == 1:
+            g = turned[cols].T.astype(jnp.bfloat16)
+            kept[:, cols] = g
+        else:
+            g = kept[:, cols]
         delta = jnp.sum(g.astype(jnp.float32) * attn[:, cols].astype(jnp.float32), axis=1, keepdims=True)
-        q = query[:, cols]
-        out = None
-        for side, (near, result) in enumerate(((near_a, grad_a), (near_b, grad_b))):
-            p = probs[head, :, side * half : (side + 1) * half]
-            d = (p.astype(jnp.float32) * (dot(g, near[:, vcols], NT) - delta)).astype(jnp.bfloat16)
-            term = dot(d, near[:, cols])
-            out = term if out is None else out + term
-            result[:, cols] = (dot(d, q, TN) * scale).astype(jnp.bfloat16)
-            result[:, vcols] = dot(p, g, TN).astype(jnp.bfloat16)
-        grad_query[:, cols] = out * scale
-
-
-def backward(query, near_a, near_b, attn, probs, partial):
+        p = probs[head, :, side * half : (side + 1) * half]
+        d = (p.astype(jnp.float32) * (dot(g, near[:, vcols], NT) - delta)).astype(jnp.bfloat16)
+        result[:, cols] = (dot(d, query[:, cols], TN) * scale).astype(jnp.bfloat16)
+        result[:, vcols] = dot(p, g, TN).astype(jnp.bfloat16)
+        term = dot(d, near[:, cols]) * scale
+        grad_query[:, cols] = term if side == 1 else before[:, cols] + term
+
+
+def backward(side, query, near, attn, probs, *rest):
     rows, width = query.shape
     in_vmem = pl.BlockSpec(memory_space=VMEM)
-    return pl.pallas_call(
-        backward_kernel,
-        out_shape=(
-            jax.ShapeDtypeStruct((rows, width), jnp.float32),
-            jax.ShapeDtypeStruct(near_a.shape, jnp.bfloat16),
-            jax.ShapeDtypeStruct(near_b.shape, jnp.bfloat16),
-        ),
-        in_specs=[in_vmem] * 6,
-        out_specs=(in_vmem,) * 3,
+    shapes = [
+        jax.ShapeDtypeStruct((rows, width), jnp.float32),
+        jax.ShapeDtypeStruct(near.shape, jnp.bfloat16),
+    ]
+    if side == 1:
+        shapes.append(jax.ShapeDtypeStruct((rows, width), jnp.bfloat16))
+    return pl.pallas_call(
+        functools.partial(backward_kernel, side),
+        out_shape=tuple(shapes),
+        in_specs=[in_vmem] * (4 + len(rest)),
+        out_specs=(in_vmem,) * len(shapes),
         compiler_params=pltpu.CompilerParams(vmem_limit_bytes=16 << 20),
         cost_estimate=pl.CostEstimate(
-            flops=8 * rows * 2 * near_a.shape[0] * width, bytes_accessed=8 << 20, transcendentals=0
-        ),
-    )(query, near_a, near_b, attn, probs, partial)
+            flops=8 * rows * near.shape[0] * width, bytes_accessed=4 << 20, transcendentals=0
+        ),
+    )(query, near, attn, probs, *rest)
 
 
 def swap(value, axis):
@@ -334,15 +340,18 @@
     sums = lax.all_to_all(sums, SEQ, 0, 0)
     back, scaled = down(place, act, pull, push, pair, sums, held)
     partial = lax.all_to_all(back, WIDE, 0, 0)
-    grad_query, grad_a, grad_b = backward(query, near_a, near_b, attn, probs, partial)
-    both = grad_a.astype(f32) + swap(grad_b, "core").astype(f32)
-    blocks = [both[i * rows : (i + 1) * rows] for i in range(6)]
-    moves = ((1, 0, 1), (3, -1, 1), (5, 1, 1), (2, -1, 0), (4, 1, 0))
+    grad_query, grad_b, grad = backward(1, query, near_b, attn, probs, partial)
+    grad_b = swap(grad_b, "core")
+    grad_query, grad_a = backward(0, query, near_a, attn, probs, grad, grad_query)
+    blocks = [
+        grad_a[i * rows : (i + 1) * rows].astype(f32) + grad_b[i * rows : (i + 1) * rows].astype(f32) for i in range(6)
+    ]
+    moves = ((3, -1, 1), (5, 1, 1), (2, -1, 0), (4, 1, 0), (1, 0, 1))
     arrived = [shifted(blocks[i].astype(bf16), planes, xl) for i, planes, xl in moves]
-    grad_own = blocks[0]
-    for block in arrived:
-        grad_own = grad_own + block.astype(f32)
-    return scaled, grad_query, grad_own[:, :width], grad_own[:, width:]
+    terms = [blocks[0]] + [block.astype(f32) for block in arrived]
+    grad_key = functools.reduce(jnp.add, [term[:, :width] for term in terms])
+    grad_value = functools.reduce(jnp.add, [term[:, width:] for term in terms])
+    return scaled, grad_query, grad_key, grad_value
 
 
 def solution(mesh):

time: 140 us -> 139 us (level)
  waiting for transfers between devices: 36.1 us -> 34 us
    ppermute x6, waiting for transfers between devices: 20 us -> 18.1 us  [swap(): return lax.ppermute(value, axis, [(0, 1), (1, 0)])]
    pallas_call x1 -> x2, Pallas kernels: 2.71 us -> 3.17 us  [backward(): pl.pallas_call(functools.partial(backward_kernel, side), out_shape=tuple(...]
  transfers between devices with their start and end apart: 14 -> 14, of which waited for: 10 -> 10; matrix products, arithmetic and copies ran while one was open for 1% -> 1% of each run, Pallas kernels for 3% -> 5%
where the time goes in v6:
time: 139 us; the launch traced here: 138 us
  blocking collectives  53.6 us (39%)
  waiting for transfers between devices  34 us (24%)
  starting transfers between devices  19.6 us (14%)
  Pallas kernels  14.4 us (10%)
  between operations  14.2 us (10%)
  other arithmetic  2.41 us (2%)
    all_to_all x1, blocking collectives, body(): lax.all_to_all(attn_out.reshape(sides * copies, depth, rows), WIDE, 0, 0)  20.6 us
    ppermute x6, waiting for transfers between devices, swap(): return lax.ppermute(value, axis, [(0, 1), (1, 0)])  18.1 us
    all_to_all x1, blocking collectives, body(): partial = lax.all_to_all(back, WIDE, 0, 0)  17.8 us
    all_to_all x1, blocking collectives, body(): sums = lax.all_to_all(sums, SEQ, 0, 0)  15.1 us
    ppermute x5, starting transfers between devices, shifted(): return lax.ppermute(value, ('z', 'xl'), pairs)  8.91 us
    ppermute x5, waiting for transfers between devices, shifted(): return lax.ppermute(value, ('z', 'xl'), pairs)  8.21 us
    ppermute x1, starting transfers between devices, down_plane(): lax.ppermute(value, 'z', [(i, (i - 1) % PLANES) for i in range(PLANES)])  5.93 us
    ppermute x6, starting transfers between devices, swap(): return lax.ppermute(value, axis, [(0, 1), (1, 0)])  4.68 us
  transfers between devices with their start and end apart: 14, of which 10 were waited for; matrix products, arithmetic and copies ran while one was open for 1% of the time, Pallas kernels for 5%

profile of v6, /device:TPU:2, one launch (start us, length us, event | category | flops | bytes accessed | tf_op | source)
XLA Modules:
  0.0 138.3 jit_solution(15589004285166226841)
XLA Ops:
  7.2 0.0 all-gather.2.cloned.1.call-start
  7.2 0.7 all-gather.2.cloned.1.call-update
  7.9 1.0 pad_add_fusion
  8.9 5.9 %collective-permute-start.2 = (bf16[128,768]{1,0:T(8,128)(2,1)S(1)}, bf16[128,768]{1,0:T(8,128)(2,1)S(1)}, u32[]{:S(2)}, u32[]{:S(2)}) collective-permute-start(bf16[128,768]{1,0:T(8,128)(2,1)S(1)} %get-tuple-element.46), channel_id=1, source_target_pairs={{0,224},{32,0},{64,32},{96,64},{128,96},{160,128},{192,160},{224,1... | collective-permute-start | bytes 589832 | tf_op jit(solution)/shard_map/ppermute | solution.py:310
  14.8 0.0 collective-permute-start.1
  14.8 0.5 collective-permute-start
  15.3 3.6 %collective-permute-done.2 = bf16[128,768]{1,0:T(8,128)(2,1)S(1)} collective-permute-done((bf16[128,768]{1,0:T(8,128)(2,1)S(1)}, bf16[128,768]{1,0:T(8,128)(2,1)S(1)}, u32[]{:S(2)}, u32[]{:S(2)}) %collective-permute-start.2) | collective-permute-done | bytes 196640 | tf_op jit(solution)/shard_map/ppermute | solution.py:310
  19.0 3.4 %collective-permute-done.1 = bf16[128,768]{1,0:T(8,128)(2,1)S(1)} collective-permute-done((bf16[128,768]{1,0:T(8,128)(2,1)S(1)}, bf16[128,768]{1,0:T(8,128)(2,1)S(1)}, u32[]{:S(2)}, u32[]{:S(2)}) %collective-permute-start.1) | collective-permute-done | bytes 196640 | tf_op jit(solution)/shard_map/ppermute | solution.py:306
  22.4 0.0 copy-start.1
  22.4 0.0 copy-start.3
  22.4 0.6 collective-permute-start.3
  23.1 0.0 collective-permute-done
  23.1 9.1 %collective-permute-done.3 = bf16[256,768]{1,0:T(8,128)(2,1)S(1)} collective-permute-done((bf16[256,768]{1,0:T(8,128)(2,1)S(1)}, bf16[256,768]{1,0:T(8,128)(2,1)S(1)}, u32[]{:S(2)}, u32[]{:S(2)}) %collective-permute-start.3) | collective-permute-done | bytes 393248 | tf_op jit(solution)/shard_map/ppermute | solution.py:302
  32.2 0.1 collective-permute-start.4
  32.4 0.1 pad_add_fusion.1.place
  32.4 2.8 %collective-permute-done.4.near_b.near = bf16[768,768]{1,0:T(8,128)(2,1)S(1)} collective-permute-done((bf16[768,768]{1,0:T(8,128)(2,1)S(1)}, bf16[768,768]{1,0:T(8,128)(2,1)S(1)}, u32[]{:S(2)}, u32[]{:S(2)}) %collective-permute-start.4) | collective-permute-done | bytes 1179680 | tf_op jit(solution)/shard_map/ppermute | solution.py:302
  35.2 0.0 copy-done.1
  35.2 0.0 copy-done.3
  35.2 3.4 %shard_map.93 = (bf16[2,8,192,128]{3,2,1,0:T(8,128)(2,1)S(1)}, bf16[128,384]{1,0:T(8,128)(2,1)S(1)}, bf16[3,128,1536]{2,1,0:T(8,128)(2,1)}) custom-call(s32[3]{0:T(128)S(1)} %pad_add_fusion.1.place, s32[32,32]{1,0:T(8,128)S(1)} %copy-done.3, bf16[128,384]{1,0:T(8,128)(2,1)S(1)} %copy-done.1, bf16[768,768]{1,0:T(8,128)(2,1)S(1)} %slice_dynamic-update-slice_fusion.near_a.near, ...), custom_call_target="tpu_custom_call" | custom-call | flops 301989888 | bytes 8388608 | tf_op jit(solution)/shard_map/pallas_call | solution.py:87
  38.6 20.6 %all_to_all.15.rows_in = bf16[16,192,128]{2,1,0:T(8,128)(2,1)S(1)} all-to-all(bf16[16,192,128]{2,1,0:T(8,128)(2,1)S(1)} %bitcast.5), channel_id=1, replica_groups=mesh['z'=8,'xl'=2,'core'=2,'y'=4,'xh'=2] {'xl','y','xh'}, dimensions={0} | all-to-all | bytes 1572864 | tf_op jit(solution)/shard_map/all_to_all | solution.py:334
  59.3 0.0 all-gather.2.cloned.1.call-done
  59.3 3.2 %shard_map.94 = (bf16[128,1280]{1,0:T(8,128)(2,1)S(1)}, bf16[8,192,1280]{2,1,0:T(8,128)(2,1)S(1)}) custom-call(s32[3]{0:T(128)S(1)} %pad_add_fusion.1.place, bf16[16,192,128]{2,1,0:T(8,128)(2,1)S(1)} %all_to_all.15.rows_in, bf16[8,192,1280]{2,1,0:T(8,128)(2,1)} %bitcast.6), custom_call_target="tpu_custom_call" | custom-call | flops 503316480 | bytes 3932160 | tf_op jit(solution)/shard_map/pallas_call | solution.py:125
  62.5 1.5 %collective-permute-start.5 = (bf16[128,1280]{1,0:T(8,128)(2,1)S(1)}, bf16[128,1280]{1,0:T(8,128)(2,1)S(1)}, u32[]{:S(2)}, u32[]{:S(2)}) collective-permute-start(bf16[128,1280]{1,0:T(8,128)(2,1)S(1)} %get-tuple-element.23), channel_id=1, source_target_pairs={{0,16},{16,0},{1,17},{17,1},{2,18},{18,2},{3,19},{19,3},{4,20},{20... | collective-permute-start | bytes 983048 | tf_op jit(solution)/shard_map/ppermute | solution.py:302
  64.0 0.0 copy-start.2
  64.0 1.3 shard_map.95.mine
  65.3 5.3 %collective-permute-done.5.got = bf16[128,1280]{1,0:T(8,128)(2,1)S(1)} collective-permute-done((bf16[128,1280]{1,0:T(8,128)(2,1)S(1)}, bf16[128,1280]{1,0:T(8,128)(2,1)S(1)}, u32[]{:S(2)}, u32[]{:S(2)}) %collective-permute-start.5) | collective-permute-done | bytes 327712 | tf_op jit(solution)/shard_map/ppermute | solution.py:302
  70.6 0.0 copy-done.2
  70.6 0.7 shard_map.96
  71.4 1.6 %collective-permute-start.6 = (bf16[2,128,1280]{2,1,0:T(8,128)(2,1)S(1)}, bf16[2,128,1280]{2,1,0:T(8,128)(2,1)S(1)}, u32[]{:S(2)}, u32[]{:S(2)}) collective-permute-start(bf16[2,128,1280]{2,1,0:T(8,128)(2,1)S(1)} %get-tuple-element.27), channel_id=1, source_target_pairs={{0,16},{16,0},{1,17},{17,1},{2,18},{18,2},{3,19},{19,3},{4,20},{20... | collective-permute-start | bytes 1966088 | tf_op jit(solution)/shard_map/ppermute | solution.py:302
  73.0 15.1 %all_to_all.16.sums = bf16[32,24,128]{2,1,0:T(8,128)(2,1)S(1)} all-to-all(bf16[32,24,128]{2,1,0:T(8,128)(2,1)S(1)} %get-tuple-element.28), channel_id=1, replica_groups=mesh['z'=8,'xl'=2,'core'=2,'y'=4,'xh'=2] {'z','xl','core'}, dimensions={0} | all-to-all | bytes 393216 | tf_op jit(solution)/shard_map/all_to_all | solution.py:340
  88.1 0.0 collective-permute-done.6.pair
  88.1 2.6 %shard_map.97 = (bf16[16,192,128]{2,1,0:T(8,128)(2,1)S(1)}, bf16[128,1280]{1,0:T(8,128)(2,1)}) custom-call(s32[3]{0:T(128)S(1)} %pad_add_fusion.1.place, f32[128,1280]{1,0:T(8,128)S(1)} %get-tuple-element.24.act, f32[128,1280]{1,0:T(8,128)S(1)} %get-tuple-element.25.pull, f32[128,1280]{1,0:T(8,128)S(1)} %get-tuple-element.26.push, ...), custom_call_target="tpu_custom_call" | custom-call | flops 1006632960 | bytes 3932160 | tf_op jit(solution)/shard_map/pallas_call | solution.py:231
  90.7 0.0 copy-start
  90.7 17.8 %all_to_all.17.refs_0_ = bf16[16,192,128]{2,1,0:T(8,128)(2,1)S(1)} all-to-all(bf16[16,192,128]{2,1,0:T(8,128)(2,1)S(1)} %get-tuple-element.32), channel_id=1, replica_groups=mesh['z'=8,'xl'=2,'core'=2,'y'=4,'xh'=2] {'xl','y','xh'}, dimensions={0} | all-to-all | bytes 1572864 | tf_op jit(solution)/shard_map/all_to_all | solution.py:342
  108.6 0.0 copy-done
  108.6 1.3 shard_map.98
  109.8 0.3 collective-permute-start.7
  110.1 1.9 %shard_map.99 = (f32[128,384]{1,0:T(8,128)}, bf16[768,768]{1,0:T(8,128)(2,1)S(1)}) custom-call(bf16[128,384]{1,0:T(8,128)(2,1)S(1)} %copy-done.1, bf16[768,768]{1,0:T(8,128)(2,1)S(1)} %slice_dynamic-update-slice_fusion.near_a.near, bf16[128,384]{1,0:T(8,128)(2,1)S(1)} %get-tuple-element.30.attn, bf16[3,128,1536]{2,1,0:T(8,128)(2,1)S(1)} %copy-done, ...), custom_call_target="tpu_custom_call" | custom-call | flops 301989888 | bytes 4194304 | tf_op jit(solution)/shard_map/pallas_call | solution.py:289
  112.0 0.9 collective-permute-done.7
  112.9 0.3 convert_add_fusion
  113.2 1.5 %collective-permute-start.12 = (bf16[128,768]{1,0:T(8,128)(2,1)S(1)}, bf16[128,768]{1,0:T(8,128)(2,1)S(1)}, u32[]{:S(2)}, u32[]{:S(2)}) collective-permute-start(bf16[128,768]{1,0:T(8,128)(2,1)S(1)} %get-tuple-element.41), channel_id=1, source_target_pairs={{0,16},{16,0},{32,48},{48,32},{64,80},{80,64},{96,112},{112,96},{1... | collective-permute-start | bytes 589832 | tf_op jit(solution)/shard_map/ppermute | solution.py:317
  114.8 2.3 %collective-permute-start.11 = (bf16[128,768]{1,0:T(8,128)(2,1)S(1)}, bf16[128,768]{1,0:T(8,128)(2,1)S(1)}, u32[]{:S(2)}, u32[]{:S(2)}) collective-permute-start(bf16[128,768]{1,0:T(8,128)(2,1)S(1)} %get-tuple-element.42), channel_id=1, source_target_pairs={{0,32},{16,48},{32,64},{48,80},{64,96},{80,112},{96,128},{112,144}... | collective-permute-start | bytes 589832 | tf_op jit(solution)/shard_map/ppermute | solution.py:317
  117.1 0.9 collective-permute-start.10
  118.0 1.1 collective-permute-start.9
  119.1 3.0 %collective-permute-start.8 = (bf16[128,768]{1,0:T(8,128)(2,1)S(1)}, bf16[128,768]{1,0:T(8,128)(2,1)S(1)}, u32[]{:S(2)}, u32[]{:S(2)}) collective-permute-start(bf16[128,768]{1,0:T(8,128)(2,1)S(1)} %get-tuple-element.45), channel_id=1, source_target_pairs={{0,240},{16,224},{32,16},{48,0},{64,48},{80,32},{96,80},{112,64},{... | collective-permute-start | bytes 589832 | tf_op jit(solution)/shard_map/ppermute | solution.py:317
  122.1 0.0 collective-permute-done.12
  122.2 1.6 %collective-permute-done.11 = bf16[128,768]{1,0:T(8,128)(2,1)S(1)} collective-permute-done((bf16[128,768]{1,0:T(8,128)(2,1)S(1)}, bf16[128,768]{1,0:T(8,128)(2,1)S(1)}, u32[]{:S(2)}, u32[]{:S(2)}) %collective-permute-start.11) | collective-permute-done | bytes 196640 | tf_op jit(solution)/shard_map/ppermute | solution.py:317
  123.8 1.1 collective-permute-done.10
  124.9 4.1 %collective-permute-done.9 = bf16[128,768]{1,0:T(8,128)(2,1)S(1)} collective-permute-done((bf16[128,768]{1,0:T(8,128)(2,1)S(1)}, bf16[128,768]{1,0:T(8,128)(2,1)S(1)}, u32[]{:S(2)}, u32[]{:S(2)}) %collective-permute-start.9) | collective-permute-done | bytes 196640 | tf_op jit(solution)/shard_map/ppermute | solution.py:317
  129.1 1.4 collective-permute-done.8
  130.5 0.9 slice_add_fusion
  (11 shorter events, 0.2 us)
Async XLA Ops:
  7.2 52.1 %all-gather.2.cloned.1.call-start = ((), (), s32[]{:S(2)}) async-start(), calls=%async_computation.3 | async-start | bytes 4177920 | tf_op jit(solution)/shard_map/all_gather | solution.py:324
  8.9 10.1 %collective-permute-start.2 = (bf16[128,768]{1,0:T(8,128)(2,1)S(1)}, bf16[128,768]{1,0:T(8,128)(2,1)S(1)}, u32[]{:S(2)}, u32[]{:S(2)}) collective-permute-start(bf16[128,768]{1,0:T(8,128)(2,1)S(1)} %get-tuple-element.46), channel_id=1, source_target_pairs={{0,224},{32,0},{64,32},{96,64},{128,96},{160,128},{192,160},{224,1... | collective-permute-start | bytes 589832 | tf_op jit(solution)/shard_map/ppermute | solution.py:310
  14.8 7.6 %collective-permute-start.1 = (bf16[128,768]{1,0:T(8,128)(2,1)S(1)}, bf16[128,768]{1,0:T(8,128)(2,1)S(1)}, u32[]{:S(2)}, u32[]{:S(2)}) collective-permute-start(bf16[128,768]{1,0:T(8,128)(2,1)S(1)} %get-tuple-element.46), channel_id=1, source_target_pairs={{0,32},{32,64},{64,96},{96,128},{128,160},{160,192},{192,224},{224... | collective-permute-start | bytes 589832 | tf_op jit(solution)/shard_map/ppermute | solution.py:306
  14.8 8.2 %collective-permute-start = (bf16[128,768]{1,0:T(8,128)(2,1)S(1)}, bf16[128,768]{1,0:T(8,128)(2,1)S(1)}, u32[]{:S(2)}, u32[]{:S(2)}) collective-permute-start(bf16[128,768]{1,0:T(8,128)(2,1)S(1)} %get-tuple-element.46), channel_id=1, source_target_pairs={{0,16},{16,0},{1,17},{17,1},{2,18},{18,2},{3,19},{19,3},{4,20},{20... | collective-permute-start | bytes 589832 | tf_op jit(solution)/shard_map/ppermute | solution.py:302
  22.4 12.8 %copy-start.1 = (bf16[128,384]{1,0:T(8,128)(2,1)S(1)}, bf16[128,384]{1,0:T(8,128)(2,1)}, u32[]{:S(2)}) copy-start(bf16[128,384]{1,0:T(8,128)(2,1)} %query.5) | copy-start | bytes 294916
  22.4 12.8 %copy-start.3 = (s32[32,32]{1,0:T(8,128)S(1)}, s32[32,32]{1,0:T(8,128)}, u32[]{:S(2)}) copy-start(s32[32,32]{1,0:T(8,128)} %mask.1) | copy-start | bytes 12292
  22.4 9.8 %collective-permute-start.3 = (bf16[256,768]{1,0:T(8,128)(2,1)S(1)}, bf16[256,768]{1,0:T(8,128)(2,1)S(1)}, u32[]{:S(2)}, u32[]{:S(2)}) collective-permute-start(bf16[256,768]{1,0:T(8,128)(2,1)S(1)} %pad_maximum_fusion), channel_id=1, source_target_pairs={{0,16},{16,0},{1,17},{17,1},{2,18},{18,2},{3,19},{19,3},{4,20},{20... | collective-permute-start | bytes 1179656 | tf_op jit(solution)/shard_map/ppermute | solution.py:302
  32.2 2.9 %collective-permute-start.4 = (bf16[768,768]{1,0:T(8,128)(2,1)S(1)}, bf16[768,768]{1,0:T(8,128)(2,1)S(1)}, u32[]{:S(2)}, u32[]{:S(2)}) collective-permute-start(bf16[768,768]{1,0:T(8,128)(2,1)S(1)} %slice_dynamic-update-slice_fusion.near_a.near), channel_id=1, source_target_pairs={{0,8},{8,0},{1,9},{9,1},{2,10},{10,2},{3,11},{11,3},{4,12},{12,4},... | collective-permute-start | bytes 3538952 | tf_op jit(solution)/shard_map/ppermute | solution.py:302
  62.5 8.1 %collective-permute-start.5 = (bf16[128,1280]{1,0:T(8,128)(2,1)S(1)}, bf16[128,1280]{1,0:T(8,128)(2,1)S(1)}, u32[]{:S(2)}, u32[]{:S(2)}) collective-permute-start(bf16[128,1280]{1,0:T(8,128)(2,1)S(1)} %get-tuple-element.23), channel_id=1, source_target_pairs={{0,16},{16,0},{1,17},{17,1},{2,18},{18,2},{3,19},{19,3},{4,20},{20... | collective-permute-start | bytes 983048 | tf_op jit(solution)/shard_map/ppermute | solution.py:302
  64.0 6.6 %copy-start.2 = (bf16[128,1280]{1,0:T(8,128)(2,1)S(1)}, bf16[128,1280]{1,0:T(8,128)(2,1)}, u32[]{:S(2)}) copy-start(bf16[128,1280]{1,0:T(8,128)(2,1)} %cot.1) | copy-start | bytes 983044
  71.4 16.7 %collective-permute-start.6 = (bf16[2,128,1280]{2,1,0:T(8,128)(2,1)S(1)}, bf16[2,128,1280]{2,1,0:T(8,128)(2,1)S(1)}, u32[]{:S(2)}, u32[]{:S(2)}) collective-permute-start(bf16[2,128,1280]{2,1,0:T(8,128)(2,1)S(1)} %get-tuple-element.27), channel_id=1, source_target_pairs={{0,16},{16,0},{1,17},{17,1},{2,18},{18,2},{3,19},{19,3},{4,20},{20... | collective-permute-start | bytes 1966088 | tf_op jit(solution)/shard_map/ppermute | solution.py:302
  90.7 17.8 %copy-start = (bf16[3,128,1536]{2,1,0:T(8,128)(2,1)S(1)}, bf16[3,128,1536]{2,1,0:T(8,128)(2,1)}, u32[]{:S(2)}) copy-start(bf16[3,128,1536]{2,1,0:T(8,128)(2,1)} %get-tuple-element.31.probs) | copy-start | bytes 3538948
  109.8 3.1 %collective-permute-start.7 = (bf16[768,768]{1,0:T(8,128)(2,1)S(1)}, bf16[768,768]{1,0:T(8,128)(2,1)S(1)}, u32[]{:S(2)}, u32[]{:S(2)}) collective-permute-start(bf16[768,768]{1,0:T(8,128)(2,1)S(1)} %get-tuple-element.37), channel_id=1, source_target_pairs={{0,8},{8,0},{1,9},{9,1},{2,10},{10,2},{3,11},{11,3},{4,12},{12,4},... | collective-permute-start | bytes 3538952 | tf_op jit(solution)/shard_map/ppermute | solution.py:302
  113.2 8.9 %collective-permute-start.12 = (bf16[128,768]{1,0:T(8,128)(2,1)S(1)}, bf16[128,768]{1,0:T(8,128)(2,1)S(1)}, u32[]{:S(2)}, u32[]{:S(2)}) collective-permute-start(bf16[128,768]{1,0:T(8,128)(2,1)S(1)} %get-tuple-element.41), channel_id=1, source_target_pairs={{0,16},{16,0},{32,48},{48,32},{64,80},{80,64},{96,112},{112,96},{1... | collective-permute-start | bytes 589832 | tf_op jit(solution)/shard_map/ppermute | solution.py:317
  114.8 9.0 %collective-permute-start.11 = (bf16[128,768]{1,0:T(8,128)(2,1)S(1)}, bf16[128,768]{1,0:T(8,128)(2,1)S(1)}, u32[]{:S(2)}, u32[]{:S(2)}) collective-permute-start(bf16[128,768]{1,0:T(8,128)(2,1)S(1)} %get-tuple-element.42), channel_id=1, source_target_pairs={{0,32},{16,48},{32,64},{48,80},{64,96},{80,112},{96,128},{112,144}... | collective-permute-start | bytes 589832 | tf_op jit(solution)/shard_map/ppermute | solution.py:317
  117.1 7.8 %collective-permute-start.10 = (bf16[128,768]{1,0:T(8,128)(2,1)S(1)}, bf16[128,768]{1,0:T(8,128)(2,1)S(1)}, u32[]{:S(2)}, u32[]{:S(2)}) collective-permute-start(bf16[128,768]{1,0:T(8,128)(2,1)S(1)} %get-tuple-element.43), channel_id=1, source_target_pairs={{0,224},{16,240},{32,0},{48,16},{64,32},{80,48},{96,64},{112,80},{... | collective-permute-start | bytes 589832 | tf_op jit(solution)/shard_map/ppermute | solution.py:317
  118.0 11.1 %collective-permute-start.9 = (bf16[128,768]{1,0:T(8,128)(2,1)S(1)}, bf16[128,768]{1,0:T(8,128)(2,1)S(1)}, u32[]{:S(2)}, u32[]{:S(2)}) collective-permute-start(bf16[128,768]{1,0:T(8,128)(2,1)S(1)} %get-tuple-element.44), channel_id=1, source_target_pairs={{0,48},{16,32},{32,80},{48,64},{64,112},{80,96},{96,144},{112,128}... | collective-permute-start | bytes 589832 | tf_op jit(solution)/shard_map/ppermute | solution.py:317
  119.1 11.4 %collective-permute-start.8 = (bf16[128,768]{1,0:T(8,128)(2,1)S(1)}, bf16[128,768]{1,0:T(8,128)(2,1)S(1)}, u32[]{:S(2)}, u32[]{:S(2)}) collective-permute-start(bf16[128,768]{1,0:T(8,128)(2,1)S(1)} %get-tuple-element.45), channel_id=1, source_target_pairs={{0,240},{16,224},{32,16},{48,0},{64,48},{80,32},{96,80},{112,64},{... | collective-permute-start | bytes 589832 | tf_op jit(solution)/shard_map/ppermute | solution.py:317
Sparse Core Ops, SparseCore 0:
  9.8 44.7 all-gather.1

commit v7 on v6

--- a/solution.py
+++ b/solution.py
@@ -203,8 +203,8 @@
     )(mine, got, cot)
 
 
-def down_kernel(place, act, pull, push, pair, sums, weight, out, scaled, grad):
-    rows, width = act.shape
+def down_kernel(place, pull, push, pair, sums, weight, out, scales, grad):
+    rows, width = pull.shape
     chunks = width // 128
     own = place[1]
     total = jnp.sum(sums[...].astype(jnp.float32), axis=0)
@@ -212,7 +212,7 @@
         cols = slice(r * 128, (r + 1) * 128)
         inv = lax.rsqrt(total[r : r + 1, :] * (1.0 / TOKENS) + EPSILON)
         back = total[chunks + r : chunks + r + 1, :] * -0.5 * inv * inv * inv * (2.0 / TOKENS)
-        scaled[:, cols] = (act[:, cols] * inv).astype(jnp.bfloat16)
+        scales[r : r + 1, :] = inv
         grad[:rows, cols] = (pull[:, cols] * inv + back * push[:, cols]).astype(jnp.bfloat16)
         far = pair[0, :, cols].astype(jnp.float32) * inv + back * pair[1, :, cols].astype(jnp.float32)
         grad[rows:, cols] = far.astype(jnp.bfloat16)
@@ -224,24 +224,42 @@
         out[pl.ds((1 - own) * parts + first, group)] = term[:, rows:].reshape(group, depth, rows)
 
 
-def down(place, act, pull, push, pair, sums, weight):
-    rows, width = act.shape
+def down(place, pull, push, pair, sums, weight):
+    rows, width = pull.shape
     parts, depth, _ = weight.shape
     in_vmem = pl.BlockSpec(memory_space=VMEM)
     return pl.pallas_call(
         down_kernel,
         out_shape=(
             jax.ShapeDtypeStruct((2 * parts, depth, rows), jnp.bfloat16),
-            jax.ShapeDtypeStruct((rows, width), jnp.bfloat16),
-        ),
-        in_specs=[pl.BlockSpec(memory_space=SMEM)] + [in_vmem] * 6,
+            jax.ShapeDtypeStruct((-(-(width // 128) // 8) * 8, 128), jnp.float32),
+        ),
+        in_specs=[pl.BlockSpec(memory_space=SMEM)] + [in_vmem] * 5,
         out_specs=(in_vmem,) * 2,
         scratch_shapes=[pltpu.VMEM((2 * rows, width), jnp.bfloat16)],
         compiler_params=pltpu.CompilerParams(vmem_limit_bytes=16 << 20),
         cost_estimate=pl.CostEstimate(
             flops=4 * rows * width * parts * depth, bytes_accessed=weight.size * 2, transcendentals=0
         ),
-    )(place, act, pull, push, pair, sums, weight)
+    )(place, pull, push, pair, sums, weight)
+
+
+def scale_kernel(act, scales, scaled):
+    for r in range(act.shape[1] // 128):
+        cols = slice(r * 128, (r + 1) * 128)
+        scaled[:, cols] = (act[:, cols] * scales[r : r + 1, :]).astype(jnp.bfloat16)
+
+
+def scale(act, scales):
+    in_vmem = pl.BlockSpec(memory_space=VMEM)
+    return pl.pallas_call(
+        scale_kernel,
+        out_shape=jax.ShapeDtypeStruct(act.shape, jnp.bfloat16),
+        in_specs=[in_vmem] * 2,
+        out_specs=in_vmem,
+        compiler_params=pltpu.CompilerParams(vmem_limit_bytes=16 << 20),
+        cost_estimate=pl.CostEstimate(flops=act.size, bytes_accessed=6 * act.size, transcendentals=0),
+    )(act, scales)
 
 
 def backward_kernel(side, query, near, attn, probs, *refs):
@@ -338,7 +356,8 @@
     act, pull, push, pair, sums = middle(mine, got, cot, lax.axis_size(SEQ))
     pair = swap(pair, "xl")
     sums = lax.all_to_all(sums, SEQ, 0, 0)
-    back, scaled = down(place, act, pull, push, pair, sums, held)
+    back, scales = down(place, pull, push, pair, sums, held)
+    scaled = scale(act, scales)
     partial = lax.all_to_all(back, WIDE, 0, 0)
     grad_query, grad_b, grad = backward(1, query, near_b, attn, probs, partial)
     grad_b = swap(grad_b, "core")

time: 139 us -> 138 us (level)
  no operation moved by 1% of the time
where the time goes in v7:
time: 138 us
  blocking collectives  53.6 us (39%)
  waiting for transfers between devices  33.2 us (24%)
  starting transfers between devices  19.6 us (14%)
  Pallas kernels  14.5 us (11%)
  between operations  14.2 us (10%)
  other arithmetic  2.41 us (2%)
    all_to_all x1, blocking collectives, body(): lax.all_to_all(attn_out.reshape(sides * copies, depth, rows), WIDE, 0, 0)  20.6 us
    ppermute x6, waiting for transfers between devices, swap(): return lax.ppermute(value, axis, [(0, 1), (1, 0)])  18.1 us
    all_to_all x1, blocking collectives, body(): partial = lax.all_to_all(back, WIDE, 0, 0)  17.8 us
    all_to_all x1, blocking collectives, body(): sums = lax.all_to_all(sums, SEQ, 0, 0)  15.1 us
    ppermute x5, starting transfers between devices, shifted(): return lax.ppermute(value, ('z', 'xl'), pairs)  8.92 us
    ppermute x5, waiting for transfers between devices, shifted(): return lax.ppermute(value, ('z', 'xl'), pairs)  7.43 us
    ppermute x1, starting transfers between devices, down_plane(): lax.ppermute(value, 'z', [(i, (i - 1) % PLANES) for i in range(PLANES)])  5.93 us
    ppermute x6, starting transfers between devices, swap(): return lax.ppermute(value, axis, [(0, 1), (1, 0)])  4.68 us
  transfers between devices with their start and end apart: 14, of which 10 were waited for; matrix products, arithmetic and copies ran while one was open for 1% of the time, Pallas kernels for 5%

profile of v7, /device:TPU:2, one launch (start us, length us, event | category | flops | bytes accessed | tf_op | source)
XLA Modules:
  0.0 137.6 jit_solution(2370499426541764552)
XLA Ops:
  7.2 0.0 all-gather.2.cloned.1.call-start
  7.2 0.7 all-gather.2.cloned.1.call-update
  7.9 1.0 pad_add_fusion
  8.9 5.9 %collective-permute-start.2 = (bf16[128,768]{1,0:T(8,128)(2,1)S(1)}, bf16[128,768]{1,0:T(8,128)(2,1)S(1)}, u32[]{:S(2)}, u32[]{:S(2)}) collective-permute-start(bf16[128,768]{1,0:T(8,128)(2,1)S(1)} %get-tuple-element.46), channel_id=1, source_target_pairs={{0,224},{32,0},{64,32},{96,64},{128,96},{160,128},{192,160},{224,1... | collective-permute-start | bytes 589832 | tf_op jit(solution)/shard_map/ppermute | solution.py:328
  14.8 0.0 collective-permute-start.1
  14.8 0.5 collective-permute-start
  15.3 3.6 %collective-permute-done.2 = bf16[128,768]{1,0:T(8,128)(2,1)S(1)} collective-permute-done((bf16[128,768]{1,0:T(8,128)(2,1)S(1)}, bf16[128,768]{1,0:T(8,128)(2,1)S(1)}, u32[]{:S(2)}, u32[]{:S(2)}) %collective-permute-start.2) | collective-permute-done | bytes 196640 | tf_op jit(solution)/shard_map/ppermute | solution.py:328
  19.0 3.4 %collective-permute-done.1 = bf16[128,768]{1,0:T(8,128)(2,1)S(1)} collective-permute-done((bf16[128,768]{1,0:T(8,128)(2,1)S(1)}, bf16[128,768]{1,0:T(8,128)(2,1)S(1)}, u32[]{:S(2)}, u32[]{:S(2)}) %collective-permute-start.1) | collective-permute-done | bytes 196640 | tf_op jit(solution)/shard_map/ppermute | solution.py:324
  22.4 0.0 copy-start.1
  22.4 0.0 copy-start.3
  22.4 0.6 collective-permute-start.3
  23.1 0.0 collective-permute-done
  23.1 9.1 %collective-permute-done.3 = bf16[256,768]{1,0:T(8,128)(2,1)S(1)} collective-permute-done((bf16[256,768]{1,0:T(8,128)(2,1)S(1)}, bf16[256,768]{1,0:T(8,128)(2,1)S(1)}, u32[]{:S(2)}, u32[]{:S(2)}) %collective-permute-start.3) | collective-permute-done | bytes 393248 | tf_op jit(solution)/shard_map/ppermute | solution.py:320
  32.2 0.1 collective-permute-start.4
  32.4 0.1 pad_add_fusion.1.place
  32.4 2.8 %collective-permute-done.4.near_b.near = bf16[768,768]{1,0:T(8,128)(2,1)S(1)} collective-permute-done((bf16[768,768]{1,0:T(8,128)(2,1)S(1)}, bf16[768,768]{1,0:T(8,128)(2,1)S(1)}, u32[]{:S(2)}, u32[]{:S(2)}) %collective-permute-start.4) | collective-permute-done | bytes 1179680 | tf_op jit(solution)/shard_map/ppermute | solution.py:320
  35.2 0.0 copy-done.1
  35.2 0.0 copy-done.3
  35.2 3.4 %shard_map.93 = (bf16[2,8,192,128]{3,2,1,0:T(8,128)(2,1)S(1)}, bf16[128,384]{1,0:T(8,128)(2,1)S(1)}, bf16[3,128,1536]{2,1,0:T(8,128)(2,1)}) custom-call(s32[3]{0:T(128)S(1)} %pad_add_fusion.1.place, s32[32,32]{1,0:T(8,128)S(1)} %copy-done.3, bf16[128,384]{1,0:T(8,128)(2,1)S(1)} %copy-done.1, bf16[768,768]{1,0:T(8,128)(2,1)S(1)} %slice_dynamic-update-slice_fusion.near_a.near, ...), custom_call_target="tpu_custom_call" | custom-call | flops 301989888 | bytes 8388608 | tf_op jit(solution)/shard_map/pallas_call | solution.py:87
  38.6 20.6 %all_to_all.15.rows_in = bf16[16,192,128]{2,1,0:T(8,128)(2,1)S(1)} all-to-all(bf16[16,192,128]{2,1,0:T(8,128)(2,1)S(1)} %bitcast.5), channel_id=1, replica_groups=mesh['z'=8,'xl'=2,'core'=2,'y'=4,'xh'=2] {'xl','y','xh'}, dimensions={0} | all-to-all | bytes 1572864 | tf_op jit(solution)/shard_map/all_to_all | solution.py:352
  59.3 0.0 all-gather.2.cloned.1.call-done
  59.3 3.2 %shard_map.94 = (bf16[128,1280]{1,0:T(8,128)(2,1)S(1)}, bf16[8,192,1280]{2,1,0:T(8,128)(2,1)S(1)}) custom-call(s32[3]{0:T(128)S(1)} %pad_add_fusion.1.place, bf16[16,192,128]{2,1,0:T(8,128)(2,1)S(1)} %all_to_all.15.rows_in, bf16[8,192,1280]{2,1,0:T(8,128)(2,1)} %bitcast.6), custom_call_target="tpu_custom_call" | custom-call | flops 503316480 | bytes 3932160 | tf_op jit(solution)/shard_map/pallas_call | solution.py:125
  62.5 1.5 %collective-permute-start.5 = (bf16[128,1280]{1,0:T(8,128)(2,1)S(1)}, bf16[128,1280]{1,0:T(8,128)(2,1)S(1)}, u32[]{:S(2)}, u32[]{:S(2)}) collective-permute-start(bf16[128,1280]{1,0:T(8,128)(2,1)S(1)} %get-tuple-element.23), channel_id=1, source_target_pairs={{0,16},{16,0},{1,17},{17,1},{2,18},{18,2},{3,19},{19,3},{4,20},{20... | collective-permute-start | bytes 983048 | tf_op jit(solution)/shard_map/ppermute | solution.py:320
  64.0 0.0 copy-start.2
  64.0 1.3 shard_map.95.mine
  65.3 5.3 %collective-permute-done.5.got = bf16[128,1280]{1,0:T(8,128)(2,1)S(1)} collective-permute-done((bf16[128,1280]{1,0:T(8,128)(2,1)S(1)}, bf16[128,1280]{1,0:T(8,128)(2,1)S(1)}, u32[]{:S(2)}, u32[]{:S(2)}) %collective-permute-start.5) | collective-permute-done | bytes 327712 | tf_op jit(solution)/shard_map/ppermute | solution.py:320
  70.6 0.0 copy-done.2
  70.6 0.7 shard_map.96
  71.4 1.6 %collective-permute-start.6 = (bf16[2,128,1280]{2,1,0:T(8,128)(2,1)S(1)}, bf16[2,128,1280]{2,1,0:T(8,128)(2,1)S(1)}, u32[]{:S(2)}, u32[]{:S(2)}) collective-permute-start(bf16[2,128,1280]{2,1,0:T(8,128)(2,1)S(1)} %get-tuple-element.27), channel_id=1, source_target_pairs={{0,16},{16,0},{1,17},{17,1},{2,18},{18,2},{3,19},{19,3},{4,20},{20... | collective-permute-start | bytes 1966088 | tf_op jit(solution)/shard_map/ppermute | solution.py:320
  73.0 15.1 %all_to_all.16.sums = bf16[32,24,128]{2,1,0:T(8,128)(2,1)S(1)} all-to-all(bf16[32,24,128]{2,1,0:T(8,128)(2,1)S(1)} %get-tuple-element.28), channel_id=1, replica_groups=mesh['z'=8,'xl'=2,'core'=2,'y'=4,'xh'=2] {'z','xl','core'}, dimensions={0} | all-to-all | bytes 393216 | tf_op jit(solution)/shard_map/all_to_all | solution.py:358
  88.1 0.0 collective-permute-done.6.pair
  88.1 2.0 %shard_map.97 = (bf16[16,192,128]{2,1,0:T(8,128)(2,1)S(1)}, f32[16,128]{1,0:T(8,128)S(1)}) custom-call(s32[3]{0:T(128)S(1)} %pad_add_fusion.1.place, f32[128,1280]{1,0:T(8,128)S(1)} %get-tuple-element.25.pull, f32[128,1280]{1,0:T(8,128)S(1)} %get-tuple-element.26.push, bf16[2,128,1280]{2,1,0:T(8,128)(2,1)S(1)} %collective-permute-done.6.pair, ...), custom_call_target="tpu_custom_call" | custom-call | flops 1006632960 | bytes 3932160 | tf_op jit(solution)/shard_map/pallas_call | solution.py:231
  90.1 0.0 copy-start
  90.1 17.8 %all_to_all.17.refs_0_ = bf16[16,192,128]{2,1,0:T(8,128)(2,1)S(1)} all-to-all(bf16[16,192,128]{2,1,0:T(8,128)(2,1)S(1)} %get-tuple-element.32), channel_id=1, replica_groups=mesh['z'=8,'xl'=2,'core'=2,'y'=4,'xh'=2] {'xl','y','xh'}, dimensions={0} | all-to-all | bytes 1572864 | tf_op jit(solution)/shard_map/all_to_all | solution.py:361
  107.9 0.0 copy-done
  107.9 1.3 shard_map.99
  109.2 0.3 collective-permute-start.7
  109.5 1.9 %shard_map.100 = (f32[128,384]{1,0:T(8,128)}, bf16[768,768]{1,0:T(8,128)(2,1)S(1)}) custom-call(bf16[128,384]{1,0:T(8,128)(2,1)S(1)} %copy-done.1, bf16[768,768]{1,0:T(8,128)(2,1)S(1)} %slice_dynamic-update-slice_fusion.near_a.near, bf16[128,384]{1,0:T(8,128)(2,1)S(1)} %get-tuple-element.30.attn, bf16[3,128,1536]{2,1,0:T(8,128)(2,1)S(1)} %copy-done, ...), custom_call_target="tpu_custom_call" | custom-call | flops 301989888 | bytes 4194304 | tf_op jit(solution)/shard_map/pallas_call | solution.py:307
  111.4 0.9 collective-permute-done.7
  112.3 0.3 convert_add_fusion
  112.6 1.5 %collective-permute-start.12 = (bf16[128,768]{1,0:T(8,128)(2,1)S(1)}, bf16[128,768]{1,0:T(8,128)(2,1)S(1)}, u32[]{:S(2)}, u32[]{:S(2)}) collective-permute-start(bf16[128,768]{1,0:T(8,128)(2,1)S(1)} %get-tuple-element.41), channel_id=1, source_target_pairs={{0,16},{16,0},{32,48},{48,32},{64,80},{80,64},{96,112},{112,96},{1... | collective-permute-start | bytes 589832 | tf_op jit(solution)/shard_map/ppermute | solution.py:335
  114.1 2.3 %collective-permute-start.11 = (bf16[128,768]{1,0:T(8,128)(2,1)S(1)}, bf16[128,768]{1,0:T(8,128)(2,1)S(1)}, u32[]{:S(2)}, u32[]{:S(2)}) collective-permute-start(bf16[128,768]{1,0:T(8,128)(2,1)S(1)} %get-tuple-element.42), channel_id=1, source_target_pairs={{0,32},{16,48},{32,64},{48,80},{64,96},{80,112},{96,128},{112,144}... | collective-permute-start | bytes 589832 | tf_op jit(solution)/shard_map/ppermute | solution.py:335
  116.4 0.9 collective-permute-start.10
  117.4 1.1 collective-permute-start.9
  118.5 3.0 %collective-permute-start.8 = (bf16[128,768]{1,0:T(8,128)(2,1)S(1)}, bf16[128,768]{1,0:T(8,128)(2,1)S(1)}, u32[]{:S(2)}, u32[]{:S(2)}) collective-permute-start(bf16[128,768]{1,0:T(8,128)(2,1)S(1)} %get-tuple-element.45), channel_id=1, source_target_pairs={{0,240},{16,224},{32,16},{48,0},{64,48},{80,32},{96,80},{112,64},{... | collective-permute-start | bytes 589832 | tf_op jit(solution)/shard_map/ppermute | solution.py:335
  121.5 0.8 shard_map.98
  122.3 0.0 collective-permute-done.12
  122.3 0.8 collective-permute-done.11
  123.2 1.1 collective-permute-done.10
  124.3 4.1 %collective-permute-done.9 = bf16[128,768]{1,0:T(8,128)(2,1)S(1)} collective-permute-done((bf16[128,768]{1,0:T(8,128)(2,1)S(1)}, bf16[128,768]{1,0:T(8,128)(2,1)S(1)}, u32[]{:S(2)}, u32[]{:S(2)}) %collective-permute-start.9) | collective-permute-done | bytes 196640 | tf_op jit(solution)/shard_map/ppermute | solution.py:335
  128.5 1.4 collective-permute-done.8
  129.9 0.9 slice_add_fusion
  (11 shorter events, 0.2 us)
Async XLA Ops:
  7.2 52.1 %all-gather.2.cloned.1.call-start = ((), (), s32[]{:S(2)}) async-start(), calls=%async_computation.3 | async-start | bytes 4177920 | tf_op jit(solution)/shard_map/all_gather | solution.py:342
  8.9 10.1 %collective-permute-start.2 = (bf16[128,768]{1,0:T(8,128)(2,1)S(1)}, bf16[128,768]{1,0:T(8,128)(2,1)S(1)}, u32[]{:S(2)}, u32[]{:S(2)}) collective-permute-start(bf16[128,768]{1,0:T(8,128)(2,1)S(1)} %get-tuple-element.46), channel_id=1, source_target_pairs={{0,224},{32,0},{64,32},{96,64},{128,96},{160,128},{192,160},{224,1... | collective-permute-start | bytes 589832 | tf_op jit(solution)/shard_map/ppermute | solution.py:328
  14.8 7.6 %collective-permute-start.1 = (bf16[128,768]{1,0:T(8,128)(2,1)S(1)}, bf16[128,768]{1,0:T(8,128)(2,1)S(1)}, u32[]{:S(2)}, u32[]{:S(2)}) collective-permute-start(bf16[128,768]{1,0:T(8,128)(2,1)S(1)} %get-tuple-element.46), channel_id=1, source_target_pairs={{0,32},{32,64},{64,96},{96,128},{128,160},{160,192},{192,224},{224... | collective-permute-start | bytes 589832 | tf_op jit(solution)/shard_map/ppermute | solution.py:324
  14.8 8.2 %collective-permute-start = (bf16[128,768]{1,0:T(8,128)(2,1)S(1)}, bf16[128,768]{1,0:T(8,128)(2,1)S(1)}, u32[]{:S(2)}, u32[]{:S(2)}) collective-permute-start(bf16[128,768]{1,0:T(8,128)(2,1)S(1)} %get-tuple-element.46), channel_id=1, source_target_pairs={{0,16},{16,0},{1,17},{17,1},{2,18},{18,2},{3,19},{19,3},{4,20},{20... | collective-permute-start | bytes 589832 | tf_op jit(solution)/shard_map/ppermute | solution.py:320
  22.4 12.8 %copy-start.1 = (bf16[128,384]{1,0:T(8,128)(2,1)S(1)}, bf16[128,384]{1,0:T(8,128)(2,1)}, u32[]{:S(2)}) copy-start(bf16[128,384]{1,0:T(8,128)(2,1)} %query.5) | copy-start | bytes 294916
  22.4 12.8 %copy-start.3 = (s32[32,32]{1,0:T(8,128)S(1)}, s32[32,32]{1,0:T(8,128)}, u32[]{:S(2)}) copy-start(s32[32,32]{1,0:T(8,128)} %mask.1) | copy-start | bytes 12292
  22.4 9.8 %collective-permute-start.3 = (bf16[256,768]{1,0:T(8,128)(2,1)S(1)}, bf16[256,768]{1,0:T(8,128)(2,1)S(1)}, u32[]{:S(2)}, u32[]{:S(2)}) collective-permute-start(bf16[256,768]{1,0:T(8,128)(2,1)S(1)} %pad_maximum_fusion), channel_id=1, source_target_pairs={{0,16},{16,0},{1,17},{17,1},{2,18},{18,2},{3,19},{19,3},{4,20},{20... | collective-permute-start | bytes 1179656 | tf_op jit(solution)/shard_map/ppermute | solution.py:320
  32.2 2.9 %collective-permute-start.4 = (bf16[768,768]{1,0:T(8,128)(2,1)S(1)}, bf16[768,768]{1,0:T(8,128)(2,1)S(1)}, u32[]{:S(2)}, u32[]{:S(2)}) collective-permute-start(bf16[768,768]{1,0:T(8,128)(2,1)S(1)} %slice_dynamic-update-slice_fusion.near_a.near), channel_id=1, source_target_pairs={{0,8},{8,0},{1,9},{9,1},{2,10},{10,2},{3,11},{11,3},{4,12},{12,4},... | collective-permute-start | bytes 3538952 | tf_op jit(solution)/shard_map/ppermute | solution.py:320
  62.5 8.1 %collective-permute-start.5 = (bf16[128,1280]{1,0:T(8,128)(2,1)S(1)}, bf16[128,1280]{1,0:T(8,128)(2,1)S(1)}, u32[]{:S(2)}, u32[]{:S(2)}) collective-permute-start(bf16[128,1280]{1,0:T(8,128)(2,1)S(1)} %get-tuple-element.23), channel_id=1, source_target_pairs={{0,16},{16,0},{1,17},{17,1},{2,18},{18,2},{3,19},{19,3},{4,20},{20... | collective-permute-start | bytes 983048 | tf_op jit(solution)/shard_map/ppermute | solution.py:320
  64.0 6.6 %copy-start.2 = (bf16[128,1280]{1,0:T(8,128)(2,1)S(1)}, bf16[128,1280]{1,0:T(8,128)(2,1)}, u32[]{:S(2)}) copy-start(bf16[128,1280]{1,0:T(8,128)(2,1)} %cot.1) | copy-start | bytes 983044
  71.4 16.7 %collective-permute-start.6 = (bf16[2,128,1280]{2,1,0:T(8,128)(2,1)S(1)}, bf16[2,128,1280]{2,1,0:T(8,128)(2,1)S(1)}, u32[]{:S(2)}, u32[]{:S(2)}) collective-permute-start(bf16[2,128,1280]{2,1,0:T(8,128)(2,1)S(1)} %get-tuple-element.27), channel_id=1, source_target_pairs={{0,16},{16,0},{1,17},{17,1},{2,18},{18,2},{3,19},{19,3},{4,20},{20... | collective-permute-start | bytes 1966088 | tf_op jit(solution)/shard_map/ppermute | solution.py:320
  90.1 17.9 %copy-start = (bf16[3,128,1536]{2,1,0:T(8,128)(2,1)S(1)}, bf16[3,128,1536]{2,1,0:T(8,128)(2,1)}, u32[]{:S(2)}) copy-start(bf16[3,128,1536]{2,1,0:T(8,128)(2,1)} %get-tuple-element.31.probs) | copy-start | bytes 3538948
  109.2 3.1 %collective-permute-start.7 = (bf16[768,768]{1,0:T(8,128)(2,1)S(1)}, bf16[768,768]{1,0:T(8,128)(2,1)S(1)}, u32[]{:S(2)}, u32[]{:S(2)}) collective-permute-start(bf16[768,768]{1,0:T(8,128)(2,1)S(1)} %get-tuple-element.37), channel_id=1, source_target_pairs={{0,8},{8,0},{1,9},{9,1},{2,10},{10,2},{3,11},{11,3},{4,12},{12,4},... | collective-permute-start | bytes 3538952 | tf_op jit(solution)/shard_map/ppermute | solution.py:320
  112.6 9.7 %collective-permute-start.12 = (bf16[128,768]{1,0:T(8,128)(2,1)S(1)}, bf16[128,768]{1,0:T(8,128)(2,1)S(1)}, u32[]{:S(2)}, u32[]{:S(2)}) collective-permute-start(bf16[128,768]{1,0:T(8,128)(2,1)S(1)} %get-tuple-element.41), channel_id=1, source_target_pairs={{0,16},{16,0},{32,48},{48,32},{64,80},{80,64},{96,112},{112,96},{1... | collective-permute-start | bytes 589832 | tf_op jit(solution)/shard_map/ppermute | solution.py:335
  114.1 9.0 %collective-permute-start.11 = (bf16[128,768]{1,0:T(8,128)(2,1)S(1)}, bf16[128,768]{1,0:T(8,128)(2,1)S(1)}, u32[]{:S(2)}, u32[]{:S(2)}) collective-permute-start(bf16[128,768]{1,0:T(8,128)(2,1)S(1)} %get-tuple-element.42), channel_id=1, source_target_pairs={{0,32},{16,48},{32,64},{48,80},{64,96},{80,112},{96,128},{112,144}... | collective-permute-start | bytes 589832 | tf_op jit(solution)/shard_map/ppermute | solution.py:335
  116.4 7.8 %collective-permute-start.10 = (bf16[128,768]{1,0:T(8,128)(2,1)S(1)}, bf16[128,768]{1,0:T(8,128)(2,1)S(1)}, u32[]{:S(2)}, u32[]{:S(2)}) collective-permute-start(bf16[128,768]{1,0:T(8,128)(2,1)S(1)} %get-tuple-element.43), channel_id=1, source_target_pairs={{0,224},{16,240},{32,0},{48,16},{64,32},{80,48},{96,64},{112,80},{... | collective-permute-start | bytes 589832 | tf_op jit(solution)/shard_map/ppermute | solution.py:335
  117.4 11.1 %collective-permute-start.9 = (bf16[128,768]{1,0:T(8,128)(2,1)S(1)}, bf16[128,768]{1,0:T(8,128)(2,1)S(1)}, u32[]{:S(2)}, u32[]{:S(2)}) collective-permute-start(bf16[128,768]{1,0:T(8,128)(2,1)S(1)} %get-tuple-element.44), channel_id=1, source_target_pairs={{0,48},{16,32},{32,80},{48,64},{64,112},{80,96},{96,144},{112,128}... | collective-permute-start | bytes 589832 | tf_op jit(solution)/shard_map/ppermute | solution.py:335
  118.5 11.4 %collective-permute-start.8 = (bf16[128,768]{1,0:T(8,128)(2,1)S(1)}, bf16[128,768]{1,0:T(8,128)(2,1)S(1)}, u32[]{:S(2)}, u32[]{:S(2)}) collective-permute-start(bf16[128,768]{1,0:T(8,128)(2,1)S(1)} %get-tuple-element.45), channel_id=1, source_target_pairs={{0,240},{16,224},{32,16},{48,0},{64,48},{80,32},{96,80},{112,64},{... | collective-permute-start | bytes 589832 | tf_op jit(solution)/shard_map/ppermute | solution.py:335
Sparse Core Ops, SparseCore 0:
  9.8 44.7 all-gather.1

commit v8 on v7

--- a/solution.py
+++ b/solution.py
@@ -99,10 +99,32 @@
     )(place, mask, query, near_a, near_b)
 
 
-def up_far_kernel(place, rows_in, weight, theirs, held, arrived):
+def turn_kernel(place, rows_in, lhs):
+    sides, depth, rows = rows_in.shape
+    parts = sides // 2
+    for far in range(2):
+        side = (1 - place[1]) if far else place[1]
+        for first in range(0, parts, GROUP):
+            block = rows_in[pl.ds(side * parts + first, GROUP)].reshape(GROUP * depth, rows)
+            turned = block.astype(jnp.float32).T.astype(jnp.bfloat16)
+            lhs[far, :, first * depth : (first + GROUP) * depth] = turned
+
+
+def turn(place, rows_in):
+    sides, depth, rows = rows_in.shape
+    in_vmem = pl.BlockSpec(memory_space=VMEM)
+    return pl.pallas_call(
+        turn_kernel,
+        out_shape=jax.ShapeDtypeStruct((2, rows, sides // 2 * depth), jnp.bfloat16),
+        in_specs=[pl.BlockSpec(memory_space=SMEM), in_vmem],
+        out_specs=in_vmem,
+        compiler_params=pltpu.CompilerParams(vmem_limit_bytes=16 << 20),
+        cost_estimate=pl.CostEstimate(flops=0, bytes_accessed=4 * rows_in.size, transcendentals=0),
+    )(place, rows_in)
+
+
+def up_far_kernel(lhs, weight, theirs, held, arrived):
     parts, depth, width = held.shape
-    rows = rows_in.shape[2]
-    other = 1 - place[1]
     copies = [pltpu.make_async_copy(weight.at[part], held.at[part], arrived.at[part]) for part in range(parts)]
     for copy in copies:
         copy.start()
@@ -110,15 +132,16 @@
     for first in range(0, parts, GROUP):
         for copy in copies[first : first + GROUP]:
             copy.wait()
-        far = rows_in[pl.ds(other * parts + first, GROUP)].reshape(GROUP * depth, rows)
-        term = dot(far, held[first : first + GROUP].reshape(GROUP * depth, width), TN)
+        far = lhs[1, :, first * depth : (first + GROUP) * depth]
+        term = dot(far, held[first : first + GROUP].reshape(GROUP * depth, width))
         total = term if total is None else total + term
     theirs[...] = total.astype(jnp.bfloat16)
 
 
-def up_far(place, rows_in, weight):
-    sides, depth, rows = rows_in.shape
-    parts = sides // 2
+def up_far(lhs, weight):
+    _, rows, depth = lhs.shape
+    parts = PLANES
+    depth = depth // parts
     width = weight.shape[1]
     in_vmem = pl.BlockSpec(memory_space=VMEM)
     in_hbm = pl.BlockSpec(memory_space=pltpu.HBM)
@@ -128,37 +151,35 @@
             jax.ShapeDtypeStruct((rows, width), jnp.bfloat16),
             VMEM((parts, depth, width), jnp.bfloat16),
         ),
-        in_specs=[pl.BlockSpec(memory_space=SMEM), in_vmem, in_hbm],
+        in_specs=[in_vmem, in_hbm],
         out_specs=(in_vmem,) * 2,
         scratch_shapes=[pltpu.SemaphoreType.DMA((parts,))],
         compiler_params=pltpu.CompilerParams(vmem_limit_bytes=46 << 20),
         cost_estimate=pl.CostEstimate(
             flops=2 * rows * width * parts * depth, bytes_accessed=weight.size * 2, transcendentals=0
         ),
-    )(place, rows_in, weight.reshape(parts, depth, width))
-
-
-def up_near_kernel(place, rows_in, held, mine):
+    )(lhs, weight.reshape(parts, depth, width))
+
+
+def up_near_kernel(lhs, held, mine):
     parts, depth, width = held.shape
-    rows = rows_in.shape[2]
-    near = rows_in[pl.ds(place[1] * parts, parts)].reshape(parts * depth, rows)
-    mine[...] = dot(near, held[...].reshape(parts * depth, width), TN)
-
-
-def up_near(place, rows_in, held):
+    mine[...] = dot(lhs[0], held[...].reshape(parts * depth, width))
+
+
+def up_near(lhs, held):
     parts, depth, width = held.shape
-    rows = rows_in.shape[2]
+    rows = lhs.shape[1]
     in_vmem = pl.BlockSpec(memory_space=VMEM)
     return pl.pallas_call(
         up_near_kernel,
         out_shape=jax.ShapeDtypeStruct((rows, width), jnp.float32),
-        in_specs=[pl.BlockSpec(memory_space=SMEM), in_vmem, in_vmem],
+        in_specs=[in_vmem, in_vmem],
         out_specs=in_vmem,
         compiler_params=pltpu.CompilerParams(vmem_limit_bytes=16 << 20),
         cost_estimate=pl.CostEstimate(
             flops=2 * rows * width * parts * depth, bytes_accessed=held.size * 2, transcendentals=0
         ),
-    )(place, rows_in, held)
+    )(lhs, held)
 
 
 def middle_kernel(mine, got, cot, act_out, pull_out, push_out, pair, sums):
@@ -350,9 +371,10 @@
     attn_out, attn, probs = attend(place, tile_mask, query, near_a, near_b, lax.axis_size(FSDP))
     sides, copies, depth, _ = attn_out.shape
     rows_in = lax.all_to_all(attn_out.reshape(sides * copies, depth, rows), WIDE, 0, 0)
-    theirs, held = up_far(place, rows_in, half_weight)
+    lhs = turn(place, rows_in)
+    theirs, held = up_far(lhs, half_weight)
     got = swap(theirs, "xl")
-    mine = up_near(place, rows_in, held)
+    mine = up_near(lhs, held)
     act, pull, push, pair, sums = middle(mine, got, cot, lax.axis_size(SEQ))
     pair = swap(pair, "xl")
     sums = lax.all_to_all(sums, SEQ, 0, 0)

time: 138 us -> 138 us (level)
  transfers between devices with their start and end apart: 14 -> 14, of which waited for: 10 -> 9; matrix products, arithmetic and copies ran while one was open for 1% -> 1% of each run, Pallas kernels for 5% -> 6%
where the time goes in v8:
time: 138 us; the launch traced here: 137 us
  blocking collectives  53.6 us (39%)
  waiting for transfers between devices  33.2 us (24%)
  starting transfers between devices  19.6 us (14%)
  between operations  14.2 us (10%)
  Pallas kernels  14.1 us (10%)
  other arithmetic  2.41 us (2%)
    all_to_all x1, blocking collectives, body(): lax.all_to_all(attn_out.reshape(sides * copies, depth, rows), WIDE, 0, 0)  20.6 us
    ppermute x6, waiting for transfers between devices, swap(): return lax.ppermute(value, axis, [(0, 1), (1, 0)])  18.7 us
    all_to_all x1, blocking collectives, body(): partial = lax.all_to_all(back, WIDE, 0, 0)  17.9 us
    all_to_all x1, blocking collectives, body(): sums = lax.all_to_all(sums, SEQ, 0, 0)  15.1 us
    ppermute x5, starting transfers between devices, shifted(): return lax.ppermute(value, ('z', 'xl'), pairs)  8.91 us
    ppermute x5, waiting for transfers between devices, shifted(): return lax.ppermute(value, ('z', 'xl'), pairs)  6.84 us
    ppermute x1, starting transfers between devices, down_plane(): lax.ppermute(value, 'z', [(i, (i - 1) % PLANES) for i in range(PLANES)])  5.93 us
    ppermute x6, starting transfers between devices, swap(): return lax.ppermute(value, axis, [(0, 1), (1, 0)])  4.69 us
  transfers between devices with their start and end apart: 14, of which 9 were waited for; matrix products, arithmetic and copies ran while one was open for 1% of the time, Pallas kernels for 6%

profile of v8, /device:TPU:2, one launch (start us, length us, event | category | flops | bytes accessed | tf_op | source)
XLA Modules:
  0.0 137.3 jit_solution(6275881993033936198)
XLA Ops:
  7.2 0.0 all-gather.2.cloned.1.call-start
  7.2 0.7 all-gather.2.cloned.1.call-update
  7.9 1.0 pad_add_fusion
  8.9 5.9 %collective-permute-start.2 = (bf16[128,768]{1,0:T(8,128)(2,1)S(1)}, bf16[128,768]{1,0:T(8,128)(2,1)S(1)}, u32[]{:S(2)}, u32[]{:S(2)}) collective-permute-start(bf16[128,768]{1,0:T(8,128)(2,1)S(1)} %get-tuple-element.46), channel_id=1, source_target_pairs={{0,224},{32,0},{64,32},{96,64},{128,96},{160,128},{192,160},{224,1... | collective-permute-start | bytes 589832 | tf_op jit(solution)/shard_map/ppermute | solution.py:349
  14.8 0.0 collective-permute-start.1
  14.8 0.5 collective-permute-start
  15.3 3.6 %collective-permute-done.2 = bf16[128,768]{1,0:T(8,128)(2,1)S(1)} collective-permute-done((bf16[128,768]{1,0:T(8,128)(2,1)S(1)}, bf16[128,768]{1,0:T(8,128)(2,1)S(1)}, u32[]{:S(2)}, u32[]{:S(2)}) %collective-permute-start.2) | collective-permute-done | bytes 196640 | tf_op jit(solution)/shard_map/ppermute | solution.py:349
  19.0 3.4 %collective-permute-done.1 = bf16[128,768]{1,0:T(8,128)(2,1)S(1)} collective-permute-done((bf16[128,768]{1,0:T(8,128)(2,1)S(1)}, bf16[128,768]{1,0:T(8,128)(2,1)S(1)}, u32[]{:S(2)}, u32[]{:S(2)}) %collective-permute-start.1) | collective-permute-done | bytes 196640 | tf_op jit(solution)/shard_map/ppermute | solution.py:345
  22.4 0.0 copy-start.1
  22.4 0.0 copy-start.3
  22.4 0.6 collective-permute-start.3
  23.1 0.0 collective-permute-done
  23.1 9.1 %collective-permute-done.3 = bf16[256,768]{1,0:T(8,128)(2,1)S(1)} collective-permute-done((bf16[256,768]{1,0:T(8,128)(2,1)S(1)}, bf16[256,768]{1,0:T(8,128)(2,1)S(1)}, u32[]{:S(2)}, u32[]{:S(2)}) %collective-permute-start.3) | collective-permute-done | bytes 393248 | tf_op jit(solution)/shard_map/ppermute | solution.py:341
  32.2 0.1 collective-permute-start.4
  32.4 0.1 pad_add_fusion.1.place
  32.4 2.8 %collective-permute-done.4.near_b.near = bf16[768,768]{1,0:T(8,128)(2,1)S(1)} collective-permute-done((bf16[768,768]{1,0:T(8,128)(2,1)S(1)}, bf16[768,768]{1,0:T(8,128)(2,1)S(1)}, u32[]{:S(2)}, u32[]{:S(2)}) %collective-permute-start.4) | collective-permute-done | bytes 1179680 | tf_op jit(solution)/shard_map/ppermute | solution.py:341
  35.2 0.0 copy-done.1
  35.2 0.0 copy-done.3
  35.2 3.4 %shard_map.93 = (bf16[2,8,192,128]{3,2,1,0:T(8,128)(2,1)S(1)}, bf16[128,384]{1,0:T(8,128)(2,1)S(1)}, bf16[3,128,1536]{2,1,0:T(8,128)(2,1)}) custom-call(s32[3]{0:T(128)S(1)} %pad_add_fusion.1.place, s32[32,32]{1,0:T(8,128)S(1)} %copy-done.3, bf16[128,384]{1,0:T(8,128)(2,1)S(1)} %copy-done.1, bf16[768,768]{1,0:T(8,128)(2,1)S(1)} %slice_dynamic-update-slice_fusion.near_a.near, ...), custom_call_target="tpu_custom_call" | custom-call | flops 301989888 | bytes 8388608 | tf_op jit(solution)/shard_map/pallas_call | solution.py:87
  38.6 20.6 %all_to_all.15.rows_in = bf16[16,192,128]{2,1,0:T(8,128)(2,1)S(1)} all-to-all(bf16[16,192,128]{2,1,0:T(8,128)(2,1)S(1)} %bitcast.5), channel_id=1, replica_groups=mesh['z'=8,'xl'=2,'core'=2,'y'=4,'xh'=2] {'xl','y','xh'}, dimensions={0} | all-to-all | bytes 1572864 | tf_op jit(solution)/shard_map/all_to_all | solution.py:373
  59.3 0.8 shard_map.94.lhs
  60.1 0.0 all-gather.2.cloned.1.call-done
  60.1 2.6 %shard_map.95 = (bf16[128,1280]{1,0:T(8,128)(2,1)S(1)}, bf16[8,192,1280]{2,1,0:T(8,128)(2,1)S(1)}) custom-call(bf16[2,128,1536]{2,1,0:T(8,128)(2,1)S(1)} %shard_map.94.lhs, bf16[8,192,1280]{2,1,0:T(8,128)(2,1)} %bitcast.6), custom_call_target="tpu_custom_call" | custom-call | flops 503316480 | bytes 3932160 | tf_op jit(solution)/shard_map/pallas_call | solution.py:148
  62.7 1.5 %collective-permute-start.5 = (bf16[128,1280]{1,0:T(8,128)(2,1)S(1)}, bf16[128,1280]{1,0:T(8,128)(2,1)S(1)}, u32[]{:S(2)}, u32[]{:S(2)}) collective-permute-start(bf16[128,1280]{1,0:T(8,128)(2,1)S(1)} %get-tuple-element.23), channel_id=1, source_target_pairs={{0,16},{16,0},{1,17},{17,1},{2,18},{18,2},{3,19},{19,3},{4,20},{20... | collective-permute-start | bytes 983048 | tf_op jit(solution)/shard_map/ppermute | solution.py:341
  64.3 0.0 copy-start.2
  64.3 0.7 shard_map.96.mine
  64.9 5.9 %collective-permute-done.5.got = bf16[128,1280]{1,0:T(8,128)(2,1)S(1)} collective-permute-done((bf16[128,1280]{1,0:T(8,128)(2,1)S(1)}, bf16[128,1280]{1,0:T(8,128)(2,1)S(1)}, u32[]{:S(2)}, u32[]{:S(2)}) %collective-permute-start.5) | collective-permute-done | bytes 327712 | tf_op jit(solution)/shard_map/ppermute | solution.py:341
  70.8 0.0 copy-done.2
  70.9 0.7 shard_map.97
  71.6 1.6 %collective-permute-start.6 = (bf16[2,128,1280]{2,1,0:T(8,128)(2,1)S(1)}, bf16[2,128,1280]{2,1,0:T(8,128)(2,1)S(1)}, u32[]{:S(2)}, u32[]{:S(2)}) collective-permute-start(bf16[2,128,1280]{2,1,0:T(8,128)(2,1)S(1)} %get-tuple-element.27), channel_id=1, source_target_pairs={{0,16},{16,0},{1,17},{17,1},{2,18},{18,2},{3,19},{19,3},{4,20},{20... | collective-permute-start | bytes 1966088 | tf_op jit(solution)/shard_map/ppermute | solution.py:341
  73.2 15.1 %all_to_all.16.sums = bf16[32,24,128]{2,1,0:T(8,128)(2,1)S(1)} all-to-all(bf16[32,24,128]{2,1,0:T(8,128)(2,1)S(1)} %get-tuple-element.28), channel_id=1, replica_groups=mesh['z'=8,'xl'=2,'core'=2,'y'=4,'xh'=2] {'z','xl','core'}, dimensions={0} | all-to-all | bytes 393216 | tf_op jit(solution)/shard_map/all_to_all | solution.py:380
  88.3 0.0 collective-permute-done.6.pair
  88.3 1.9 %shard_map.98 = (bf16[16,192,128]{2,1,0:T(8,128)(2,1)S(1)}, f32[16,128]{1,0:T(8,128)S(1)}) custom-call(s32[3]{0:T(128)S(1)} %pad_add_fusion.1.place, f32[128,1280]{1,0:T(8,128)S(1)} %get-tuple-element.25.pull, f32[128,1280]{1,0:T(8,128)S(1)} %get-tuple-element.26.push, bf16[2,128,1280]{2,1,0:T(8,128)(2,1)S(1)} %collective-permute-done.6.pair, ...), custom_call_target="tpu_custom_call" | custom-call | flops 1006632960 | bytes 3932160 | tf_op jit(solution)/shard_map/pallas_call | solution.py:252
  90.3 0.0 copy-start
  90.3 17.9 %all_to_all.17.refs_0_ = bf16[16,192,128]{2,1,0:T(8,128)(2,1)S(1)} all-to-all(bf16[16,192,128]{2,1,0:T(8,128)(2,1)S(1)} %get-tuple-element.32), channel_id=1, replica_groups=mesh['z'=8,'xl'=2,'core'=2,'y'=4,'xh'=2] {'xl','y','xh'}, dimensions={0} | all-to-all | bytes 1572864 | tf_op jit(solution)/shard_map/all_to_all | solution.py:383
  108.1 0.0 copy-done
  108.1 1.3 shard_map.100
  109.4 0.3 collective-permute-start.7
  109.7 1.9 %shard_map.101 = (f32[128,384]{1,0:T(8,128)}, bf16[768,768]{1,0:T(8,128)(2,1)S(1)}) custom-call(bf16[128,384]{1,0:T(8,128)(2,1)S(1)} %copy-done.1, bf16[768,768]{1,0:T(8,128)(2,1)S(1)} %slice_dynamic-update-slice_fusion.near_a.near, bf16[128,384]{1,0:T(8,128)(2,1)S(1)} %get-tuple-element.30.attn, bf16[3,128,1536]{2,1,0:T(8,128)(2,1)S(1)} %copy-done, ...), custom_call_target="tpu_custom_call" | custom-call | flops 301989888 | bytes 4194304 | tf_op jit(solution)/shard_map/pallas_call | solution.py:328
  111.6 0.9 collective-permute-done.7
  112.5 0.3 convert_add_fusion
  112.8 1.5 %collective-permute-start.12 = (bf16[128,768]{1,0:T(8,128)(2,1)S(1)}, bf16[128,768]{1,0:T(8,128)(2,1)S(1)}, u32[]{:S(2)}, u32[]{:S(2)}) collective-permute-start(bf16[128,768]{1,0:T(8,128)(2,1)S(1)} %get-tuple-element.41), channel_id=1, source_target_pairs={{0,16},{16,0},{32,48},{48,32},{64,80},{80,64},{96,112},{112,96},{1... | collective-permute-start | bytes 589832 | tf_op jit(solution)/shard_map/ppermute | solution.py:356
  114.3 0.9 collective-permute-start.11
  115.2 2.3 %collective-permute-start.10 = (bf16[128,768]{1,0:T(8,128)(2,1)S(1)}, bf16[128,768]{1,0:T(8,128)(2,1)S(1)}, u32[]{:S(2)}, u32[]{:S(2)}) collective-permute-start(bf16[128,768]{1,0:T(8,128)(2,1)S(1)} %get-tuple-element.43), channel_id=1, source_target_pairs={{0,224},{16,240},{32,0},{48,16},{64,32},{80,48},{96,64},{112,80},{... | collective-permute-start | bytes 589832 | tf_op jit(solution)/shard_map/ppermute | solution.py:356
  117.6 0.0 collective-permute-start.9
  117.6 4.1 %collective-permute-start.8 = (bf16[128,768]{1,0:T(8,128)(2,1)S(1)}, bf16[128,768]{1,0:T(8,128)(2,1)S(1)}, u32[]{:S(2)}, u32[]{:S(2)}) collective-permute-start(bf16[128,768]{1,0:T(8,128)(2,1)S(1)} %get-tuple-element.45), channel_id=1, source_target_pairs={{0,240},{16,224},{32,16},{48,0},{64,48},{80,32},{96,80},{112,64},{... | collective-permute-start | bytes 589832 | tf_op jit(solution)/shard_map/ppermute | solution.py:356
  121.7 0.8 shard_map.99
  122.5 0.0 collective-permute-done.12
  122.5 0.8 collective-permute-done.11
  123.4 0.0 collective-permute-done.10
  123.4 5.6 %collective-permute-done.9 = bf16[128,768]{1,0:T(8,128)(2,1)S(1)} collective-permute-done((bf16[128,768]{1,0:T(8,128)(2,1)S(1)}, bf16[128,768]{1,0:T(8,128)(2,1)S(1)}, u32[]{:S(2)}, u32[]{:S(2)}) %collective-permute-start.9) | collective-permute-done | bytes 196640 | tf_op jit(solution)/shard_map/ppermute | solution.py:356
  129.1 0.4 collective-permute-done.8
  129.5 0.9 slice_add_fusion
  (11 shorter events, 0.2 us)
Async XLA Ops:
  7.2 53.0 %all-gather.2.cloned.1.call-start = ((), (), s32[]{:S(2)}) async-start(), calls=%async_computation.3 | async-start | bytes 4177920 | tf_op jit(solution)/shard_map/all_gather | solution.py:363
  8.9 10.1 %collective-permute-start.2 = (bf16[128,768]{1,0:T(8,128)(2,1)S(1)}, bf16[128,768]{1,0:T(8,128)(2,1)S(1)}, u32[]{:S(2)}, u32[]{:S(2)}) collective-permute-start(bf16[128,768]{1,0:T(8,128)(2,1)S(1)} %get-tuple-element.46), channel_id=1, source_target_pairs={{0,224},{32,0},{64,32},{96,64},{128,96},{160,128},{192,160},{224,1... | collective-permute-start | bytes 589832 | tf_op jit(solution)/shard_map/ppermute | solution.py:349
  14.8 7.6 %collective-permute-start.1 = (bf16[128,768]{1,0:T(8,128)(2,1)S(1)}, bf16[128,768]{1,0:T(8,128)(2,1)S(1)}, u32[]{:S(2)}, u32[]{:S(2)}) collective-permute-start(bf16[128,768]{1,0:T(8,128)(2,1)S(1)} %get-tuple-element.46), channel_id=1, source_target_pairs={{0,32},{32,64},{64,96},{96,128},{128,160},{160,192},{192,224},{224... | collective-permute-start | bytes 589832 | tf_op jit(solution)/shard_map/ppermute | solution.py:345
  14.8 8.2 %collective-permute-start = (bf16[128,768]{1,0:T(8,128)(2,1)S(1)}, bf16[128,768]{1,0:T(8,128)(2,1)S(1)}, u32[]{:S(2)}, u32[]{:S(2)}) collective-permute-start(bf16[128,768]{1,0:T(8,128)(2,1)S(1)} %get-tuple-element.46), channel_id=1, source_target_pairs={{0,16},{16,0},{1,17},{17,1},{2,18},{18,2},{3,19},{19,3},{4,20},{20... | collective-permute-start | bytes 589832 | tf_op jit(solution)/shard_map/ppermute | solution.py:341
  22.4 12.8 %copy-start.1 = (bf16[128,384]{1,0:T(8,128)(2,1)S(1)}, bf16[128,384]{1,0:T(8,128)(2,1)}, u32[]{:S(2)}) copy-start(bf16[128,384]{1,0:T(8,128)(2,1)} %query.5) | copy-start | bytes 294916
  22.4 12.8 %copy-start.3 = (s32[32,32]{1,0:T(8,128)S(1)}, s32[32,32]{1,0:T(8,128)}, u32[]{:S(2)}) copy-start(s32[32,32]{1,0:T(8,128)} %mask.1) | copy-start | bytes 12292
  22.4 9.8 %collective-permute-start.3 = (bf16[256,768]{1,0:T(8,128)(2,1)S(1)}, bf16[256,768]{1,0:T(8,128)(2,1)S(1)}, u32[]{:S(2)}, u32[]{:S(2)}) collective-permute-start(bf16[256,768]{1,0:T(8,128)(2,1)S(1)} %pad_maximum_fusion), channel_id=1, source_target_pairs={{0,16},{16,0},{1,17},{17,1},{2,18},{18,2},{3,19},{19,3},{4,20},{20... | collective-permute-start | bytes 1179656 | tf_op jit(solution)/shard_map/ppermute | solution.py:341
  32.2 2.9 %collective-permute-start.4 = (bf16[768,768]{1,0:T(8,128)(2,1)S(1)}, bf16[768,768]{1,0:T(8,128)(2,1)S(1)}, u32[]{:S(2)}, u32[]{:S(2)}) collective-permute-start(bf16[768,768]{1,0:T(8,128)(2,1)S(1)} %slice_dynamic-update-slice_fusion.near_a.near), channel_id=1, source_target_pairs={{0,8},{8,0},{1,9},{9,1},{2,10},{10,2},{3,11},{11,3},{4,12},{12,4},... | collective-permute-start | bytes 3538952 | tf_op jit(solution)/shard_map/ppermute | solution.py:341
  62.7 8.1 %collective-permute-start.5 = (bf16[128,1280]{1,0:T(8,128)(2,1)S(1)}, bf16[128,1280]{1,0:T(8,128)(2,1)S(1)}, u32[]{:S(2)}, u32[]{:S(2)}) collective-permute-start(bf16[128,1280]{1,0:T(8,128)(2,1)S(1)} %get-tuple-element.23), channel_id=1, source_target_pairs={{0,16},{16,0},{1,17},{17,1},{2,18},{18,2},{3,19},{19,3},{4,20},{20... | collective-permute-start | bytes 983048 | tf_op jit(solution)/shard_map/ppermute | solution.py:341
  64.3 6.6 %copy-start.2 = (bf16[128,1280]{1,0:T(8,128)(2,1)S(1)}, bf16[128,1280]{1,0:T(8,128)(2,1)}, u32[]{:S(2)}) copy-start(bf16[128,1280]{1,0:T(8,128)(2,1)} %cot.1) | copy-start | bytes 983044
  71.6 16.8 %collective-permute-start.6 = (bf16[2,128,1280]{2,1,0:T(8,128)(2,1)S(1)}, bf16[2,128,1280]{2,1,0:T(8,128)(2,1)S(1)}, u32[]{:S(2)}, u32[]{:S(2)}) collective-permute-start(bf16[2,128,1280]{2,1,0:T(8,128)(2,1)S(1)} %get-tuple-element.27), channel_id=1, source_target_pairs={{0,16},{16,0},{1,17},{17,1},{2,18},{18,2},{3,19},{19,3},{4,20},{20... | collective-permute-start | bytes 1966088 | tf_op jit(solution)/shard_map/ppermute | solution.py:341
  90.3 17.9 %copy-start = (bf16[3,128,1536]{2,1,0:T(8,128)(2,1)S(1)}, bf16[3,128,1536]{2,1,0:T(8,128)(2,1)}, u32[]{:S(2)}) copy-start(bf16[3,128,1536]{2,1,0:T(8,128)(2,1)} %get-tuple-element.31.probs) | copy-start | bytes 3538948
  109.4 3.1 %collective-permute-start.7 = (bf16[768,768]{1,0:T(8,128)(2,1)S(1)}, bf16[768,768]{1,0:T(8,128)(2,1)S(1)}, u32[]{:S(2)}, u32[]{:S(2)}) collective-permute-start(bf16[768,768]{1,0:T(8,128)(2,1)S(1)} %get-tuple-element.37), channel_id=1, source_target_pairs={{0,8},{8,0},{1,9},{9,1},{2,10},{10,2},{3,11},{11,3},{4,12},{12,4},... | collective-permute-start | bytes 3538952 | tf_op jit(solution)/shard_map/ppermute | solution.py:341
  112.8 9.7 %collective-permute-start.12 = (bf16[128,768]{1,0:T(8,128)(2,1)S(1)}, bf16[128,768]{1,0:T(8,128)(2,1)S(1)}, u32[]{:S(2)}, u32[]{:S(2)}) collective-permute-start(bf16[128,768]{1,0:T(8,128)(2,1)S(1)} %get-tuple-element.41), channel_id=1, source_target_pairs={{0,16},{16,0},{32,48},{48,32},{64,80},{80,64},{96,112},{112,96},{1... | collective-permute-start | bytes 589832 | tf_op jit(solution)/shard_map/ppermute | solution.py:356
  114.3 9.0 %collective-permute-start.11 = (bf16[128,768]{1,0:T(8,128)(2,1)S(1)}, bf16[128,768]{1,0:T(8,128)(2,1)S(1)}, u32[]{:S(2)}, u32[]{:S(2)}) collective-permute-start(bf16[128,768]{1,0:T(8,128)(2,1)S(1)} %get-tuple-element.42), channel_id=1, source_target_pairs={{0,32},{16,48},{32,64},{48,80},{64,96},{80,112},{96,128},{112,144}... | collective-permute-start | bytes 589832 | tf_op jit(solution)/shard_map/ppermute | solution.py:356
  115.2 8.1 %collective-permute-start.10 = (bf16[128,768]{1,0:T(8,128)(2,1)S(1)}, bf16[128,768]{1,0:T(8,128)(2,1)S(1)}, u32[]{:S(2)}, u32[]{:S(2)}) collective-permute-start(bf16[128,768]{1,0:T(8,128)(2,1)S(1)} %get-tuple-element.43), channel_id=1, source_target_pairs={{0,224},{16,240},{32,0},{48,16},{64,32},{80,48},{96,64},{112,80},{... | collective-permute-start | bytes 589832 | tf_op jit(solution)/shard_map/ppermute | solution.py:356
  117.6 11.5 %collective-permute-start.9 = (bf16[128,768]{1,0:T(8,128)(2,1)S(1)}, bf16[128,768]{1,0:T(8,128)(2,1)S(1)}, u32[]{:S(2)}, u32[]{:S(2)}) collective-permute-start(bf16[128,768]{1,0:T(8,128)(2,1)S(1)} %get-tuple-element.44), channel_id=1, source_target_pairs={{0,48},{16,32},{32,80},{48,64},{64,112},{80,96},{96,144},{112,128}... | collective-permute-start | bytes 589832 | tf_op jit(solution)/shard_map/ppermute | solution.py:356
  117.6 11.9 %collective-permute-start.8 = (bf16[128,768]{1,0:T(8,128)(2,1)S(1)}, bf16[128,768]{1,0:T(8,128)(2,1)S(1)}, u32[]{:S(2)}, u32[]{:S(2)}) collective-permute-start(bf16[128,768]{1,0:T(8,128)(2,1)S(1)} %get-tuple-element.45), channel_id=1, source_target_pairs={{0,240},{16,224},{32,16},{48,0},{64,48},{80,32},{96,80},{112,64},{... | collective-permute-start | bytes 589832 | tf_op jit(solution)/shard_map/ppermute | solution.py:356
Sparse Core Ops, SparseCore 0:
  9.8 44.7 all-gather.1

commit v9 on v8

--- a/solution.py
+++ b/solution.py
@@ -337,6 +337,30 @@
     )(query, near, attn, probs, *rest)
 
 
+def finish_kernel(own, *refs):
+    arrived, (grad_key, grad_value) = refs[:-2], refs[-2:]
+    width = grad_key.shape[1]
+    for out, low in ((grad_key, 0), (grad_value, width)):
+        total = own[:, low : low + width]
+        for block in arrived:
+            total = total + block[:, low : low + width].astype(jnp.float32)
+        out[...] = total
+
+
+def finish(own, *arrived):
+    rows, width = own.shape
+    in_vmem = pl.BlockSpec(memory_space=VMEM)
+    half = jax.ShapeDtypeStruct((rows, width // 2), jnp.float32)
+    return pl.pallas_call(
+        finish_kernel,
+        out_shape=(half, half),
+        in_specs=[in_vmem] * (1 + len(arrived)),
+        out_specs=(in_vmem,) * 2,
+        compiler_params=pltpu.CompilerParams(vmem_limit_bytes=16 << 20),
+        cost_estimate=pl.CostEstimate(flops=own.size * len(arrived), bytes_accessed=20 * own.size, transcendentals=0),
+    )(own, *arrived)
+
+
 def swap(value, axis):
     return lax.ppermute(value, axis, [(0, 1), (1, 0)])
 
@@ -389,9 +413,7 @@
     ]
     moves = ((3, -1, 1), (5, 1, 1), (2, -1, 0), (4, 1, 0), (1, 0, 1))
     arrived = [shifted(blocks[i].astype(bf16), planes, xl) for i, planes, xl in moves]
-    terms = [blocks[0]] + [block.astype(f32) for block in arrived]
-    grad_key = functools.reduce(jnp.add, [term[:, :width] for term in terms])
-    grad_value = functools.reduce(jnp.add, [term[:, width:] for term in terms])
+    grad_key, grad_value = finish(blocks[0], *arrived)
     return scaled, grad_query, grad_key, grad_value
 
 

time: 138 us -> 137 us (level)
  no operation moved by 1% of the time
where the time goes in v9:
time: 137 us
  blocking collectives  53.6 us (39%)
  waiting for transfers between devices  33.4 us (24%)
  starting transfers between devices  19.6 us (14%)
  Pallas kernels  14.9 us (11%)
  between operations  14.2 us (10%)
    all_to_all x1, blocking collectives, body(): lax.all_to_all(attn_out.reshape(sides * copies, depth, rows), WIDE, 0, 0)  20.6 us
    ppermute x6, waiting for transfers between devices, swap(): return lax.ppermute(value, axis, [(0, 1), (1, 0)])  18.7 us
    all_to_all x1, blocking collectives, body(): partial = lax.all_to_all(back, WIDE, 0, 0)  17.9 us
    all_to_all x1, blocking collectives, body(): sums = lax.all_to_all(sums, SEQ, 0, 0)  15.1 us
    ppermute x5, starting transfers between devices, shifted(): return lax.ppermute(value, ('z', 'xl'), pairs)  8.91 us
    ppermute x5, waiting for transfers between devices, shifted(): return lax.ppermute(value, ('z', 'xl'), pairs)  6.97 us
    ppermute x1, starting transfers between devices, down_plane(): lax.ppermute(value, 'z', [(i, (i - 1) % PLANES) for i in range(PLANES)])  5.93 us
    ppermute x6, starting transfers between devices, swap(): return lax.ppermute(value, axis, [(0, 1), (1, 0)])  4.69 us
  transfers between devices with their start and end apart: 14, of which 9 were waited for; matrix products, arithmetic and copies ran while one was open for 1% of the time, Pallas kernels for 6%

profile of v9, /device:TPU:2, one launch (start us, length us, event | category | flops | bytes accessed | tf_op | source)
XLA Modules:
  0.0 137.1 jit_solution(3954681987764911991)
XLA Ops:
  7.2 0.0 all-gather.2.cloned.1.call-start
  7.2 0.7 all-gather.2.cloned.1.call-update
  7.9 1.0 pad_add_fusion
  8.9 5.9 %collective-permute-start.2 = (bf16[128,768]{1,0:T(8,128)(2,1)S(1)}, bf16[128,768]{1,0:T(8,128)(2,1)S(1)}, u32[]{:S(2)}, u32[]{:S(2)}) collective-permute-start(bf16[128,768]{1,0:T(8,128)(2,1)S(1)} %get-tuple-element.48), channel_id=1, source_target_pairs={{0,224},{32,0},{64,32},{96,64},{128,96},{160,128},{192,160},{224,1... | collective-permute-start | bytes 589832 | tf_op jit(solution)/shard_map/ppermute | solution.py:373
  14.8 0.0 collective-permute-start.1
  14.8 0.5 collective-permute-start
  15.3 3.6 %collective-permute-done.2 = bf16[128,768]{1,0:T(8,128)(2,1)S(1)} collective-permute-done((bf16[128,768]{1,0:T(8,128)(2,1)S(1)}, bf16[128,768]{1,0:T(8,128)(2,1)S(1)}, u32[]{:S(2)}, u32[]{:S(2)}) %collective-permute-start.2) | collective-permute-done | bytes 196640 | tf_op jit(solution)/shard_map/ppermute | solution.py:373
  19.0 3.4 %collective-permute-done.1 = bf16[128,768]{1,0:T(8,128)(2,1)S(1)} collective-permute-done((bf16[128,768]{1,0:T(8,128)(2,1)S(1)}, bf16[128,768]{1,0:T(8,128)(2,1)S(1)}, u32[]{:S(2)}, u32[]{:S(2)}) %collective-permute-start.1) | collective-permute-done | bytes 196640 | tf_op jit(solution)/shard_map/ppermute | solution.py:369
  22.4 0.0 copy-start.1
  22.4 0.0 copy-start.3
  22.4 0.6 collective-permute-start.3
  23.1 0.0 collective-permute-done
  23.1 9.1 %collective-permute-done.3 = bf16[256,768]{1,0:T(8,128)(2,1)S(1)} collective-permute-done((bf16[256,768]{1,0:T(8,128)(2,1)S(1)}, bf16[256,768]{1,0:T(8,128)(2,1)S(1)}, u32[]{:S(2)}, u32[]{:S(2)}) %collective-permute-start.3) | collective-permute-done | bytes 393248 | tf_op jit(solution)/shard_map/ppermute | solution.py:365
  32.2 0.1 collective-permute-start.4
  32.4 0.1 pad_add_fusion.1.place
  32.4 2.8 %collective-permute-done.4.near_b.near = bf16[768,768]{1,0:T(8,128)(2,1)S(1)} collective-permute-done((bf16[768,768]{1,0:T(8,128)(2,1)S(1)}, bf16[768,768]{1,0:T(8,128)(2,1)S(1)}, u32[]{:S(2)}, u32[]{:S(2)}) %collective-permute-start.4) | collective-permute-done | bytes 1179680 | tf_op jit(solution)/shard_map/ppermute | solution.py:365
  35.2 0.0 copy-done.1
  35.2 0.0 copy-done.3
  35.2 3.4 %shard_map.93 = (bf16[2,8,192,128]{3,2,1,0:T(8,128)(2,1)S(1)}, bf16[128,384]{1,0:T(8,128)(2,1)S(1)}, bf16[3,128,1536]{2,1,0:T(8,128)(2,1)}) custom-call(s32[3]{0:T(128)S(1)} %pad_add_fusion.1.place, s32[32,32]{1,0:T(8,128)S(1)} %copy-done.3, bf16[128,384]{1,0:T(8,128)(2,1)S(1)} %copy-done.1, bf16[768,768]{1,0:T(8,128)(2,1)S(1)} %slice_dynamic-update-slice_fusion.near_a.near, ...), custom_call_target="tpu_custom_call" | custom-call | flops 301989888 | bytes 8388608 | tf_op jit(solution)/shard_map/pallas_call | solution.py:87
  38.6 20.6 %all_to_all.15.rows_in = bf16[16,192,128]{2,1,0:T(8,128)(2,1)S(1)} all-to-all(bf16[16,192,128]{2,1,0:T(8,128)(2,1)S(1)} %bitcast.5), channel_id=1, replica_groups=mesh['z'=8,'xl'=2,'core'=2,'y'=4,'xh'=2] {'xl','y','xh'}, dimensions={0} | all-to-all | bytes 1572864 | tf_op jit(solution)/shard_map/all_to_all | solution.py:397
  59.3 0.8 shard_map.94.lhs
  60.1 0.0 all-gather.2.cloned.1.call-done
  60.1 2.6 %shard_map.95 = (bf16[128,1280]{1,0:T(8,128)(2,1)S(1)}, bf16[8,192,1280]{2,1,0:T(8,128)(2,1)S(1)}) custom-call(bf16[2,128,1536]{2,1,0:T(8,128)(2,1)S(1)} %shard_map.94.lhs, bf16[8,192,1280]{2,1,0:T(8,128)(2,1)} %bitcast.6), custom_call_target="tpu_custom_call" | custom-call | flops 503316480 | bytes 3932160 | tf_op jit(solution)/shard_map/pallas_call | solution.py:148
  62.7 1.5 %collective-permute-start.5 = (bf16[128,1280]{1,0:T(8,128)(2,1)S(1)}, bf16[128,1280]{1,0:T(8,128)(2,1)S(1)}, u32[]{:S(2)}, u32[]{:S(2)}) collective-permute-start(bf16[128,1280]{1,0:T(8,128)(2,1)S(1)} %get-tuple-element.25), channel_id=1, source_target_pairs={{0,16},{16,0},{1,17},{17,1},{2,18},{18,2},{3,19},{19,3},{4,20},{20... | collective-permute-start | bytes 983048 | tf_op jit(solution)/shard_map/ppermute | solution.py:365
  64.3 0.0 copy-start.2
  64.3 0.7 shard_map.96.mine
  64.9 5.9 %collective-permute-done.5.got = bf16[128,1280]{1,0:T(8,128)(2,1)S(1)} collective-permute-done((bf16[128,1280]{1,0:T(8,128)(2,1)S(1)}, bf16[128,1280]{1,0:T(8,128)(2,1)S(1)}, u32[]{:S(2)}, u32[]{:S(2)}) %collective-permute-start.5) | collective-permute-done | bytes 327712 | tf_op jit(solution)/shard_map/ppermute | solution.py:365
  70.8 0.0 copy-done.2
  70.9 0.7 shard_map.97
  71.6 1.6 %collective-permute-start.6 = (bf16[2,128,1280]{2,1,0:T(8,128)(2,1)S(1)}, bf16[2,128,1280]{2,1,0:T(8,128)(2,1)S(1)}, u32[]{:S(2)}, u32[]{:S(2)}) collective-permute-start(bf16[2,128,1280]{2,1,0:T(8,128)(2,1)S(1)} %get-tuple-element.29), channel_id=1, source_target_pairs={{0,16},{16,0},{1,17},{17,1},{2,18},{18,2},{3,19},{19,3},{4,20},{20... | collective-permute-start | bytes 1966088 | tf_op jit(solution)/shard_map/ppermute | solution.py:365
  73.2 15.1 %all_to_all.16.sums = bf16[32,24,128]{2,1,0:T(8,128)(2,1)S(1)} all-to-all(bf16[32,24,128]{2,1,0:T(8,128)(2,1)S(1)} %get-tuple-element.30), channel_id=1, replica_groups=mesh['z'=8,'xl'=2,'core'=2,'y'=4,'xh'=2] {'z','xl','core'}, dimensions={0} | all-to-all | bytes 393216 | tf_op jit(solution)/shard_map/all_to_all | solution.py:404
  88.3 0.0 collective-permute-done.6.pair
  88.3 1.9 %shard_map.98 = (bf16[16,192,128]{2,1,0:T(8,128)(2,1)S(1)}, f32[16,128]{1,0:T(8,128)S(1)}) custom-call(s32[3]{0:T(128)S(1)} %pad_add_fusion.1.place, f32[128,1280]{1,0:T(8,128)S(1)} %get-tuple-element.27.pull, f32[128,1280]{1,0:T(8,128)S(1)} %get-tuple-element.28.push, bf16[2,128,1280]{2,1,0:T(8,128)(2,1)S(1)} %collective-permute-done.6.pair, ...), custom_call_target="tpu_custom_call" | custom-call | flops 1006632960 | bytes 3932160 | tf_op jit(solution)/shard_map/pallas_call | solution.py:252
  90.3 0.0 copy-start
  90.3 17.9 %all_to_all.17.refs_0_ = bf16[16,192,128]{2,1,0:T(8,128)(2,1)S(1)} all-to-all(bf16[16,192,128]{2,1,0:T(8,128)(2,1)S(1)} %get-tuple-element.34), channel_id=1, replica_groups=mesh['z'=8,'xl'=2,'core'=2,'y'=4,'xh'=2] {'xl','y','xh'}, dimensions={0} | all-to-all | bytes 1572864 | tf_op jit(solution)/shard_map/all_to_all | solution.py:407
  108.1 0.0 copy-done
  108.1 1.3 shard_map.100
  109.4 0.3 collective-permute-start.7
  109.7 1.9 %shard_map.101 = (f32[128,384]{1,0:T(8,128)}, bf16[768,768]{1,0:T(8,128)(2,1)S(1)}) custom-call(bf16[128,384]{1,0:T(8,128)(2,1)S(1)} %copy-done.1, bf16[768,768]{1,0:T(8,128)(2,1)S(1)} %slice_dynamic-update-slice_fusion.near_a.near, bf16[128,384]{1,0:T(8,128)(2,1)S(1)} %get-tuple-element.32.attn, bf16[3,128,1536]{2,1,0:T(8,128)(2,1)S(1)} %copy-done, ...), custom_call_target="tpu_custom_call" | custom-call | flops 301989888 | bytes 4194304 | tf_op jit(solution)/shard_map/pallas_call | solution.py:328
  111.6 0.9 collective-permute-done.7
  112.5 0.3 add_convert_fusion
  112.8 1.5 %collective-permute-start.12 = (bf16[128,768]{1,0:T(8,128)(2,1)S(1)}, bf16[128,768]{1,0:T(8,128)(2,1)S(1)}, u32[]{:S(2)}, u32[]{:S(2)}) collective-permute-start(bf16[128,768]{1,0:T(8,128)(2,1)S(1)} %get-tuple-element.42), channel_id=1, source_target_pairs={{0,16},{16,0},{32,48},{48,32},{64,80},{80,64},{96,112},{112,96},{1... | collective-permute-start | bytes 589832 | tf_op jit(solution)/shard_map/ppermute | solution.py:380
  114.3 0.9 collective-permute-start.11
  115.2 2.3 %collective-permute-start.10 = (bf16[128,768]{1,0:T(8,128)(2,1)S(1)}, bf16[128,768]{1,0:T(8,128)(2,1)S(1)}, u32[]{:S(2)}, u32[]{:S(2)}) collective-permute-start(bf16[128,768]{1,0:T(8,128)(2,1)S(1)} %get-tuple-element.44), channel_id=1, source_target_pairs={{0,224},{16,240},{32,0},{48,16},{64,32},{80,48},{96,64},{112,80},{... | collective-permute-start | bytes 589832 | tf_op jit(solution)/shard_map/ppermute | solution.py:380
  117.6 0.0 collective-permute-start.9
  117.6 4.1 %collective-permute-start.8 = (bf16[128,768]{1,0:T(8,128)(2,1)S(1)}, bf16[128,768]{1,0:T(8,128)(2,1)S(1)}, u32[]{:S(2)}, u32[]{:S(2)}) collective-permute-start(bf16[128,768]{1,0:T(8,128)(2,1)S(1)} %get-tuple-element.46), channel_id=1, source_target_pairs={{0,240},{16,224},{32,16},{48,0},{64,48},{80,32},{96,80},{112,64},{... | collective-permute-start | bytes 589832 | tf_op jit(solution)/shard_map/ppermute | solution.py:380
  121.7 0.8 shard_map.99
  122.5 0.0 collective-permute-done.12.refs_4_
  122.5 0.8 collective-permute-done.11.refs_3_
  123.3 0.0 collective-permute-done.10.refs_2_
  123.3 5.7 %collective-permute-done.9.refs_1_ = bf16[128,768]{1,0:T(8,128)(2,1)S(1)} collective-permute-done((bf16[128,768]{1,0:T(8,128)(2,1)S(1)}, bf16[128,768]{1,0:T(8,128)(2,1)S(1)}, u32[]{:S(2)}, u32[]{:S(2)}) %collective-permute-start.9) | collective-permute-done | bytes 196640 | tf_op jit(solution)/shard_map/ppermute | solution.py:380
  129.0 0.4 collective-permute-done.8.refs_0_
  129.5 0.8 shard_map.102
  (6 shorter events, 0.1 us)
Async XLA Ops:
  7.2 53.0 %all-gather.2.cloned.1.call-start = ((), (), s32[]{:S(2)}) async-start(), calls=%async_computation.3 | async-start | bytes 4177920 | tf_op jit(solution)/shard_map/all_gather | solution.py:387
  8.9 10.1 %collective-permute-start.2 = (bf16[128,768]{1,0:T(8,128)(2,1)S(1)}, bf16[128,768]{1,0:T(8,128)(2,1)S(1)}, u32[]{:S(2)}, u32[]{:S(2)}) collective-permute-start(bf16[128,768]{1,0:T(8,128)(2,1)S(1)} %get-tuple-element.48), channel_id=1, source_target_pairs={{0,224},{32,0},{64,32},{96,64},{128,96},{160,128},{192,160},{224,1... | collective-permute-start | bytes 589832 | tf_op jit(solution)/shard_map/ppermute | solution.py:373
  14.8 7.6 %collective-permute-start.1 = (bf16[128,768]{1,0:T(8,128)(2,1)S(1)}, bf16[128,768]{1,0:T(8,128)(2,1)S(1)}, u32[]{:S(2)}, u32[]{:S(2)}) collective-permute-start(bf16[128,768]{1,0:T(8,128)(2,1)S(1)} %get-tuple-element.48), channel_id=1, source_target_pairs={{0,32},{32,64},{64,96},{96,128},{128,160},{160,192},{192,224},{224... | collective-permute-start | bytes 589832 | tf_op jit(solution)/shard_map/ppermute | solution.py:369
  14.8 8.2 %collective-permute-start = (bf16[128,768]{1,0:T(8,128)(2,1)S(1)}, bf16[128,768]{1,0:T(8,128)(2,1)S(1)}, u32[]{:S(2)}, u32[]{:S(2)}) collective-permute-start(bf16[128,768]{1,0:T(8,128)(2,1)S(1)} %get-tuple-element.48), channel_id=1, source_target_pairs={{0,16},{16,0},{1,17},{17,1},{2,18},{18,2},{3,19},{19,3},{4,20},{20... | collective-permute-start | bytes 589832 | tf_op jit(solution)/shard_map/ppermute | solution.py:365
  22.4 12.8 %copy-start.1 = (bf16[128,384]{1,0:T(8,128)(2,1)S(1)}, bf16[128,384]{1,0:T(8,128)(2,1)}, u32[]{:S(2)}) copy-start(bf16[128,384]{1,0:T(8,128)(2,1)} %query.5) | copy-start | bytes 294916
  22.4 12.8 %copy-start.3 = (s32[32,32]{1,0:T(8,128)S(1)}, s32[32,32]{1,0:T(8,128)}, u32[]{:S(2)}) copy-start(s32[32,32]{1,0:T(8,128)} %mask.1) | copy-start | bytes 12292
  22.4 9.8 %collective-permute-start.3 = (bf16[256,768]{1,0:T(8,128)(2,1)S(1)}, bf16[256,768]{1,0:T(8,128)(2,1)S(1)}, u32[]{:S(2)}, u32[]{:S(2)}) collective-permute-start(bf16[256,768]{1,0:T(8,128)(2,1)S(1)} %pad_maximum_fusion), channel_id=1, source_target_pairs={{0,16},{16,0},{1,17},{17,1},{2,18},{18,2},{3,19},{19,3},{4,20},{20... | collective-permute-start | bytes 1179656 | tf_op jit(solution)/shard_map/ppermute | solution.py:365
  32.2 2.9 %collective-permute-start.4 = (bf16[768,768]{1,0:T(8,128)(2,1)S(1)}, bf16[768,768]{1,0:T(8,128)(2,1)S(1)}, u32[]{:S(2)}, u32[]{:S(2)}) collective-permute-start(bf16[768,768]{1,0:T(8,128)(2,1)S(1)} %slice_dynamic-update-slice_fusion.near_a.near), channel_id=1, source_target_pairs={{0,8},{8,0},{1,9},{9,1},{2,10},{10,2},{3,11},{11,3},{4,12},{12,4},... | collective-permute-start | bytes 3538952 | tf_op jit(solution)/shard_map/ppermute | solution.py:365
  62.7 8.1 %collective-permute-start.5 = (bf16[128,1280]{1,0:T(8,128)(2,1)S(1)}, bf16[128,1280]{1,0:T(8,128)(2,1)S(1)}, u32[]{:S(2)}, u32[]{:S(2)}) collective-permute-start(bf16[128,1280]{1,0:T(8,128)(2,1)S(1)} %get-tuple-element.25), channel_id=1, source_target_pairs={{0,16},{16,0},{1,17},{17,1},{2,18},{18,2},{3,19},{19,3},{4,20},{20... | collective-permute-start | bytes 983048 | tf_op jit(solution)/shard_map/ppermute | solution.py:365
  64.3 6.6 %copy-start.2 = (bf16[128,1280]{1,0:T(8,128)(2,1)S(1)}, bf16[128,1280]{1,0:T(8,128)(2,1)}, u32[]{:S(2)}) copy-start(bf16[128,1280]{1,0:T(8,128)(2,1)} %cot.1) | copy-start | bytes 983044
  71.6 16.8 %collective-permute-start.6 = (bf16[2,128,1280]{2,1,0:T(8,128)(2,1)S(1)}, bf16[2,128,1280]{2,1,0:T(8,128)(2,1)S(1)}, u32[]{:S(2)}, u32[]{:S(2)}) collective-permute-start(bf16[2,128,1280]{2,1,0:T(8,128)(2,1)S(1)} %get-tuple-element.29), channel_id=1, source_target_pairs={{0,16},{16,0},{1,17},{17,1},{2,18},{18,2},{3,19},{19,3},{4,20},{20... | collective-permute-start | bytes 1966088 | tf_op jit(solution)/shard_map/ppermute | solution.py:365
  90.3 17.9 %copy-start = (bf16[3,128,1536]{2,1,0:T(8,128)(2,1)S(1)}, bf16[3,128,1536]{2,1,0:T(8,128)(2,1)}, u32[]{:S(2)}) copy-start(bf16[3,128,1536]{2,1,0:T(8,128)(2,1)} %get-tuple-element.33.probs) | copy-start | bytes 3538948
  109.4 3.1 %collective-permute-start.7 = (bf16[768,768]{1,0:T(8,128)(2,1)S(1)}, bf16[768,768]{1,0:T(8,128)(2,1)S(1)}, u32[]{:S(2)}, u32[]{:S(2)}) collective-permute-start(bf16[768,768]{1,0:T(8,128)(2,1)S(1)} %get-tuple-element.39), channel_id=1, source_target_pairs={{0,8},{8,0},{1,9},{9,1},{2,10},{10,2},{3,11},{11,3},{4,12},{12,4},... | collective-permute-start | bytes 3538952 | tf_op jit(solution)/shard_map/ppermute | solution.py:365
  112.8 9.7 %collective-permute-start.12 = (bf16[128,768]{1,0:T(8,128)(2,1)S(1)}, bf16[128,768]{1,0:T(8,128)(2,1)S(1)}, u32[]{:S(2)}, u32[]{:S(2)}) collective-permute-start(bf16[128,768]{1,0:T(8,128)(2,1)S(1)} %get-tuple-element.42), channel_id=1, source_target_pairs={{0,16},{16,0},{32,48},{48,32},{64,80},{80,64},{96,112},{112,96},{1... | collective-permute-start | bytes 589832 | tf_op jit(solution)/shard_map/ppermute | solution.py:380
  114.3 9.0 %collective-permute-start.11 = (bf16[128,768]{1,0:T(8,128)(2,1)S(1)}, bf16[128,768]{1,0:T(8,128)(2,1)S(1)}, u32[]{:S(2)}, u32[]{:S(2)}) collective-permute-start(bf16[128,768]{1,0:T(8,128)(2,1)S(1)} %get-tuple-element.43), channel_id=1, source_target_pairs={{0,32},{16,48},{32,64},{48,80},{64,96},{80,112},{96,128},{112,144}... | collective-permute-start | bytes 589832 | tf_op jit(solution)/shard_map/ppermute | solution.py:380
  115.2 8.1 %collective-permute-start.10 = (bf16[128,768]{1,0:T(8,128)(2,1)S(1)}, bf16[128,768]{1,0:T(8,128)(2,1)S(1)}, u32[]{:S(2)}, u32[]{:S(2)}) collective-permute-start(bf16[128,768]{1,0:T(8,128)(2,1)S(1)} %get-tuple-element.44), channel_id=1, source_target_pairs={{0,224},{16,240},{32,0},{48,16},{64,32},{80,48},{96,64},{112,80},{... | collective-permute-start | bytes 589832 | tf_op jit(solution)/shard_map/ppermute | solution.py:380
  117.6 11.5 %collective-permute-start.9 = (bf16[128,768]{1,0:T(8,128)(2,1)S(1)}, bf16[128,768]{1,0:T(8,128)(2,1)S(1)}, u32[]{:S(2)}, u32[]{:S(2)}) collective-permute-start(bf16[128,768]{1,0:T(8,128)(2,1)S(1)} %get-tuple-element.45), channel_id=1, source_target_pairs={{0,48},{16,32},{32,80},{48,64},{64,112},{80,96},{96,144},{112,128}... | collective-permute-start | bytes 589832 | tf_op jit(solution)/shard_map/ppermute | solution.py:380
  117.6 11.9 %collective-permute-start.8 = (bf16[128,768]{1,0:T(8,128)(2,1)S(1)}, bf16[128,768]{1,0:T(8,128)(2,1)S(1)}, u32[]{:S(2)}, u32[]{:S(2)}) collective-permute-start(bf16[128,768]{1,0:T(8,128)(2,1)S(1)} %get-tuple-element.46), channel_id=1, source_target_pairs={{0,240},{16,224},{32,16},{48,0},{64,48},{80,32},{96,80},{112,64},{... | collective-permute-start | bytes 589832 | tf_op jit(solution)/shard_map/ppermute | solution.py:380
Sparse Core Ops, SparseCore 0:
  9.8 44.7 all-gather.1
